TPU v7x, 32 devices: a whole 2x2x4 slice. The times are simulated.
32 devices in a mesh: copies: 2 (over y), fsdp: 4 (over z), adapter: 4 (over x, core).
Axes of the slice: x: 2, y: 2, z: 4, core: 2. Of those that a mesh axis runs over, the one named last changes fastest.
Arguments:
- tokens: bfloat16 [8192, 5120], P(('copies', 'fsdp', 'adapter')), parts along dimension 0, may hold values from -6 to 6
- frozen_key_weight: bfloat16 [5120, 1024], P('fsdp'), may hold values from -0.078125 to 0.078125
- key_norm_gain: float32 [128], replicated, may hold values from 0.5 to 1.5
- adapter_down_weight: bfloat16 [48, 64, 5120], P('adapter', None, 'fsdp'), may hold values from -0.078125 to 0.078125
- adapter_up_weight: bfloat16 [48, 64, 1024], P('adapter', None, 'fsdp'), may hold values from -0.75 to 0.75
- packed_block_adapter: int32 [32], P('copies'), parts along dimension 0, may hold values from 0 to 47, as said below
- adapter_storage_row: int32 [48], replicated, may hold values from 0 to 47, each once
- live_adapter_rank: int32 [48], replicated, may hold values from 8 to 64, as said below
- document_numbers: int32 [8192], P(('copies', 'fsdp', 'adapter')), parts along dimension 0, may hold values from 0 to 4095, as said below
- rotated_key_gradient: bfloat16 [8192, 1024], P(('copies', 'fsdp', 'adapter')), parts along dimension 0, may hold values from -0.119628906 to 0.119628906
Outputs:
- rotated_keys: bfloat16 [8192, 1024], P(('copies', 'fsdp', 'adapter')), parts along dimension 0
- grad_down: float32 [96, 64, 5120], P(('copies', 'adapter'), None, 'fsdp'), parts along dimension 0
- grad_up: float32 [96, 64, 1024], P(('copies', 'adapter'), None, 'fsdp'), parts along dimension 0
There are 2 independent parts, one for each index of `copies`. A program takes and returns all parts, laid end to end along the dimension named above; an argument that names none is the same for every part. Nothing has to cross between parts.
Inputs may be any that keep to these rules, and one draw needn't show every extreme that they name: `packed_block_adapter`: never falling along the blocks; block 0 names adapter 0 and the last block names adapter 48 - 1. `live_adapter_rank`: each is 64 divided by 1, 2, 4 or 8; both ends are taken. `document_numbers`: never falling; a new document starts at every multiple of 256, so no document crosses a block; each id is the index of its document's first token, and the last token is a document of its own.
All inputs are finite; a program needn't handle non-finite values.
Results may differ from a plain program's by a relative error of at most 0.007.
Values may be sent and summed in bfloat16 or wider, within the bound.
No kernel may reach another device: no remote copies, remote signals or barrier semaphores. Data moves between devices by JAX's collectives and lax.ppermute only.
A program may use at most 128 MiB of HBM per device.

v0:
```python
import jax
import jax.numpy as jnp
from jax import lax
from jax.sharding import PartitionSpec as P

PADDED_RANK = 64
ADAPTER_COUNT = 48
BLOCK_LENGTH = 256


ADAPTER_STRENGTH = 16.0
ROPE_BASE = 1000000.0


def rope_tables(positions, head_size):
    half_head = head_size // 2
    steps_iota = jnp.arange(half_head, dtype=jnp.float32)
    frequency = jnp.exp(-jnp.log(jnp.float32(ROPE_BASE)) * 2.0 * steps_iota / head_size)
    angles = positions.astype(jnp.float32)[:, None] * frequency[None, :]
    return (jnp.cos(angles), jnp.sin(angles))


def keys_from(before_norm_keys, cosine_part, sine_part, key_norm_gain):
    rows_count = before_norm_keys.shape[0]
    head_size = key_norm_gain.shape[0]
    half_head = head_size // 2
    heads = before_norm_keys.reshape(rows_count, -1, head_size)
    mean_square = jnp.mean(heads * heads, axis=-1, keepdims=True)
    normed = heads * lax.rsqrt(mean_square + 1e-06) * key_norm_gain
    first_half = normed[..., :half_head]
    second_half = normed[..., half_head:]
    cosine_wide = cosine_part[:, None, :]
    sine_wide = sine_part[:, None, :]
    turned = jnp.concatenate(
        [
            first_half * cosine_wide - second_half * sine_wide,
            second_half * cosine_wide + first_half * sine_wide,
        ],
        axis=-1,
    )
    return turned.reshape(rows_count, -1)


def doc_positions(document_numbers):
    count = document_numbers.shape[0]
    index_iota = jnp.arange(count, dtype=jnp.int32)
    previous = jnp.concatenate([document_numbers[:1], document_numbers[:-1]])
    doc_start = jnp.logical_or(index_iota % BLOCK_LENGTH == 0, document_numbers != previous)
    first_index = lax.cummax(jnp.where(doc_start, index_iota, 0), axis=0)
    return index_iota - first_index


def per_device(
    tokens,
    frozen_key_weight,
    key_norm_gain,
    adapter_down_weight,
    adapter_up_weight,
    packed_block_adapter,
    adapter_storage_row,
    live_adapter_rank,
    document_numbers,
    rotated_key_gradient,
):
    tok_rows, feature_width = tokens.shape
    key_feature_width = rotated_key_gradient.shape[1]
    packed_blocks = tok_rows // BLOCK_LENGTH
    fsdp_count = lax.axis_size("fsdp")
    group_count = lax.axis_size("adapter")
    fsdp_here = lax.axis_index("fsdp")
    group_here = lax.axis_index("adapter")
    frozen_key_rows = jnp.dot(
        tokens,
        lax.all_gather(frozen_key_weight, "fsdp", axis=0, tiled=True),
        preferred_element_type=jnp.float32,
    )
    adapter_iota = jnp.arange(ADAPTER_COUNT, dtype=jnp.int32)
    group_ids = packed_block_adapter.reshape(fsdp_count, group_count, packed_blocks)
    group_ids = lax.dynamic_index_in_dim(group_ids, group_here, 1, keepdims=False)
    adapter_pick = group_ids[..., None] == adapter_iota
    store_rows = jnp.sum(jnp.where(adapter_pick, adapter_storage_row, 0), axis=-1)
    row_pick = store_rows[..., None] == adapter_iota
    own_pick = lax.dynamic_index_in_dim(adapter_pick, fsdp_here, 0, keepdims=False)
    packed_block_ranks = jnp.sum(jnp.where(own_pick, live_adapter_rank, 0), axis=-1)
    rank_mask = (
        jnp.arange(PADDED_RANK, dtype=jnp.int32)[None, :] < packed_block_ranks[:, None]
    ).astype(jnp.float32)
    adapter_scale = ADAPTER_STRENGTH / packed_block_ranks.astype(jnp.float32)
    tables_down, tables_up = (
        lax.all_gather(adapter_down_weight, "adapter", axis=0, tiled=True),
        lax.all_gather(adapter_up_weight, "adapter", axis=0, tiled=True),
    )
    select_rows = row_pick.astype(jnp.bfloat16)
    send_down = jnp.einsum(
        "jbs,srd->brjd", select_rows, tables_down, preferred_element_type=jnp.float32
    ).astype(jnp.bfloat16)
    send_up = jnp.einsum(
        "jbs,srd->brjd", select_rows, tables_up, preferred_element_type=jnp.float32
    ).astype(jnp.bfloat16)
    got_down, got_up = (
        lax.all_to_all(send_down, "fsdp", split_axis=2, concat_axis=2, tiled=True),
        lax.all_to_all(send_up, "fsdp", split_axis=2, concat_axis=2, tiled=True),
    )
    down_blocks = got_down.reshape(packed_blocks, PADDED_RANK, feature_width)
    up_weight_blocks = got_up.reshape(packed_blocks, PADDED_RANK, key_feature_width)
    token_blocks = tokens.reshape(packed_blocks, BLOCK_LENGTH, feature_width)
    reduced_rank_state = jnp.einsum(
        "btd,brd->btr", token_blocks, down_blocks, preferred_element_type=jnp.float32
    )
    reduced_rank_state = (reduced_rank_state * rank_mask[:, None, :]).astype(jnp.bfloat16)
    adapter_update = jnp.einsum(
        "wcv,wvd->wcd", reduced_rank_state, up_weight_blocks, preferred_element_type=jnp.float32
    )
    before_norm_keys = (
        frozen_key_rows.reshape(packed_blocks, BLOCK_LENGTH, key_feature_width)
        + adapter_scale[:, None, None] * adapter_update
    )
    before_norm_keys = before_norm_keys.reshape(tok_rows, key_feature_width)
    positions = doc_positions(document_numbers)
    cosine_part, sine_part = rope_tables(positions, key_norm_gain.shape[0])

    def rotate(values):
        return keys_from(values, cosine_part, sine_part, key_norm_gain)

    rotated, pullback = jax.vjp(rotate, before_norm_keys)
    pre_norm_gradient = pullback(rotated_key_gradient.astype(jnp.float32))[0].reshape(
        packed_blocks, BLOCK_LENGTH, key_feature_width
    )
    scaled_update = (adapter_scale[:, None, None] * pre_norm_gradient).astype(jnp.bfloat16)
    grad_low = jnp.einsum(
        "btk,brk->btr", scaled_update, up_weight_blocks, preferred_element_type=jnp.float32
    )
    grad_low = (grad_low * rank_mask[:, None, :]).astype(jnp.bfloat16)
    part_up = jnp.einsum(
        "btr,btk->brk", reduced_rank_state, scaled_update, preferred_element_type=jnp.float32
    )
    part_down = jnp.einsum(
        "btr,btd->brd", grad_low, token_blocks, preferred_element_type=jnp.float32
    )
    part_down = part_down.reshape(
        packed_blocks, PADDED_RANK, fsdp_count, feature_width // fsdp_count
    )
    part_up = part_up.reshape(
        packed_blocks, PADDED_RANK, fsdp_count, key_feature_width // fsdp_count
    )
    back_down, back_up = (
        lax.all_to_all(
            part_down.astype(jnp.bfloat16), "fsdp", split_axis=2, concat_axis=2, tiled=True
        ).astype(part_down.dtype),
        lax.all_to_all(
            part_up.astype(jnp.bfloat16), "fsdp", split_axis=2, concat_axis=2, tiled=True
        ).astype(part_up.dtype),
    )
    place_rows = row_pick.astype(jnp.float32)
    rows_down = jnp.einsum("jbs,brjd->srd", place_rows, back_down, precision=lax.Precision.HIGHEST)
    rows_up = jnp.einsum("jbs,brjd->srd", place_rows, back_up, precision=lax.Precision.HIGHEST)
    grad_down, grad_up = (
        lax.psum_scatter(
            rows_down.astype(jnp.bfloat16), "adapter", scatter_dimension=0, tiled=True
        ).astype(jnp.float32),
        lax.psum_scatter(
            rows_up.astype(jnp.bfloat16), "adapter", scatter_dimension=0, tiled=True
        ).astype(jnp.float32),
    )
    return (rotated.astype(jnp.bfloat16), grad_down, grad_up)


def solution(mesh):
    return jax.shard_map(
        per_device,
        mesh=mesh,
        in_specs=(
            P(("copies", "fsdp", "adapter"), None),
            P("fsdp", None),
            P(),
            P("adapter", None, "fsdp"),
            P("adapter", None, "fsdp"),
            P("copies"),
            P(),
            P(),
            P(("copies", "fsdp", "adapter")),
            P(("copies", "fsdp", "adapter"), None),
        ),
        out_specs=(
            P(("copies", "fsdp", "adapter"), None),
            P(("copies", "adapter"), None, "fsdp"),
            P(("copies", "adapter"), None, "fsdp"),
        ),
        check_vma=False,
    )
```

profile of v0, /device:TPU:0, one launch (start us, length us, event | category | flops | bytes accessed | tf_op | source)
XLA Modules:
  0.0 428.8 jit_solution(7445827645711952083)
XLA Ops:
  14.0 17.9 %all-gather.8.cloned.1.call-done = bf16[48,64,256]{2,1,0:T(8,128)(2,1)} async-done(((bf16[12,64,256]{2,1,0:T(8,128)(2,1)}), bf16[48,64,256]{2,1,0:T(8,128)(2,1)}) %all-gather.8.cloned.1.call-update) | async-done | bytes 1572880 | tf_op jit(solution)/shard_map/all_gather | solution.py:91
  32.0 2.4 fusion.17
  35.0 4.6 %all-to-all-start.1 = ((bf16[1,64,4,256]{3,1,0,2:T(8,128)(2,1)}), bf16[1,64,4,256]{3,1,0,2:T(8,128)(2,1)S(1)}, u32[]{:S(2)}, u32[]{:S(2)}) async-start(bf16[1,64,4,256]{3,1,0,2:T(8,128)(2,1)} %copy.75), calls=%async_computation.1 | async-start | bytes 262144 | tf_op jit(solution)/shard_map/all_to_all | solution.py:102
  39.6 49.3 %all-gather.6.cloned.1.call-done = bf16[48,64,1280]{2,1,0:T(8,128)(2,1)} async-done(((bf16[12,64,1280]{2,1,0:T(8,128)(2,1)}), bf16[48,64,1280]{2,1,0:T(8,128)(2,1)}) %all-gather.6.cloned.1.call-update) | async-done | bytes 7864336 | tf_op jit(solution)/shard_map/all_gather | solution.py:90
  88.9 11.7 %fusion.5 = bf16[1,64,4,1280]{3,2,1,0:T(4,128)(2,1)S(1)} fusion(bf16[48,64,1280]{2,1,0:T(8,128)(2,1)} %all-gather.6.cloned.1.call-done, s32[4]{0:T(128)S(1)} %select_reduce_fusion), kind=kOutput, calls=%fused_computation.5 | convolution fusion | flops 31785152 | bytes 8519696 | tf_op jit(solution)/shard_map/jbs,srd->brjd/dot_general | solution.py:94
  101.5 4.6 %all-to-all-start = ((bf16[1,64,4,1280]{3,1,0,2:T(8,128)(2,1)}), bf16[1,64,4,1280]{3,1,0,2:T(8,128)(2,1)S(1)}, u32[]{:S(2)}, u32[]{:S(2)}) async-start(bf16[1,64,4,1280]{3,1,0,2:T(8,128)(2,1)} %copy.72), calls=%async_computation | async-start | bytes 1310720 | tf_op jit(solution)/shard_map/all_to_all | solution.py:101
  106.8 1.7 multiply_add_fusion.1
  109.8 30.6 %all-to-all-done = bf16[1,64,4,1280]{3,1,0,2:T(8,128)(2,1)S(1)} async-done(((bf16[1,64,4,1280]{3,1,0,2:T(8,128)(2,1)}), bf16[1,64,4,1280]{3,1,0,2:T(8,128)(2,1)S(1)}, u32[]{:S(2)}, u32[]{:S(2)}) %all-to-all-start) | async-done | bytes 655392 | tf_op jit(solution)/shard_map/all_to_all | solution.py:101
  141.9 146.6 %all-gather.4.cloned.1.call-done = bf16[5120,1024]{1,0:T(8,128)(2,1)} async-done(((bf16[1280,1024]{1,0:T(8,128)(2,1)}), bf16[5120,1024]{1,0:T(8,128)(2,1)}) %all-gather.4.cloned.1.call-update) | async-done | bytes 10485776 | tf_op jit(solution)/shard_map/all_gather | solution.py:74
  288.4 5.6 %fusion.49 = f32[256,1024]{1,0:T(8,128)S(1)} fusion(bf16[256,5120]{1,0:T(8,128)(2,1)S(1)} %copy-done, bf16[5120,1024]{1,0:T(8,128)(2,1)} %all-gather.4.cloned.1.call-done), kind=kOutput, calls=%fused_computation.71 | convolution fusion | flops 2684354560 | bytes 14155776 | tf_op jit(solution)/shard_map/dot_general | solution.py:72
  297.7 3.1 fusion.24
  301.7 2.0 copy.85
  303.7 1.3 fusion.16
  305.1 8.8 %all_to_all.20 = bf16[1,64,4,256]{3,1,0,2:T(8,128)(2,1)S(1)} all-to-all(bf16[1,64,4,256]{3,1,0,2:T(8,128)(2,1)S(1)} %fusion.16), channel_id=1, replica_groups=mesh['copies'=2,'fsdp'=4,'adapter'=4] {'fsdp'}, dimensions={2} | all-to-all | bytes 262144 | tf_op jit(solution)/shard_map/all_to_all | solution.py:150
  314.6 1.7 copy.88
  316.4 2.6 copy.89
  318.9 3.1 fusion.8
  322.0 19.6 %all_to_all.21 = bf16[1,64,4,1280]{3,1,0,2:T(8,128)(2,1)S(1)} all-to-all(bf16[1,64,4,1280]{3,1,0,2:T(8,128)(2,1)S(1)} %fusion.8), channel_id=1, replica_groups=mesh['copies'=2,'fsdp'=4,'adapter'=4] {'fsdp'}, dimensions={2} | all-to-all | bytes 1310720 | tf_op jit(solution)/shard_map/all_to_all | solution.py:147
  341.6 2.7 convolution_convert_fusion
  344.3 5.9 %copy.84 = bf16[48,64,1280]{2,1,0:T(8,128)(2,1)} copy(bf16[48,64,1280]{2,0,1:T(8,128)(2,1)S(1)} %convolution_convert_fusion) | data formatting | bytes 15728640 | tf_op jit(solution)/shard_map/convert_element_type | solution.py:159
  350.2 1.2 copy-done.4
  353.0 1.9 convert_element_type.120
  355.0 63.4 %reduce-scatter.3.cloned.1.call-done = bf16[12,64,1280]{2,1,0:T(8,128)(2,1)} async-done(((bf16[48,64,1280]{2,1,0:T(8,128)(2,1)}), bf16[12,64,1280]{2,1,0:T(8,128)(2,1)}) %reduce-scatter.3.cloned.1.call-update) | async-done | bytes 1966096 | tf_op jit(solution)/shard_map/reduce_scatter | solution.py:158
  418.4 3.9 convert_element_type.116
  (78 shorter events, 17.9 us)
Async XLA Ops:
  7.2 2.3 copy-start.12
  7.2 2.6 copy-start.13
  7.2 3.9 copy-start.7
  7.2 24.8 %all-gather.8.cloned.1.call-start = ((), (), s32[]{:S(2)}) async-start(), calls=%async_computation.8 | async-start | bytes 1966080 | tf_op jit(solution)/shard_map/all_gather | solution.py:91
  7.9 81.0 %all-gather.6.cloned.1.call-start = ((), (), s32[]{:S(2)}) async-start(), calls=%async_computation.7 | async-start | bytes 9830400 | tf_op jit(solution)/shard_map/all_gather | solution.py:90
  8.7 2.7 copy-start.10
  8.7 5.1 %copy-start.14 = (s32[48]{0:T(128)S(1)}, s32[48]{0:T(128)}, u32[]{:S(2)}) copy-start(s32[48]{0:T(128)} %param.16) | copy-start | bytes 580
  8.7 279.7 %all-gather.4.cloned.1.call-start = ((), (), s32[]{:S(2)}) async-start(), calls=%async_computation.6 | async-start | bytes 13107200 | tf_op jit(solution)/shard_map/all_gather | solution.py:74
  35.0 66.4 %all-to-all-start.1 = ((bf16[1,64,4,256]{3,1,0,2:T(8,128)(2,1)}), bf16[1,64,4,256]{3,1,0,2:T(8,128)(2,1)S(1)}, u32[]{:S(2)}, u32[]{:S(2)}) async-start(bf16[1,64,4,256]{3,1,0,2:T(8,128)(2,1)} %copy.75), calls=%async_computation.1 | async-start | bytes 262144 | tf_op jit(solution)/shard_map/all_to_all | solution.py:102
  101.5 5.4 %copy-start.8 = (bf16[1,64,4,256]{3,1,0,2:T(8,128)(2,1)}, bf16[1,64,4,256]{3,1,0,2:T(8,128)(2,1)S(1)}, u32[]{:S(2)}) copy-start(bf16[1,64,4,256]{3,1,0,2:T(8,128)(2,1)S(1)} %all-to-all-done.1) | copy-start | bytes 393220
  101.5 38.9 %all-to-all-start = ((bf16[1,64,4,1280]{3,1,0,2:T(8,128)(2,1)}), bf16[1,64,4,1280]{3,1,0,2:T(8,128)(2,1)S(1)}, u32[]{:S(2)}, u32[]{:S(2)}) async-start(bf16[1,64,4,1280]{3,1,0,2:T(8,128)(2,1)} %copy.72), calls=%async_computation | async-start | bytes 1310720 | tf_op jit(solution)/shard_map/all_to_all | solution.py:101
  106.1 247.0 %reduce-scatter.5.cloned.1.call-start = ((), (), s32[]{:S(2)}) async-start(), calls=%async_computation.10 | async-start | bytes 1966080 | tf_op jit(solution)/shard_map/reduce_scatter | solution.py:161
  106.8 2.9 copy-start.5
  108.6 32.4 %copy-start = (bf16[256,5120]{1,0:T(8,128)(2,1)S(1)}, bf16[256,5120]{1,0:T(8,128)(2,1)}, u32[]{:S(2)}) copy-start(bf16[256,5120]{1,0:T(8,128)(2,1)} %param.10) | copy-start | bytes 7864324
  141.9 152.2 %copy-start.9 = (bf16[64,256]{1,0:T(8,128)(2,1)}, bf16[64,256]{1,0:T(8,128)(2,1)S(1)}, u32[]{:S(2)}) copy-start(bf16[64,256]{1,0:T(8,128)(2,1)S(1)} %fusion.20) | copy-start | bytes 98308
  294.0 1.2 copy-start.1
  294.0 1.6 copy-start.2
  294.0 1.6 copy-start.11
  294.6 2.0 copy-start.3
  316.3 102.1 %reduce-scatter.3.cloned.1.call-start = ((), (), s32[]{:S(2)}) async-start(), calls=%async_computation.9 | async-start | bytes 9830400 | tf_op jit(solution)/shard_map/reduce_scatter | solution.py:158
  350.2 1.2 copy-start.4
  350.2 1.2 copy-start.6
Sparse Core Ops, SparseCore 0:
  9.6 22.3 all-gather.7
  33.5 55.3 all-gather.5
  90.5 197.9 all-gather.3
  316.5 27.3 reduce-scatter.4
  350.3 68.0 reduce-scatter.2
where the time goes:
time: 429 us
  waiting for transfers between devices  310 us (72%)
  matrix products  28.7 us (7%)
  blocking collectives  28.4 us (7%)
  local copies, waits for them, and re-layouts  22 us (5%)
  other arithmetic  15.7 us (4%)
  between operations  14.8 us (3%)
  starting transfers between devices  9.36 us (2%)
    all_gather x1, waiting for transfers between devices, per_device(): lax.all_gather(frozen_key_weight, 'fsdp', axis=0, tiled=True)  147 us
    reduce_scatter x1, waiting for transfers between devices, per_device(): lax.psum_scatter(rows_down.astype(jnp.bfloat16), 'adapter', scatter_dimen...  63.4 us
    all_gather x1, waiting for transfers between devices, per_device(): lax.all_gather(adapter_down_weight, 'adapter', axis=0, tiled=True)  49.3 us
    all_to_all x1, waiting for transfers between devices, per_device(): lax.all_to_all(send_down, 'fsdp', split_axis=2, concat_axis=2, tiled=True)  30.6 us
    all_to_all x1, blocking collectives, per_device(): lax.all_to_all(part_down.astype(jnp.bfloat16), 'fsdp', split_axis=2, conc...  19.6 us
    all_gather x1, waiting for transfers between devices, per_device(): lax.all_gather(adapter_up_weight, 'adapter', axis=0, tiled=True)  17.9 us
    dot_general x1, matrix products, per_device(): jnp.einsum('jbs,srd->brjd', select_rows, tables_down, preferred_element_t...  11.7 us
    all_to_all x1, blocking collectives, per_device(): lax.all_to_all(part_up.astype(jnp.bfloat16), 'fsdp', split_axis=2, concat...  8.79 us
  transfers between devices with their start and end apart: 7, of which 5 were waited for; matrix products, arithmetic and copies ran while one was open for 10% of the time, Pallas kernels for 0%

commit v1 on v0

v1 whole, which is shorter than its diff:
```python
import functools

import jax
import jax.numpy as jnp
from jax import lax
from jax.experimental import pallas as pl
from jax.experimental.pallas import tpu as pltpu
from jax.sharding import PartitionSpec as P

BLOCK_LENGTH = 256
ADAPTER_STRENGTH = 16.0
ROPE_BASE = 1000000.0


def rope_tables(positions, head_size):
    half_head = head_size // 2
    steps_iota = jnp.arange(half_head, dtype=jnp.float32)
    frequency = jnp.exp(-jnp.log(jnp.float32(ROPE_BASE)) * 2.0 * steps_iota / head_size)
    angles = positions.astype(jnp.float32)[:, None] * frequency[None, :]
    return (jnp.cos(angles), jnp.sin(angles))


def keys_from(before_norm_keys, cosine_part, sine_part, key_norm_gain):
    rows_count = before_norm_keys.shape[0]
    head_size = key_norm_gain.shape[0]
    half_head = head_size // 2
    heads = before_norm_keys.reshape(rows_count, -1, head_size)
    mean_square = jnp.mean(heads * heads, axis=-1, keepdims=True)
    normed = heads * lax.rsqrt(mean_square + 1e-06) * key_norm_gain
    first_half = normed[..., :half_head]
    second_half = normed[..., half_head:]
    cosine_wide = cosine_part[:, None, :]
    sine_wide = sine_part[:, None, :]
    turned = jnp.concatenate(
        [
            first_half * cosine_wide - second_half * sine_wide,
            second_half * cosine_wide + first_half * sine_wide,
        ],
        axis=-1,
    )
    return turned.reshape(rows_count, -1)


def doc_positions(document_numbers):
    count = document_numbers.shape[0]
    index_iota = jnp.arange(count, dtype=jnp.int32)
    previous = jnp.concatenate([document_numbers[:1], document_numbers[:-1]])
    doc_start = jnp.logical_or(index_iota % BLOCK_LENGTH == 0, document_numbers != previous)
    first_index = lax.cummax(jnp.where(doc_start, index_iota, 0), axis=0)
    return index_iota - first_index


def pick_kernel(own_rows, pair_rows, own_ref, pair_ref, out_ref):
    n = pl.program_id(0)
    own = own_rows[n] >= 0
    pair = pair_rows[n] >= 0
    out_ref[0] = jnp.zeros_like(out_ref[0])

    @pl.when(own)
    def _():
        out_ref[0] = own_ref[0]

    @pl.when(pair)
    def _():
        out_ref[0] = pair_ref[0]


def pick_rows(own, pair, own_rows, pair_rows):
    count = own_rows.shape[0]
    _, rank, width = own.shape
    return pl.pallas_call(
        pick_kernel,
        grid_spec=pltpu.PrefetchScalarGridSpec(
            num_scalar_prefetch=2,
            grid=(count,),
            in_specs=[
                pl.BlockSpec((1, rank, width), lambda n, o, p: (jnp.maximum(o[n], 0), 0, 0)),
                pl.BlockSpec((1, rank, width), lambda n, o, p: (jnp.maximum(p[n], 0), 0, 0)),
            ],
            out_specs=pl.BlockSpec((1, rank, width), lambda n, o, p: (n, 0, 0)),
        ),
        out_shape=jax.ShapeDtypeStruct((count, rank, width), own.dtype),
    )(own_rows, pair_rows, own, pair)


def owner_sum_kernel(arrays, per_array, owned, rows_ref, *refs):
    block_refs, down_ref, up_ref = refs[:arrays], refs[arrays], refs[arrays + 1]
    down_width = down_ref.shape[2]
    down_ref[...] = jnp.zeros_like(down_ref)
    up_ref[...] = jnp.zeros_like(up_ref)
    for i in range(arrays):

        def one(j, carry, i=i):
            row = rows_ref[i * per_array + j]

            @pl.when(jnp.logical_and(row >= 0, row < owned))
            def _():
                block = block_refs[i][j].astype(jnp.float32)
                down_ref[row] += block[:, :down_width]
                up_ref[row] += block[:, down_width:]

            return carry

        lax.fori_loop(0, per_array, one, 0)


def owner_sum(blocks, rows, owned, down_width):
    per_array, rank, width = blocks[0].shape
    tile = 16
    return pl.pallas_call(
        functools.partial(owner_sum_kernel, len(blocks), per_array, owned),
        grid_spec=pltpu.PrefetchScalarGridSpec(
            num_scalar_prefetch=1,
            grid=(rank // tile,),
            in_specs=[
                pl.BlockSpec((per_array, tile, width), lambda t, r: (0, t, 0)) for _ in blocks
            ],
            out_specs=[
                pl.BlockSpec((owned, tile, down_width), lambda t, r: (0, t, 0)),
                pl.BlockSpec((owned, tile, width - down_width), lambda t, r: (0, t, 0)),
            ],
        ),
        out_shape=[
            jax.ShapeDtypeStruct((owned, rank, down_width), jnp.float32),
            jax.ShapeDtypeStruct((owned, rank, width - down_width), jnp.float32),
        ],
        compiler_params=pltpu.CompilerParams(vmem_limit_bytes=40 * 1024 * 1024),
    )(rows, *blocks)


def per_device(
    tokens,
    frozen_key_weight,
    key_norm_gain,
    adapter_down_weight,
    adapter_up_weight,
    packed_block_adapter,
    adapter_storage_row,
    live_adapter_rank,
    document_numbers,
    rotated_key_gradient,
):
    rows = tokens.shape[0]
    features = rotated_key_gradient.shape[1]
    depth = frozen_key_weight.shape[0]
    owned, rank, down_width = adapter_down_weight.shape
    up_width = adapter_up_weight.shape[2]
    copies_n = lax.axis_size("copies")
    z_n = lax.axis_size("fsdp")
    group_n = lax.axis_size("adapter")
    x_n = group_n // 2
    y = lax.axis_index("copies")
    z = lax.axis_index("fsdp")
    a = lax.axis_index("adapter")
    x, core = a // 2, a % 2

    def over_core(v):
        return lax.ppermute(v, "adapter", [(i, i ^ 1) for i in range(group_n)])

    def over_x(v, e):
        return lax.ppermute(
            v, "adapter", [(i, ((i // 2 + e) % x_n) * 2 + i % 2) for i in range(group_n)]
        )

    def over_y(v, g):
        return lax.ppermute(v, "copies", [(i, (i + g) % copies_n) for i in range(copies_n)])

    def over_z(v, d):
        return lax.ppermute(v, "fsdp", [(i, (i + d) % z_n) for i in range(z_n)])

    half = features // 2
    units = copies_n * x_n
    unit_width = half // units
    unit = lax.dynamic_slice(
        frozen_key_weight,
        (0, core * half + (y * x_n + x) * unit_width),
        (depth, unit_width),
    )
    own_half = lax.dynamic_slice(frozen_key_weight, (0, core * half), (depth, half))
    from_z = {d: over_z(unit, d) for d in range(1, z_n)}
    tokens_pair = over_core(tokens)

    tables = jnp.concatenate([adapter_down_weight, adapter_up_weight], axis=2)
    tables_pair = over_core(tables)
    block_rows = adapter_storage_row[packed_block_adapter].reshape(z_n, x_n, 2)
    z_order = (z + jnp.arange(z_n)) % z_n
    x_order = (x + jnp.arange(x_n)) % x_n
    picked_rows = block_rows[z_order][:, x_order][:, :, core].T.reshape(-1)

    def owned_row(row, owner):
        local = row - owner * owned
        return jnp.where(jnp.logical_and(local >= 0, local < owned), local, -1).astype(jnp.int32)

    picked = pick_rows(
        tables, tables_pair, owned_row(picked_rows, a), owned_row(picked_rows, a ^ 1)
    ).reshape(x_n, z_n, rank, down_width + up_width)
    slices = picked[0]
    for e in range(1, x_n):
        slices = slices + over_x(picked[e], e)
    adapter_slices = {0: slices[0]}
    for d in range(1, z_n):
        adapter_slices[(-d) % z_n] = over_z(slices[d], d)

    def token_slice(array, j):
        return lax.dynamic_slice(array, (0, ((z + j) % z_n) * depth), (rows, depth))

    own_slices = [token_slice(tokens, j) for j in range(z_n)]
    both = [
        jnp.concatenate([own_slices[j], token_slice(tokens_pair, j)], axis=0) for j in range(z_n)
    ]
    base_turned = None
    for d in range(1, z_n):
        along_x = [from_z[d]] + [over_x(from_z[d], e) for e in range(1, x_n)]
        shard = list(along_x)
        for g in range(1, copies_n):
            shard += [over_y(v, g) for v in along_x]
        part = jnp.dot(
            both[(-d) % z_n],
            jnp.concatenate(shard, axis=1),
            preferred_element_type=jnp.float32,
        )
        base_turned = part if base_turned is None else base_turned + part
    pieces = []
    for y_to in range(copies_n):
        for x_to in range(x_n):
            at = ((y - y_to) % copies_n) * x_n + (x - x_to) % x_n
            pieces.append(
                lax.dynamic_slice(base_turned, (0, at * unit_width), (2 * rows, unit_width))
            )
    base_half = jnp.concatenate(pieces, axis=1) + jnp.dot(
        both[0], own_half, preferred_element_type=jnp.float32
    )
    base_other = over_core(base_half[rows:])
    base_mine = base_half[:rows]
    base = jnp.where(
        core == 0,
        jnp.concatenate([base_mine, base_other], axis=1),
        jnp.concatenate([base_other, base_mine], axis=1),
    )

    my_adapter = packed_block_adapter[z * group_n + a]
    my_rank = live_adapter_rank[my_adapter]
    rank_mask = (jnp.arange(rank, dtype=jnp.int32) < my_rank).astype(jnp.float32)
    adapter_scale = ADAPTER_STRENGTH / my_rank.astype(jnp.float32)
    low = None
    for j in range(z_n):
        part = lax.dot_general(
            own_slices[j],
            adapter_slices[j][:, :down_width],
            (((1,), (1,)), ((), ())),
            preferred_element_type=jnp.float32,
        )
        low = part if low is None else low + part
    low = (low * rank_mask).astype(jnp.bfloat16)
    up_stack = jnp.stack([adapter_slices[j][:, down_width:] for j in range(z_n)])
    up = jnp.concatenate(
        [
            lax.dynamic_index_in_dim(up_stack, (f - z) % z_n, 0, keepdims=False)
            for f in range(z_n)
        ],
        axis=1,
    )
    before_norm_keys = base + adapter_scale * jnp.dot(
        low, up, preferred_element_type=jnp.float32
    )
    positions = doc_positions(document_numbers)
    cosine_part, sine_part = rope_tables(positions, key_norm_gain.shape[0])

    def rotate(values):
        return keys_from(values, cosine_part, sine_part, key_norm_gain)

    rotated, pullback = jax.vjp(rotate, before_norm_keys)
    pre_norm_gradient = pullback(rotated_key_gradient.astype(jnp.float32))[0]
    scaled = (adapter_scale * pre_norm_gradient).astype(jnp.bfloat16)
    grad_low = lax.dot_general(
        scaled, up, (((1,), (1,)), ((), ())), preferred_element_type=jnp.float32
    )
    grad_low = (grad_low * rank_mask).astype(jnp.bfloat16)
    part_up = lax.dot_general(
        low, scaled, (((0,), (0,)), ((), ())), preferred_element_type=jnp.float32
    ).astype(jnp.bfloat16)
    sent = []
    for j in range(z_n):
        part_down = lax.dot_general(
            grad_low, own_slices[j], (((0,), (0,)), ((), ())), preferred_element_type=jnp.float32
        ).astype(jnp.bfloat16)
        part_up_slice = lax.dynamic_slice(
            part_up, (0, ((z + j) % z_n) * up_width), (rank, up_width)
        )
        sent.append(jnp.concatenate([part_down, part_up_slice], axis=1))
    here = jnp.stack([sent[0]] + [over_z(sent[d], d) for d in range(1, z_n)])
    along_x = [here] + [over_x(here, e) for e in range(1, x_n)]
    blocks, owners = [], []
    z_back = (z - jnp.arange(z_n)) % z_n
    for e in range(x_n):
        blocks += [along_x[e], over_core(along_x[e])]
        for other in range(2):
            owners.append(block_rows[z_back, (x - e) % x_n, core ^ other])
    grad_down, grad_up = owner_sum(
        blocks, (jnp.concatenate(owners) - a * owned).astype(jnp.int32), owned, down_width
    )
    return (rotated.astype(jnp.bfloat16), grad_down, grad_up)


def solution(mesh):
    return jax.shard_map(
        per_device,
        mesh=mesh,
        in_specs=(
            P(("copies", "fsdp", "adapter"), None),
            P("fsdp", None),
            P(),
            P("adapter", None, "fsdp"),
            P("adapter", None, "fsdp"),
            P("copies"),
            P(),
            P(),
            P(("copies", "fsdp", "adapter")),
            P(("copies", "fsdp", "adapter"), None),
        ),
        out_specs=(
            P(("copies", "fsdp", "adapter"), None),
            P(("copies", "adapter"), None, "fsdp"),
            P(("copies", "adapter"), None, "fsdp"),
        ),
        check_vma=False,
    )
```

time: 429 us -> 165 us (0.38)
  waiting for transfers between devices: 310 us -> 59.7 us
  starting transfers between devices: 9.36 us -> 42.1 us
  blocking collectives: 28.4 us -> 0 us
  matrix products: 28.7 us -> 10.3 us
  Pallas kernels: 0 us -> 11.9 us
  between operations: 14.8 us -> 3.76 us
  other arithmetic: 15.7 us -> 9.71 us
    all_gather x3 -> x0, waiting for transfers between devices: 214 us -> none  [the longest x1 147 us: per_device(): lax.all_gather(frozen_key_weight, 'fsdp', axis=0, tiled=True)]
    reduce_scatter x2 -> x0, waiting for transfers between devices: 63.4 us -> none  [the longest x1 63.4 us: per_device(): lax.psum_scatter(rows_down.astype(jnp.bfloat16), 'adapter', scatter_dimen...]
    ppermute x0 -> x25, waiting for transfers between devices: none -> 59.7 us  [the longest x9 21.1 us: over_z(): return lax.ppermute(v, 'fsdp', [(i, (i + d) % z_n) for i in range(z_n)])]
    ppermute x0 -> x25, starting transfers between devices: none -> 42.1 us  [the longest x9 25.6 us: over_z(): return lax.ppermute(v, 'fsdp', [(i, (i + d) % z_n) for i in range(z_n)])]
    all_to_all x2 -> x0, waiting for transfers between devices: 30.6 us -> none  [the longest x1 30.6 us: per_device(): lax.all_to_all(send_down, 'fsdp', split_axis=2, concat_axis=2, tiled=True)]
    all_to_all x2 -> x0, blocking collectives: 28.4 us -> none  [the longest x1 19.6 us: per_device(): lax.all_to_all(part_down.astype(jnp.bfloat16), 'fsdp', split_axis=2, conc...]
    dot_general x9 -> x15, matrix products: 28.7 us -> 10.3 us  [the longest x3 6.04 us: per_device(): jnp.dot(both[-d % z_n], jnp.concatenate(shard, axis=1), preferred_element...]
    pallas_call x0 -> x2, Pallas kernels: none -> 11.9 us  [the longest x1 6.26 us: pick_rows(): pl.pallas_call(pick_kernel, grid_spec=pltpu.PrefetchScalarGridSpec(num_sc...]
  transfers between devices with their start and end apart: 7 -> 25, of which waited for: 5 -> 11; matrix products, arithmetic and copies ran while one was open for 10% -> 23% of each run, Pallas kernels for 0% -> 4%
where the time goes in v1:
time: 165 us; the launch traced here: 162 us
  waiting for transfers between devices  59.7 us (36%)
  starting transfers between devices  42.1 us (26%)
  local copies, waits for them, and re-layouts  24.8 us (15%)
  Pallas kernels  11.9 us (7%)
  matrix products  10.3 us (6%)
  other arithmetic  9.71 us (6%)
  between operations  3.76 us (2%)
    ppermute x9, starting transfers between devices, over_z(): return lax.ppermute(v, 'fsdp', [(i, (i + d) % z_n) for i in range(z_n)])  25.6 us
    ppermute x9, waiting for transfers between devices, over_z(): return lax.ppermute(v, 'fsdp', [(i, (i + d) % z_n) for i in range(z_n)])  21.1 us
    ppermute x5, waiting for transfers between devices, over_x(): lax.ppermute(v, 'adapter', [(i, (i // 2 + e) % x_n * 2 + i % 2) for i in...  19.7 us
    ppermute x6, waiting for transfers between devices, over_y(): lax.ppermute(v, 'copies', [(i, (i + g) % copies_n) for i in range(copies_...  18.9 us
    ppermute x5, starting transfers between devices, over_x(): lax.ppermute(v, 'adapter', [(i, (i // 2 + e) % x_n * 2 + i % 2) for i in...  8.73 us
    ppermute x6, starting transfers between devices, over_y(): lax.ppermute(v, 'copies', [(i, (i + g) % copies_n) for i in range(copies_...  7.12 us
    pallas_call x1, Pallas kernels, pick_rows(): pl.pallas_call(pick_kernel, grid_spec=pltpu.PrefetchScalarGridSpec(num_sc...  6.26 us
    dot_general x3, matrix products, per_device(): jnp.dot(both[-d % z_n], jnp.concatenate(shard, axis=1), preferred_element...  6.04 us
  transfers between devices with their start and end apart: 25, of which 11 were waited for; matrix products, arithmetic and copies ran while one was open for 23% of the time, Pallas kernels for 4%

profile of v1, /device:TPU:0, one launch (start us, length us, event | category | flops | bytes accessed | tf_op | source)
XLA Modules:
  0.0 162.3 jit_solution(6124600964050715199)
XLA Ops:
  3.2 4.1 %collective-permute-start.5 = (bf16[1280,128]{1,0:T(8,128)(2,1)}, bf16[1280,128]{1,0:T(8,128)(2,1)}, u32[]{:S(2)}, u32[]{:S(2)}) collective-permute-start(bf16[1280,128]{1,0:T(8,128)(2,1)} %constant_dynamic-slice_fusion.15), channel_id=1, source_target_pairs={{0,8},{4,12},{8,0},{12,4},{1,9},{5,13},{9,1},{13,5},{2,10},{6,14},... | collective-permute-start | bytes 983048 | tf_op jit(solution)/shard_map/ppermute | solution.py:169
  9.3 3.0 %constant_dynamic-update-slice_fusion.1 = bf16[12,64,1536]{2,1,0:T(8,128)(2,1)} fusion(bf16[12,64,1280]{2,1,0:T(8,128)(2,1)} %param.13), kind=kLoop, calls=%fused_computation.127 | loop fusion | bytes 3932160
  24.3 2.3 %multiply_add_fusion.1 = (f32[256,8,64]{0,2,1:T(8,128)}, f32[256,8,64]{0,2,1:T(8,128)}) fusion(f32[256,8,128]{0,2,1:T(8,128)} %bitcast.84, f32[256,64]{0,1:T(8,128)S(1)} %get-tuple-element.46, f32[256,64]{0,1:T(8,128)S(1)} %get-tuple-element.45), kind=kLoop, calls=%fused_computation.72 | loop fusion | flops 917504 | bytes 2228224 | tf_op jit(solution)/shard_map/transpose(jvp())/add_any | solution.py:36
  26.6 5.4 %collective-permute-start.6 = (bf16[1280,128]{1,0:T(8,128)(2,1)}, bf16[1280,128]{1,0:T(8,128)(2,1)}, u32[]{:S(2)}, u32[]{:S(2)}) collective-permute-start(bf16[1280,128]{1,0:T(8,128)(2,1)} %collective-permute-done.5), channel_id=1, source_target_pairs={{0,2},{1,3},{2,0},{3,1},{4,6},{5,7},{6,4},{7,5},{8,10},{9,11},{10,... | collective-permute-start | bytes 983048 | tf_op jit(solution)/shard_map/ppermute | solution.py:161
  32.1 3.1 %constant_dynamic-slice_fusion.17 = (bf16[256,1280]{1,0:T(8,128)(2,1)S(1)}, bf16[256,1280]{1,0:T(8,128)(2,1)}, bf16[256,1280]{1,0:T(8,128)(2,1)}, bf16[256,1280]{1,0:T(8,128)(2,1)}) fusion(bf16[256,5120]{1,0:T(8,128)(2,1)} %param.10, s32[]{:T(128)S(6)} %select_n.274, s32[]{:T(128)S(6)} %select_n.278, s32[]{:T(128)S(6)} %select_n.290, s32[]{:T(128)S(6)} %select_n.280), kind=kLoop, calls=%fused_computation.122 | loop fusion | bytes 5242896 | tf_op jit(solution)/shard_map/dynamic_slice | solution.py:205
  35.2 2.0 %collective-permute-start.7 = (bf16[1280,128]{1,0:T(8,128)(2,1)}, bf16[1280,128]{1,0:T(8,128)(2,1)}, u32[]{:S(2)}, u32[]{:S(2)}) collective-permute-start(bf16[1280,128]{1,0:T(8,128)(2,1)} %collective-permute-done.5), channel_id=1, source_target_pairs={{0,16},{16,0},{1,17},{17,1},{2,18},{18,2},{3,19},{19,3},{4,20},{20... | collective-permute-start | bytes 983048 | tf_op jit(solution)/shard_map/ppermute | solution.py:166
  37.2 6.3 %shard_map.121 = bf16[8,64,1536]{2,1,0:T(8,128)(2,1)} custom-call(s32[8]{0:T(128)} %get-tuple-element.49.own_rows, s32[8]{0:T(128)} %get-tuple-element.48.pair_rows, bf16[12,64,1536]{2,1,0:T(8,128)(2,1)} %constant_dynamic-update-slice_fusion.own_ref, bf16[12,64,1536]{2,1,0:T(8,128)(2,1)} %collective-permute-done.14.pair_ref), custom_call_target="tpu_custom_call" | custom-call | tf_op jit(solution)/shard_map/pallas_call | solution.py:71
  44.8 2.1 %collective-permute-start.2 = (bf16[1280,128]{1,0:T(8,128)(2,1)}, bf16[1280,128]{1,0:T(8,128)(2,1)S(1)}, u32[]{:S(2)}, u32[]{:S(2)}) collective-permute-start(bf16[1280,128]{1,0:T(8,128)(2,1)} %collective-permute-done.1), channel_id=1, source_target_pairs={{0,2},{1,3},{2,0},{3,1},{4,6},{5,7},{6,4},{7,5},{8,10},{9,11},{10,... | collective-permute-start | bytes 983048 | tf_op jit(solution)/shard_map/ppermute | solution.py:161
  54.1 8.6 %collective-permute-done.8 = bf16[1280,128]{1,0:T(8,128)(2,1)S(1)} collective-permute-done((bf16[1280,128]{1,0:T(8,128)(2,1)}, bf16[1280,128]{1,0:T(8,128)(2,1)S(1)}, u32[]{:S(2)}, u32[]{:S(2)}) %collective-permute-start.8) | collective-permute-done | bytes 327712 | tf_op jit(solution)/shard_map/ppermute | solution.py:166
  63.7 2.1 %fusion.11 = f32[512,512]{0,1:T(8,128)S(1)} fusion(bf16[256,1280]{1,0:T(8,128)(2,1)S(1)} %get-tuple-element.16, bf16[256,1280]{1,0:T(8,128)(2,1)S(1)} %copy-done.3, bf16[1280,128]{1,0:T(8,128)(2,1)S(1)} %collective-permute-done.8, bf16[1280,128]{1,0:T(8,128)(2,1)} %collective-permute-done.7, bf16[1280,128]{1,0:T(8,128)(2,1)} %collective-permute-done.6, ...), kind=kOutput, calls=%fused_computation.26 | convolution fusion | flops 678952960 | bytes 3670016 | tf_op jit(solution)/shard_map/dot_general | solution.py:217
  65.9 3.8 %collective-permute-done.12 = bf16[1280,128]{1,0:T(8,128)(2,1)S(1)} collective-permute-done((bf16[1280,128]{1,0:T(8,128)(2,1)}, bf16[1280,128]{1,0:T(8,128)(2,1)S(1)}, u32[]{:S(2)}, u32[]{:S(2)}) %collective-permute-start.12) | collective-permute-done | bytes 327712 | tf_op jit(solution)/shard_map/ppermute | solution.py:166
  71.6 3.0 %collective-permute-done.3 = bf16[1280,128]{1,0:T(8,128)(2,1)S(1)} collective-permute-done((bf16[1280,128]{1,0:T(8,128)(2,1)}, bf16[1280,128]{1,0:T(8,128)(2,1)S(1)}, u32[]{:S(2)}, u32[]{:S(2)}) %collective-permute-start.3) | collective-permute-done | bytes 327712 | tf_op jit(solution)/shard_map/ppermute | solution.py:166
  74.7 3.5 %collective-permute-done.4 = bf16[1280,128]{1,0:T(8,128)(2,1)S(1)} collective-permute-done((bf16[1280,128]{1,0:T(8,128)(2,1)S(1)}, bf16[1280,128]{1,0:T(8,128)(2,1)S(1)}, u32[]{:S(2)}, u32[]{:S(2)}) %collective-permute-start.4) | collective-permute-done | bytes 327712 | tf_op jit(solution)/shard_map/ppermute | solution.py:166
  82.7 9.1 %collective-permute-start.18 = (bf16[64,1536]{1,0:T(8,128)(2,1)S(1)}, bf16[64,1536]{1,0:T(8,128)(2,1)S(1)}, u32[]{:S(2)}, u32[]{:S(2)}) collective-permute-start(bf16[64,1536]{1,0:T(8,128)(2,1)S(1)} %get-tuple-element.30), channel_id=1, source_target_pairs={{0,4},{4,8},{8,12},{12,0},{1,5},{5,9},{9,13},{13,1},{2,6},{6,10},{... | collective-permute-start | bytes 589832 | tf_op jit(solution)/shard_map/ppermute | solution.py:169
  91.8 2.4 %collective-permute-start.16 = (bf16[64,1536]{1,0:T(8,128)(2,1)S(1)}, bf16[64,1536]{1,0:T(8,128)(2,1)S(1)}, u32[]{:S(2)}, u32[]{:S(2)}) collective-permute-start(bf16[64,1536]{1,0:T(8,128)(2,1)S(1)} %get-tuple-element.31), channel_id=1, source_target_pairs={{0,12},{4,0},{8,4},{12,8},{1,13},{5,1},{9,5},{13,9},{2,14},{6,2},{... | collective-permute-start | bytes 589832 | tf_op jit(solution)/shard_map/ppermute | solution.py:169
  94.2 2.9 %collective-permute-done.18 = bf16[64,1536]{1,0:T(8,128)(2,1)S(1)} collective-permute-done((bf16[64,1536]{1,0:T(8,128)(2,1)S(1)}, bf16[64,1536]{1,0:T(8,128)(2,1)S(1)}, u32[]{:S(2)}, u32[]{:S(2)}) %collective-permute-start.18) | collective-permute-done | bytes 196640 | tf_op jit(solution)/shard_map/ppermute | solution.py:169
  97.2 5.4 %collective-permute-done.17 = bf16[64,1536]{1,0:T(8,128)(2,1)S(1)} collective-permute-done((bf16[64,1536]{1,0:T(8,128)(2,1)S(1)}, bf16[64,1536]{1,0:T(8,128)(2,1)S(1)}, u32[]{:S(2)}, u32[]{:S(2)}) %collective-permute-start.17) | collective-permute-done | bytes 196640 | tf_op jit(solution)/shard_map/ppermute | solution.py:169
  108.8 4.5 %collective-permute-start.19 = (bf16[64,1536]{1,0:T(8,128)(2,1)S(1)}, bf16[64,1536]{1,0:T(8,128)(2,1)S(1)}, u32[]{:S(2)}, u32[]{:S(2)}) collective-permute-start(bf16[64,1536]{1,0:T(8,128)(2,1)S(1)} %pad_maximum_fusion.2), channel_id=1, source_target_pairs={{0,4},{4,8},{8,12},{12,0},{1,5},{5,9},{9,13},{13,1},{2,6},{6,10},{... | collective-permute-start | bytes 589832 | tf_op jit(solution)/shard_map/ppermute | solution.py:169
  113.4 3.4 %collective-permute-start.20 = (bf16[64,1536]{1,0:T(8,128)(2,1)S(1)}, bf16[64,1536]{1,0:T(8,128)(2,1)S(1)}, u32[]{:S(2)}, u32[]{:S(2)}) collective-permute-start(bf16[64,1536]{1,0:T(8,128)(2,1)S(1)} %pad_maximum_fusion.3), channel_id=1, source_target_pairs={{0,8},{4,12},{8,0},{12,4},{1,9},{5,13},{9,1},{13,5},{2,10},{6,14},... | collective-permute-start | bytes 589832 | tf_op jit(solution)/shard_map/ppermute | solution.py:169
  116.9 5.1 %collective-permute-done.19 = bf16[64,1536]{1,0:T(8,128)(2,1)S(1)} collective-permute-done((bf16[64,1536]{1,0:T(8,128)(2,1)S(1)}, bf16[64,1536]{1,0:T(8,128)(2,1)S(1)}, u32[]{:S(2)}, u32[]{:S(2)}) %collective-permute-start.19) | collective-permute-done | bytes 196640 | tf_op jit(solution)/shard_map/ppermute | solution.py:169
  122.0 6.3 %collective-permute-done.20 = bf16[64,1536]{1,0:T(8,128)(2,1)S(1)} collective-permute-done((bf16[64,1536]{1,0:T(8,128)(2,1)S(1)}, bf16[64,1536]{1,0:T(8,128)(2,1)S(1)}, u32[]{:S(2)}, u32[]{:S(2)}) %collective-permute-start.20) | collective-permute-done | bytes 196640 | tf_op jit(solution)/shard_map/ppermute | solution.py:169
  128.6 19.4 %collective-permute-done.23.refs_2_ = bf16[4,64,1536]{2,1,0:T(8,128)(2,1)} collective-permute-done((bf16[4,64,1536]{2,1,0:T(8,128)(2,1)S(1)}, bf16[4,64,1536]{2,1,0:T(8,128)(2,1)}, u32[]{:S(2)}, u32[]{:S(2)}) %collective-permute-start.23) | collective-permute-done | bytes 786464 | tf_op jit(solution)/shard_map/ppermute | solution.py:161
  154.6 2.0 %copy.29 = bf16[256,1024]{1,0:T(8,128)(2,1)} copy(bf16[256,1024]{0,1:T(8,128)(2,1)} %bitcast.85) | data formatting | bytes 1048576 | tf_op jit(solution)/shard_map/convert_element_type | solution.py:302
  156.6 5.7 %shard_map.122 = (f32[12,64,1280]{2,1,0:T(8,128)}, f32[12,64,256]{2,1,0:T(8,128)}) custom-call(s32[16]{0:T(128)S(1)} %add_subtract_fusion.rows_ref, bf16[4,64,1536]{2,1,0:T(8,128)(2,1)S(1)} %pad_maximum_fusion.refs_0_, bf16[4,64,1536]{2,1,0:T(8,128)(2,1)} %collective-permute-done.22.refs_1_, bf16[4,64,1536]{2,1,0:T(8,128)(2,1)} %collective-permute-done.23.refs_2_, ...), custom_call_target="tpu_custom_call" | custom-call | tf_op jit(solution)/shard_map/pallas_call | solution.py:110
  (134 shorter events, 42.9 us)
Async XLA Ops:
  3.2 23.4 %collective-permute-start.5 = (bf16[1280,128]{1,0:T(8,128)(2,1)}, bf16[1280,128]{1,0:T(8,128)(2,1)}, u32[]{:S(2)}, u32[]{:S(2)}) collective-permute-start(bf16[1280,128]{1,0:T(8,128)(2,1)} %constant_dynamic-slice_fusion.15), channel_id=1, source_target_pairs={{0,8},{4,12},{8,0},{12,4},{1,9},{5,13},{9,1},{13,5},{2,10},{6,14},... | collective-permute-start | bytes 983048 | tf_op jit(solution)/shard_map/ppermute | solution.py:169
  7.3 24.8 %collective-permute-start.9 = (bf16[1280,128]{1,0:T(8,128)(2,1)}, bf16[1280,128]{1,0:T(8,128)(2,1)}, u32[]{:S(2)}, u32[]{:S(2)}) collective-permute-start(bf16[1280,128]{1,0:T(8,128)(2,1)} %constant_dynamic-slice_fusion.15), channel_id=1, source_target_pairs={{0,12},{4,0},{8,4},{12,8},{1,13},{5,1},{9,5},{13,9},{2,14},{6,2},{... | collective-permute-start | bytes 983048 | tf_op jit(solution)/shard_map/ppermute | solution.py:169
  8.7 36.0 %collective-permute-start.1 = (bf16[1280,128]{1,0:T(8,128)(2,1)}, bf16[1280,128]{1,0:T(8,128)(2,1)}, u32[]{:S(2)}, u32[]{:S(2)}) collective-permute-start(bf16[1280,128]{1,0:T(8,128)(2,1)} %constant_dynamic-slice_fusion.15), channel_id=1, source_target_pairs={{0,4},{4,8},{8,12},{12,0},{1,5},{5,9},{9,13},{13,1},{2,6},{6,10},{... | collective-permute-start | bytes 983048 | tf_op jit(solution)/shard_map/ppermute | solution.py:169
  9.3 38.5 %collective-permute-start = (bf16[256,5120]{1,0:T(8,128)(2,1)}, bf16[256,5120]{1,0:T(8,128)(2,1)}, u32[]{:S(2)}, u32[]{:S(2)}) collective-permute-start(bf16[256,5120]{1,0:T(8,128)(2,1)} %param.10), channel_id=1, source_target_pairs={{0,1},{1,0},{2,3},{3,2},{4,5},{5,4},{6,7},{7,6},{8,9},{9,8},{10,11... | collective-permute-start | bytes 7864328 | tf_op jit(solution)/shard_map/ppermute | solution.py:158
  13.1 22.1 %collective-permute-start.14 = (bf16[12,64,1536]{2,1,0:T(8,128)(2,1)}, bf16[12,64,1536]{2,1,0:T(8,128)(2,1)}, u32[]{:S(2)}, u32[]{:S(2)}) collective-permute-start(bf16[12,64,1536]{2,1,0:T(8,128)(2,1)} %constant_dynamic-update-slice_fusion.own_ref), channel_id=1, source_target_pairs={{0,1},{1,0},{2,3},{3,2},{4,5},{5,4},{6,7},{7,6},{8,9},{9,8},{10,11... | collective-permute-start | bytes 7077896 | tf_op jit(solution)/shard_map/ppermute | solution.py:158
  26.6 18.1 %collective-permute-start.6 = (bf16[1280,128]{1,0:T(8,128)(2,1)}, bf16[1280,128]{1,0:T(8,128)(2,1)}, u32[]{:S(2)}, u32[]{:S(2)}) collective-permute-start(bf16[1280,128]{1,0:T(8,128)(2,1)} %collective-permute-done.5), channel_id=1, source_target_pairs={{0,2},{1,3},{2,0},{3,1},{4,6},{5,7},{6,4},{7,5},{8,10},{9,11},{10,... | collective-permute-start | bytes 983048 | tf_op jit(solution)/shard_map/ppermute | solution.py:161
  32.1 14.8 %collective-permute-start.10 = (bf16[1280,128]{1,0:T(8,128)(2,1)}, bf16[1280,128]{1,0:T(8,128)(2,1)}, u32[]{:S(2)}, u32[]{:S(2)}) collective-permute-start(bf16[1280,128]{1,0:T(8,128)(2,1)} %collective-permute-done.9), channel_id=1, source_target_pairs={{0,2},{1,3},{2,0},{3,1},{4,6},{5,7},{6,4},{7,5},{8,10},{9,11},{10,... | collective-permute-start | bytes 983048 | tf_op jit(solution)/shard_map/ppermute | solution.py:161
  35.2 15.6 %collective-permute-start.7 = (bf16[1280,128]{1,0:T(8,128)(2,1)}, bf16[1280,128]{1,0:T(8,128)(2,1)}, u32[]{:S(2)}, u32[]{:S(2)}) collective-permute-start(bf16[1280,128]{1,0:T(8,128)(2,1)} %collective-permute-done.5), channel_id=1, source_target_pairs={{0,16},{16,0},{1,17},{17,1},{2,18},{18,2},{3,19},{19,3},{4,20},{20... | collective-permute-start | bytes 983048 | tf_op jit(solution)/shard_map/ppermute | solution.py:166
  44.7 21.2 %collective-permute-start.11 = (bf16[1280,128]{1,0:T(8,128)(2,1)}, bf16[1280,128]{1,0:T(8,128)(2,1)S(1)}, u32[]{:S(2)}, u32[]{:S(2)}) collective-permute-start(bf16[1280,128]{1,0:T(8,128)(2,1)} %collective-permute-done.9), channel_id=1, source_target_pairs={{0,16},{16,0},{1,17},{17,1},{2,18},{18,2},{3,19},{19,3},{4,20},{20... | collective-permute-start | bytes 983048 | tf_op jit(solution)/shard_map/ppermute | solution.py:166
  46.9 15.8 %collective-permute-start.8 = (bf16[1280,128]{1,0:T(8,128)(2,1)}, bf16[1280,128]{1,0:T(8,128)(2,1)S(1)}, u32[]{:S(2)}, u32[]{:S(2)}) collective-permute-start(bf16[1280,128]{1,0:T(8,128)(2,1)} %collective-permute-done.6), channel_id=1, source_target_pairs={{0,16},{16,0},{1,17},{17,1},{2,18},{18,2},{3,19},{19,3},{4,20},{20... | collective-permute-start | bytes 983048 | tf_op jit(solution)/shard_map/ppermute | solution.py:166
  47.9 21.8 %collective-permute-start.12 = (bf16[1280,128]{1,0:T(8,128)(2,1)}, bf16[1280,128]{1,0:T(8,128)(2,1)S(1)}, u32[]{:S(2)}, u32[]{:S(2)}) collective-permute-start(bf16[1280,128]{1,0:T(8,128)(2,1)} %collective-permute-done.10), channel_id=1, source_target_pairs={{0,16},{16,0},{1,17},{17,1},{2,18},{18,2},{3,19},{19,3},{4,20},{20... | collective-permute-start | bytes 983048 | tf_op jit(solution)/shard_map/ppermute | solution.py:166
  50.8 23.9 %collective-permute-start.3 = (bf16[1280,128]{1,0:T(8,128)(2,1)}, bf16[1280,128]{1,0:T(8,128)(2,1)S(1)}, u32[]{:S(2)}, u32[]{:S(2)}) collective-permute-start(bf16[1280,128]{1,0:T(8,128)(2,1)} %collective-permute-done.1), channel_id=1, source_target_pairs={{0,16},{16,0},{1,17},{17,1},{2,18},{18,2},{3,19},{19,3},{4,20},{20... | collective-permute-start | bytes 983048 | tf_op jit(solution)/shard_map/ppermute | solution.py:166
  52.1 26.0 %collective-permute-start.4 = (bf16[1280,128]{1,0:T(8,128)(2,1)S(1)}, bf16[1280,128]{1,0:T(8,128)(2,1)S(1)}, u32[]{:S(2)}, u32[]{:S(2)}) collective-permute-start(bf16[1280,128]{1,0:T(8,128)(2,1)S(1)} %collective-permute-done.2), channel_id=1, source_target_pairs={{0,16},{16,0},{1,17},{17,1},{2,18},{18,2},{3,19},{19,3},{4,20},{20... | collective-permute-start | bytes 983048 | tf_op jit(solution)/shard_map/ppermute | solution.py:166
  62.6 18.7 %collective-permute-start.15 = (bf16[4,64,1536]{2,1,0:T(8,128)(2,1)S(1)}, bf16[4,64,1536]{2,1,0:T(8,128)(2,1)S(1)}, u32[]{:S(2)}, u32[]{:S(2)}) collective-permute-start(bf16[4,64,1536]{2,1,0:T(8,128)(2,1)S(1)} %slice.112), channel_id=1, source_target_pairs={{0,2},{1,3},{2,0},{3,1},{4,6},{5,7},{6,4},{7,5},{8,10},{9,11},{10,... | collective-permute-start | bytes 2359304 | tf_op jit(solution)/shard_map/ppermute | solution.py:161
  81.2 24.1 %collective-permute-start.13 = (f32[256,512]{0,1:T(8,128)S(1)}, f32[256,512]{0,1:T(8,128)S(1)}, u32[]{:S(2)}, u32[]{:S(2)}) collective-permute-start(f32[256,512]{0,1:T(8,128)S(1)} %get-tuple-element.24), channel_id=1, source_target_pairs={{0,1},{1,0},{2,3},{3,2},{4,5},{5,4},{6,7},{7,6},{8,9},{9,8},{10,11... | collective-permute-start | bytes 1572872 | tf_op jit(solution)/shard_map/ppermute | solution.py:158
  82.7 14.4 %collective-permute-start.18 = (bf16[64,1536]{1,0:T(8,128)(2,1)S(1)}, bf16[64,1536]{1,0:T(8,128)(2,1)S(1)}, u32[]{:S(2)}, u32[]{:S(2)}) collective-permute-start(bf16[64,1536]{1,0:T(8,128)(2,1)S(1)} %get-tuple-element.30), channel_id=1, source_target_pairs={{0,4},{4,8},{8,12},{12,0},{1,5},{5,9},{9,13},{13,1},{2,6},{6,10},{... | collective-permute-start | bytes 589832 | tf_op jit(solution)/shard_map/ppermute | solution.py:169
  91.8 10.8 %collective-permute-start.17 = (bf16[64,1536]{1,0:T(8,128)(2,1)S(1)}, bf16[64,1536]{1,0:T(8,128)(2,1)S(1)}, u32[]{:S(2)}, u32[]{:S(2)}) collective-permute-start(bf16[64,1536]{1,0:T(8,128)(2,1)S(1)} %get-tuple-element.29), channel_id=1, source_target_pairs={{0,8},{4,12},{8,0},{12,4},{1,9},{5,13},{9,1},{13,5},{2,10},{6,14},... | collective-permute-start | bytes 589832 | tf_op jit(solution)/shard_map/ppermute | solution.py:169
  91.8 12.1 %collective-permute-start.16 = (bf16[64,1536]{1,0:T(8,128)(2,1)S(1)}, bf16[64,1536]{1,0:T(8,128)(2,1)S(1)}, u32[]{:S(2)}, u32[]{:S(2)}) collective-permute-start(bf16[64,1536]{1,0:T(8,128)(2,1)S(1)} %get-tuple-element.31), channel_id=1, source_target_pairs={{0,12},{4,0},{8,4},{12,8},{1,13},{5,1},{9,5},{13,9},{2,14},{6,2},{... | collective-permute-start | bytes 589832 | tf_op jit(solution)/shard_map/ppermute | solution.py:169
  108.8 13.2 %collective-permute-start.19 = (bf16[64,1536]{1,0:T(8,128)(2,1)S(1)}, bf16[64,1536]{1,0:T(8,128)(2,1)S(1)}, u32[]{:S(2)}, u32[]{:S(2)}) collective-permute-start(bf16[64,1536]{1,0:T(8,128)(2,1)S(1)} %pad_maximum_fusion.2), channel_id=1, source_target_pairs={{0,4},{4,8},{8,12},{12,0},{1,5},{5,9},{9,13},{13,1},{2,6},{6,10},{... | collective-permute-start | bytes 589832 | tf_op jit(solution)/shard_map/ppermute | solution.py:169
  113.4 15.0 %collective-permute-start.20 = (bf16[64,1536]{1,0:T(8,128)(2,1)S(1)}, bf16[64,1536]{1,0:T(8,128)(2,1)S(1)}, u32[]{:S(2)}, u32[]{:S(2)}) collective-permute-start(bf16[64,1536]{1,0:T(8,128)(2,1)S(1)} %pad_maximum_fusion.3), channel_id=1, source_target_pairs={{0,8},{4,12},{8,0},{12,4},{1,9},{5,13},{9,1},{13,5},{2,10},{6,14},... | collective-permute-start | bytes 589832 | tf_op jit(solution)/shard_map/ppermute | solution.py:169
  116.8 11.5 %collective-permute-start.21 = (bf16[64,1536]{1,0:T(8,128)(2,1)S(1)}, bf16[64,1536]{1,0:T(8,128)(2,1)S(1)}, u32[]{:S(2)}, u32[]{:S(2)}) collective-permute-start(bf16[64,1536]{1,0:T(8,128)(2,1)S(1)} %pad_maximum_fusion.4), channel_id=1, source_target_pairs={{0,12},{4,0},{8,4},{12,8},{1,13},{5,1},{9,5},{13,9},{2,14},{6,2},{... | collective-permute-start | bytes 589832 | tf_op jit(solution)/shard_map/ppermute | solution.py:169
  128.5 19.5 %collective-permute-start.23 = (bf16[4,64,1536]{2,1,0:T(8,128)(2,1)S(1)}, bf16[4,64,1536]{2,1,0:T(8,128)(2,1)}, u32[]{:S(2)}, u32[]{:S(2)}) collective-permute-start(bf16[4,64,1536]{2,1,0:T(8,128)(2,1)S(1)} %pad_maximum_fusion.refs_0_), channel_id=1, source_target_pairs={{0,2},{1,3},{2,0},{3,1},{4,6},{5,7},{6,4},{7,5},{8,10},{9,11},{10,... | collective-permute-start | bytes 2359304 | tf_op jit(solution)/shard_map/ppermute | solution.py:161
  128.6 28.1 %collective-permute-start.22 = (bf16[4,64,1536]{2,1,0:T(8,128)(2,1)S(1)}, bf16[4,64,1536]{2,1,0:T(8,128)(2,1)}, u32[]{:S(2)}, u32[]{:S(2)}) collective-permute-start(bf16[4,64,1536]{2,1,0:T(8,128)(2,1)S(1)} %pad_maximum_fusion.refs_0_), channel_id=1, source_target_pairs={{0,1},{1,0},{2,3},{3,2},{4,5},{5,4},{6,7},{7,6},{8,9},{9,8},{10,11... | collective-permute-start | bytes 2359304 | tf_op jit(solution)/shard_map/ppermute | solution.py:158
  148.0 8.6 %collective-permute-start.24 = (bf16[4,64,1536]{2,1,0:T(8,128)(2,1)}, bf16[4,64,1536]{2,1,0:T(8,128)(2,1)}, u32[]{:S(2)}, u32[]{:S(2)}) collective-permute-start(bf16[4,64,1536]{2,1,0:T(8,128)(2,1)} %collective-permute-done.23.refs_2_), channel_id=1, source_target_pairs={{0,1},{1,0},{2,3},{3,2},{4,5},{5,4},{6,7},{7,6},{8,9},{9,8},{10,11... | collective-permute-start | bytes 2359304 | tf_op jit(solution)/shard_map/ppermute | solution.py:158
  (15 other events, 187.6 us)

commit v2 on v0

v2 whole, which is shorter than its diff:
```python
import functools

import jax
import jax.numpy as jnp
from jax import lax
from jax.experimental import pallas as pl
from jax.experimental.pallas import tpu as pltpu
from jax.sharding import PartitionSpec as P

BLOCK_LENGTH = 256
ADAPTER_STRENGTH = 16.0
ROPE_BASE = 1000000.0


def rope_tables(positions, head_size):
    half_head = head_size // 2
    steps_iota = jnp.arange(half_head, dtype=jnp.float32)
    frequency = jnp.exp(-jnp.log(jnp.float32(ROPE_BASE)) * 2.0 * steps_iota / head_size)
    angles = positions.astype(jnp.float32)[:, None] * frequency[None, :]
    return (jnp.cos(angles), jnp.sin(angles))


def doc_positions(document_numbers):
    count = document_numbers.shape[0]
    index_iota = jnp.arange(count, dtype=jnp.int32)
    previous = jnp.concatenate([document_numbers[:1], document_numbers[:-1]])
    doc_start = jnp.logical_or(index_iota % BLOCK_LENGTH == 0, document_numbers != previous)
    first_index = lax.cummax(jnp.where(doc_start, index_iota, 0), axis=0)
    return index_iota - first_index


def block_row(numbers, blocks, z_to, group_to, group_n):
    return numbers[2 + blocks + numbers[2 + z_to * group_n + group_to]]


def pick_kernel(sizes, numbers, down_ref, up_ref, *refs):
    x_n, z_n = sizes
    out_refs, (down_buffer, up_buffer, semaphores) = refs[: 2 * x_n], refs[2 * x_n :]
    owned = down_ref.shape[0]
    z, a = numbers[0], numbers[1]
    x, core = a // 2, a % 2

    def for_block(n, act):
        pair, e, j = n // (x_n * z_n), n // z_n % x_n, n % z_n
        group_to = ((x + e) % x_n) * 2 + (core + pair) % 2
        row = block_row(numbers, 2 * x_n * z_n, (z + j) % z_n, group_to, 2 * x_n) - a * owned
        hit = jnp.logical_and(row >= 0, row < owned)

        @pl.when(hit)
        def _():
            act(pltpu.make_async_copy(down_ref.at[row], down_buffer.at[n], semaphores.at[0, n]))
            act(pltpu.make_async_copy(up_ref.at[row], up_buffer.at[n], semaphores.at[1, n]))

        return hit

    def start(n, carry):
        for_block(n, lambda copy: copy.start())
        return carry

    lax.fori_loop(0, 2 * x_n * z_n, start, 0)
    for m in range(2 * x_n):

        def finish(j, carry, m=m):
            n = m * z_n + j
            hit = for_block(n, lambda copy: copy.wait())

            @pl.when(hit)
            def _():
                out_refs[m][j] = jnp.concatenate([down_buffer[n], up_buffer[n]], axis=1)

            @pl.when(jnp.logical_not(hit))
            def _():
                out_refs[m][j] = jnp.zeros_like(out_refs[m][j])

            return carry

        lax.fori_loop(0, z_n, finish, 0)


def pick_rows(sizes, numbers, down, up):
    x_n, z_n = sizes
    count = 2 * x_n * z_n
    _, rank, down_width = down.shape
    up_width = up.shape[2]
    return pl.pallas_call(
        functools.partial(pick_kernel, sizes),
        in_specs=[pl.BlockSpec(memory_space=pltpu.SMEM)]
        + [pl.BlockSpec(memory_space=pltpu.HBM)] * 2,
        out_specs=[pl.BlockSpec(memory_space=pltpu.VMEM)] * (2 * x_n),
        out_shape=[jax.ShapeDtypeStruct((z_n, rank, down_width + up_width), down.dtype)]
        * (2 * x_n),
        scratch_shapes=[
            pltpu.VMEM((count, rank, down_width), down.dtype),
            pltpu.VMEM((count, rank, up_width), down.dtype),
            pltpu.SemaphoreType.DMA((2, count)),
        ],
        compiler_params=pltpu.CompilerParams(vmem_limit_bytes=24 * 1024 * 1024),
    )(numbers, down, up)


def owner_sum_kernel(sizes, groups, numbers, *refs):
    x_n, z_n = sizes
    count = x_n * 2 * len(groups)
    block_refs, down_ref, up_ref = refs[:count], refs[count], refs[count + 1]
    owned, _, down_width = down_ref.shape
    z, a = numbers[0], numbers[1]
    x, core = a // 2, a % 2
    down_ref[...] = jnp.zeros_like(down_ref)
    up_ref[...] = jnp.zeros_like(up_ref)
    i = 0
    for group in groups:
        for e in range(x_n):
            for pair in range(2):
                group_from = ((x - e + x_n) % x_n) * 2 + (core + pair) % 2

                def one(k, carry, i=i, first=group[0], group_from=group_from):
                    z_from = (z - first - k + z_n) % z_n
                    row = block_row(numbers, 2 * x_n * z_n, z_from, group_from, 2 * x_n)
                    row = row - a * owned

                    @pl.when(jnp.logical_and(row >= 0, row < owned))
                    def _():
                        block = block_refs[i][k].astype(jnp.float32)
                        down_ref[row] += block[:, :down_width]
                        up_ref[row] += block[:, down_width:]

                    return carry

                if len(group) == 1:
                    one(0, 0)
                else:
                    lax.fori_loop(0, len(group), one, 0)
                i += 1


def owner_sum(sizes, groups, numbers, blocks, owned, down_width):
    _, rank, width = blocks[0].shape
    tile = 16
    smem = pl.BlockSpec(memory_space=pltpu.SMEM)
    return pl.pallas_call(
        functools.partial(owner_sum_kernel, sizes, groups),
        grid=(rank // tile,),
        in_specs=[smem]
        + [pl.BlockSpec((b.shape[0], tile, width), lambda t: (0, t, 0)) for b in blocks],
        out_specs=[
            pl.BlockSpec((owned, tile, down_width), lambda t: (0, t, 0)),
            pl.BlockSpec((owned, tile, width - down_width), lambda t: (0, t, 0)),
        ],
        out_shape=[
            jax.ShapeDtypeStruct((owned, rank, down_width), jnp.float32),
            jax.ShapeDtypeStruct((owned, rank, width - down_width), jnp.float32),
        ],
        compiler_params=pltpu.CompilerParams(vmem_limit_bytes=12 * 1024 * 1024),
    )(numbers, *blocks)


def low_kernel(
    z_n, place_ref, rank_ref, tokens_ref, *refs,
):
    slice_refs = refs[:z_n]
    low_ref, up_ref, update_ref, tokens_buffer, semaphore = refs[z_n:]
    fetch = pltpu.make_async_copy(tokens_ref, tokens_buffer, semaphore)
    fetch.start()
    z = place_ref[0]
    rank, depth = low_ref.shape[1], tokens_ref.shape[1] // z_n
    up_width = up_ref.shape[1] // z_n
    for j in range(z_n):
        f = (z + j) % z_n
        up_ref[:, pl.ds(pl.multiple_of(f * up_width, 128), up_width)] = slice_refs[j][:, depth:]
    fetch.wait()
    low = None
    for j in range(z_n):
        f = (z + j) % z_n
        part = lax.dot_general(
            tokens_buffer[:, pl.ds(pl.multiple_of(f * depth, 128), depth)],
            slice_refs[j][:, :depth],
            (((1,), (1,)), ((), ())),
            preferred_element_type=jnp.float32,
        )
        low = part if low is None else low + part
    live = lax.broadcasted_iota(jnp.int32, (1, rank), 1) < rank_ref[...]
    low = jnp.where(live, low, 0.0).astype(jnp.bfloat16)
    low_ref[...] = low
    scale = ADAPTER_STRENGTH / rank_ref[...].astype(jnp.float32)
    update_ref[...] = scale * jnp.dot(
        low, up_ref[...], preferred_element_type=jnp.float32
    )


def low_and_update(z_n, place, live_rank, tokens, slices):
    rows, width = tokens.shape
    rank, slice_width = slices[0].shape
    depth = width // z_n
    up_width = slice_width - depth
    features = up_width * z_n
    smem = pl.BlockSpec(memory_space=pltpu.SMEM)
    vmem = pl.BlockSpec(memory_space=pltpu.VMEM)
    if depth % 128 == 0 and up_width % 128 == 0:
        return pl.pallas_call(
            functools.partial(low_kernel, z_n),
            in_specs=[smem, vmem, pl.BlockSpec(memory_space=pltpu.HBM)] + [vmem] * z_n,
            out_specs=[vmem] * 3,
            out_shape=[
                jax.ShapeDtypeStruct((rows, rank), jnp.bfloat16),
                jax.ShapeDtypeStruct((rank, features), jnp.bfloat16),
                jax.ShapeDtypeStruct((rows, features), jnp.float32),
            ],
            scratch_shapes=[pltpu.VMEM((rows, width), tokens.dtype), pltpu.SemaphoreType.DMA],
            compiler_params=pltpu.CompilerParams(vmem_limit_bytes=16 * 1024 * 1024),
        )(place, live_rank, tokens, *slices)
    z = place[0]
    stack = jnp.stack(slices)[(jnp.arange(z_n) - z) % z_n]
    down = jnp.swapaxes(stack[:, :, :depth], 0, 1).reshape(rank, width)
    up = jnp.swapaxes(stack[:, :, depth:], 0, 1).reshape(rank, features)
    low = lax.dot_general(
        tokens, down, (((1,), (1,)), ((), ())), preferred_element_type=jnp.float32
    )
    live = jnp.arange(rank, dtype=jnp.int32)[None, :] < live_rank
    low = jnp.where(live, low, 0.0).astype(jnp.bfloat16)
    scale = ADAPTER_STRENGTH / live_rank.astype(jnp.float32)
    return low, up, scale * jnp.dot(low, up, preferred_element_type=jnp.float32)


def norm_kernel(
    z_n, units, place_ref, columns_ref, rank_ref, *refs,
):
    base_refs, refs = refs[: 2 * units], refs[2 * units :]
    update_ref, low_ref, up_ref, cosine_ref, sine_ref, gain_ref = refs[:6]
    gradient_ref, tokens_ref, keys_ref = refs[6:9]
    refs = refs[9:]
    sent_refs, (tokens_buffer, gradient_buffer, part_up, semaphores) = refs[:-4], refs[-4:]
    fetch_gradient = pltpu.make_async_copy(gradient_ref, gradient_buffer, semaphores.at[0])
    fetch_tokens = pltpu.make_async_copy(tokens_ref, tokens_buffer, semaphores.at[1])
    fetch_gradient.start()
    fetch_tokens.start()
    z, core = place_ref[0], place_ref[1] % 2
    scale = ADAPTER_STRENGTH / rank_ref[...].astype(jnp.float32)
    head = gain_ref.shape[1]
    width = base_refs[0].shape[1]
    half = units * width
    low = low_ref[...]
    cosine, sine, gain = cosine_ref[...], sine_ref[...], gain_ref[...]
    gain_cosine, gain_sine = cosine * gain, sine * pltpu.roll(gain, head // 2, 1)
    grad_low = None
    fetch_gradient.wait()
    for n, base_ref in enumerate(base_refs):
        first = (core if n < units else 1 - core) * half + columns_ref[n % units]
        for i in range(width // head):
            at = pl.ds(pl.multiple_of(first + i * head, 128), head)
            up = up_ref[:, at]
            pre = base_ref[:, i * head : (i + 1) * head] + update_ref[:, at]
            inverse = lax.rsqrt(jnp.mean(pre * pre, axis=1, keepdims=True) + 1e-06)
            unit = pre * inverse
            keys = unit * gain_cosine + pltpu.roll(unit, head // 2, 1) * gain_sine
            keys_ref[:, at] = keys.astype(keys_ref.dtype)
            gradient = gradient_buffer[:, at].astype(jnp.float32)
            turned = gain * (gradient * cosine - pltpu.roll(gradient, head // 2, 1) * sine)
            along = jnp.mean(turned * unit, axis=1, keepdims=True)
            scaled = ((scale * inverse) * (turned - unit * along)).astype(jnp.bfloat16)
            part_low = lax.dot_general(
                scaled, up, (((1,), (1,)), ((), ())), preferred_element_type=jnp.float32
            )
            grad_low = part_low if grad_low is None else grad_low + part_low
            part_up[:, at] = lax.dot_general(
                low, scaled, (((0,), (0,)), ((), ())), preferred_element_type=jnp.float32
            ).astype(part_up.dtype)
    live = lax.broadcasted_iota(jnp.int32, (1, low.shape[1]), 1) < rank_ref[...]
    grad_low = jnp.where(live, grad_low, 0.0).astype(jnp.bfloat16)
    fetch_tokens.wait()
    if len(sent_refs) == 2:
        sent_refs[0][...] = lax.dot_general(
            grad_low, tokens_buffer[...], (((0,), (0,)), ((), ())),
            preferred_element_type=jnp.float32,
        ).astype(jnp.bfloat16)
        sent_refs[1][...] = part_up[...]
        return
    depth = tokens_ref.shape[1] // z_n
    up_width = part_up.shape[1] // z_n
    for j in range(z_n):
        f = (z + j) % z_n
        sent_refs[j][:, :depth] = lax.dot_general(
            grad_low,
            tokens_buffer[:, pl.ds(pl.multiple_of(f * depth, 128), depth)],
            (((0,), (0,)), ((), ())),
            preferred_element_type=jnp.float32,
        ).astype(jnp.bfloat16)
        sent_refs[j][:, depth:] = part_up[:, pl.ds(pl.multiple_of(f * up_width, 128), up_width)]


def norm_and_back(
    z_n, place, columns, live_rank, bases, update, low, up, cosine, sine, gain,
    gradient, tokens,
):
    rows, features = gradient.shape
    rank = up.shape[0]
    width = tokens.shape[1]
    depth, up_width = width // z_n, features // z_n
    aligned = depth % 128 == 0 and up_width % 128 == 0
    if aligned:
        sent = [jax.ShapeDtypeStruct((rank, depth + up_width), jnp.bfloat16)] * z_n
    else:
        sent = [
            jax.ShapeDtypeStruct((rank, width), jnp.bfloat16),
            jax.ShapeDtypeStruct((rank, features), jnp.bfloat16),
        ]
    smem = pl.BlockSpec(memory_space=pltpu.SMEM)
    vmem = pl.BlockSpec(memory_space=pltpu.VMEM)
    hbm = pl.BlockSpec(memory_space=pltpu.HBM)
    outs = pl.pallas_call(
        functools.partial(norm_kernel, z_n, len(bases) // 2),
        in_specs=[smem] * 2 + [vmem] * (len(bases) + 7) + [hbm] * 2,
        out_specs=[vmem] * (1 + len(sent)),
        out_shape=[jax.ShapeDtypeStruct((rows, features), jnp.bfloat16)] + sent,
        scratch_shapes=[
            pltpu.VMEM((rows, width), tokens.dtype),
            pltpu.VMEM((rows, features), gradient.dtype),
            pltpu.VMEM((rank, features), jnp.bfloat16),
            pltpu.SemaphoreType.DMA((2,)),
        ],
        compiler_params=pltpu.CompilerParams(vmem_limit_bytes=24 * 1024 * 1024),
    )(
        place, columns, live_rank, *bases, update, low, up, cosine, sine, gain,
        gradient, tokens,
    )
    if aligned:
        return outs[0], outs[1:]
    z = place[0]
    return outs[0], [
        jnp.concatenate(
            [
                lax.dynamic_slice(outs[1], (0, ((z + j) % z_n) * depth), (rank, depth)),
                lax.dynamic_slice(outs[2], (0, ((z + j) % z_n) * up_width), (rank, up_width)),
            ],
            axis=1,
        )
        for j in range(z_n)
    ]


def dots_kernel(z_n, shards, totals, place_ref, tokens_ref, pair_ref, *refs):
    count = sum(len(group) for group in shards)
    unit_refs, refs = refs[:count], refs[count:]
    total_refs, out_refs = refs[: 2 * totals], refs[2 * totals : 2 * totals + 2 * len(shards)]
    buffers, semaphores = refs[-4:-2], refs[-2:]
    depth = unit_refs[0].shape[0]
    only = {d for group in shards for d in group}
    fetches = []
    for side, ref in enumerate((tokens_ref, pair_ref)):
        if len(only) == 1:
            at = pl.multiple_of(((place_ref[0] - min(only) + z_n) % z_n) * depth, 128)
            ref = ref.at[:, pl.ds(at, depth)]
        fetches.append(pltpu.make_async_copy(ref, buffers[side], semaphores[side]))
        fetches[side].start()
    for side in range(2):
        fetches[side].wait()
        n = 0
        for u, group in enumerate(shards):
            value = None
            for d in group:
                at = pl.multiple_of(((place_ref[0] - d + z_n) % z_n) * depth, 128)
                left = (
                    buffers[side][...]
                    if len(only) == 1
                    else buffers[side][:, pl.ds(at, depth)]
                )
                part = jnp.dot(left, unit_refs[n][...], preferred_element_type=jnp.float32)
                value = part if value is None else value + part
                n += 1
            if totals:
                value = value + total_refs[side * totals + u][...]
            out_refs[side * len(shards) + u][...] = value


def add_dots(z_n, place, tokens, pair, shards, units, totals):
    rows = tokens.shape[0]
    depth, width = units[0][0].shape
    count = len(shards)
    if depth % 128 or width % 128:
        outs = []
        for side, array in enumerate((tokens, pair)):
            for u, group in enumerate(shards):
                value = totals[side * count + u] if totals else 0.0
                for d, unit in zip(group, units[u]):
                    at = ((place[0] - d) % z_n) * depth
                    value = value + jnp.dot(
                        lax.dynamic_slice(array, (0, at), (rows, depth)),
                        unit,
                        preferred_element_type=jnp.float32,
                    )
                outs.append(value)
        return outs
    hbm = pl.BlockSpec(memory_space=pltpu.HBM)
    vmem = pl.BlockSpec(memory_space=pltpu.VMEM)
    flat = [unit for group in units for unit in group]
    only = {d for group in shards for d in group}
    buffer = pltpu.VMEM((rows, depth if len(only) == 1 else tokens.shape[1]), tokens.dtype)
    outs = pl.pallas_call(
        functools.partial(dots_kernel, z_n, shards, len(totals) // 2),
        in_specs=[pl.BlockSpec(memory_space=pltpu.SMEM), hbm, hbm]
        + [vmem] * (len(flat) + len(totals)),
        out_specs=[vmem] * (2 * count),
        out_shape=[jax.ShapeDtypeStruct((rows, width), jnp.float32)] * (2 * count),
        scratch_shapes=[buffer, buffer, pltpu.SemaphoreType.DMA, pltpu.SemaphoreType.DMA],
        compiler_params=pltpu.CompilerParams(vmem_limit_bytes=20 * 1024 * 1024),
    )(place, tokens, pair, *flat, *totals)
    return list(outs)


def after(value, *others):
    return lax.optimization_barrier((value,) + others)[0]


def per_device(
    tokens,
    frozen_key_weight,
    key_norm_gain,
    adapter_down_weight,
    adapter_up_weight,
    packed_block_adapter,
    adapter_storage_row,
    live_adapter_rank,
    document_numbers,
    rotated_key_gradient,
):
    rows = tokens.shape[0]
    features = rotated_key_gradient.shape[1]
    depth = frozen_key_weight.shape[0]
    owned, rank, down_width = adapter_down_weight.shape
    up_width = adapter_up_weight.shape[2]
    copies_n = lax.axis_size("copies")
    z_n = lax.axis_size("fsdp")
    group_n = lax.axis_size("adapter")
    x_n = group_n // 2
    y = lax.axis_index("copies")
    z = lax.axis_index("fsdp")
    a = lax.axis_index("adapter")
    x, core = a // 2, a % 2

    def over_core(v):
        return lax.ppermute(v, "adapter", [(i, i ^ 1) for i in range(group_n)])

    def over_x(v, e):
        return lax.ppermute(
            v, "adapter", [(i, ((i // 2 + e) % x_n) * 2 + i % 2) for i in range(group_n)]
        )

    def over_y(v, g):
        return lax.ppermute(v, "copies", [(i, (i + g) % copies_n) for i in range(copies_n)])

    def over_z(v, d):
        return lax.ppermute(v, "fsdp", [(i, (i + d) % z_n) for i in range(z_n)])

    half = features // 2
    units = copies_n * x_n
    unit_width = half // units

    def unit_at(y_at, x_at):
        at = core * half + (y_at * x_n + x_at) * unit_width
        return lax.dynamic_slice(frozen_key_weight, (0, at), (depth, unit_width))

    unit = unit_at(y, x)
    sizes = (x_n, z_n)
    place = jnp.stack([z, a]).astype(jnp.int32)
    numbers = jnp.concatenate([place, packed_block_adapter, adapter_storage_row])
    shifts = sorted(range(1, z_n), key=lambda d: min(d, z_n - d))
    final = len(shifts) - 1

    tokens_pair = over_core(tokens)
    picked = pick_rows(sizes, numbers, adapter_down_weight, adapter_up_weight)
    taken = [over_core(picked[x_n + e]) for e in range(x_n)]
    away = [picked[e] + after(taken[e], tokens_pair, taken[0]) for e in range(1, x_n)]
    slices = picked[0] + taken[0]
    from_z = {d: over_z(unit if k < 2 else after(unit, *away), d) for k, d in enumerate(shifts)}
    for e in range(1, x_n):
        slices = slices + over_x(away[e - 1], e)

    documents, packed, ranks, gain = lax.optimization_barrier(
        (
            document_numbers,
            packed_block_adapter,
            live_adapter_rank,
            key_norm_gain,
            away[0],
        )
    )[:4]
    mine = jnp.arange(packed.shape[0], dtype=jnp.int32) == z * group_n + a
    mine = jnp.arange(ranks.shape[0], dtype=jnp.int32) == jnp.sum(jnp.where(mine, packed, 0))
    live_rank = jnp.sum(jnp.where(mine, ranks, 0)).reshape(1, 1)
    cosine_part, sine_part = rope_tables(doc_positions(documents), key_norm_gain.shape[0])
    cosine = jnp.concatenate([cosine_part, cosine_part], axis=1)
    sine = jnp.concatenate([-sine_part, sine_part], axis=1)

    frozen_key_weight = after(frozen_key_weight, away[0])
    own_units = [
        unit_at((y - g) % copies_n, (x - e) % x_n) for g in range(copies_n) for e in range(x_n)
    ]
    along_x, along_y, diagonal = [], [], []
    for k, d in enumerate(shifts):
        gate = away[0] if k < 2 else along_y[k - 2][-1]
        along_y.append([over_y(after(from_z[d], gate), g) for g in range(1, copies_n)])
    for k, d in enumerate(shifts):
        gate = (away[0], along_y[0][-1], slices)[min(k, 2)]
        along_x.append([over_x(after(from_z[d], gate), e) for e in range(1, x_n)])
    for k, d in enumerate(shifts):
        if k < final:
            gate = along_y[k + 1][-1]
            diagonal.append(
                [[over_y(after(v, gate), g) for v in along_x[k]] for g in range(1, copies_n)]
            )
    adapter_slices = {0: slices[0]}
    for k, d in enumerate(shifts):
        gates = (along_x[0][-1],) if k >= 2 else ()
        adapter_slices[(-d) % z_n] = over_z(after(slices[d], *gates), d)
    diagonal.append(
        [
            [over_x(after(v, along_x[max(final - 1, 0)][-1]), e) for e in range(1, x_n)]
            for v in along_y[final]
        ]
    )
    shards = {0: own_units}
    for k, d in enumerate(shifts):
        shards[d] = [from_z[d]] + along_x[k]
        for g in range(1, copies_n):
            shards[d] += [along_y[k][g - 1]] + diagonal[k][g - 1]
    order = [0] + shifts
    groups = [order] * (units - 1) + [order[:-1]]
    first = add_dots(
        z_n,
        after(place, cosine, sine, live_rank, *adapter_slices.values()),
        tokens,
        tokens_pair,
        groups,
        [[shards[d][u] for d in group] for u, group in enumerate(groups)],
        [],
    )
    last = add_dots(
        z_n,
        place,
        tokens,
        tokens_pair,
        [order[-1:]],
        [[shards[order[-1]][-1]]],
        [first[units - 1], first[-1]],
    )
    bases = first[: units - 1] + [last[0]]
    bases += [over_core(v) for v in first[units:-1] + [last[1]]]
    head = key_norm_gain.shape[0]
    columns = [
        (((y - g) % copies_n) * x_n + (x - e) % x_n) * unit_width
        for g in range(copies_n)
        for e in range(x_n)
    ]
    if unit_width % head:
        natural = []
        for side in (bases[:units], bases[units:]):
            stack = jnp.stack(side)
            order = jnp.stack(
                [
                    ((y - y_at) % copies_n) * x_n + (x - x_at) % x_n
                    for y_at in range(copies_n)
                    for x_at in range(x_n)
                ]
            )
            whole = jnp.swapaxes(stack[order], 0, 1).reshape(rows, half)
            natural.append(whole)
        bases = natural
        columns = [jnp.zeros_like(z)]

    low, up, update = low_and_update(
        z_n,
        place,
        live_rank,
        tokens,
        [adapter_slices[j] for j in range(z_n)],
    )
    rotated, sent = norm_and_back(
        z_n,
        place,
        jnp.stack(columns).astype(jnp.int32),
        live_rank,
        bases,
        update,
        low,
        up,
        cosine,
        sine,
        gain[None],
        rotated_key_gradient,
        tokens,
    )
    order = [0] + shifts if z_n <= 4 else list(range(z_n))
    step = -(-z_n // 4)
    groups = [tuple(order[k : k + step]) for k in range(0, z_n, step)]
    arrived = {d: sent[0] if d == 0 else over_z(sent[d], d) for d in order}
    blocks = []
    for group in groups:
        if len(group) == 1:
            here = arrived[group[0]][None]
        else:
            here = jnp.stack([arrived[d] for d in group])
        for e in range(x_n):
            there = over_x(here, e) if e else here
            blocks += [there, over_core(there)]
    grad_down, grad_up = owner_sum(
        sizes,
        groups,
        numbers,
        blocks,
        owned,
        down_width,
    )
    return (rotated, grad_down, grad_up)


def solution(mesh):
    return jax.shard_map(
        per_device,
        mesh=mesh,
        in_specs=(
            P(("copies", "fsdp", "adapter"), None),
            P("fsdp", None),
            P(),
            P("adapter", None, "fsdp"),
            P("adapter", None, "fsdp"),
            P("copies"),
            P(),
            P(),
            P(("copies", "fsdp", "adapter")),
            P(("copies", "fsdp", "adapter"), None),
        ),
        out_specs=(
            P(("copies", "fsdp", "adapter"), None),
            P(("copies", "adapter"), None, "fsdp"),
            P(("copies", "adapter"), None, "fsdp"),
        ),
        check_vma=False,
    )
```

time: 429 us -> 125 us (0.29)
  waiting for transfers between devices: 310 us -> 35.8 us
  starting transfers between devices: 9.36 us -> 46.1 us
  matrix products: 28.7 us -> 0 us
  blocking collectives: 28.4 us -> 0 us
  Pallas kernels: 0 us -> 24.3 us
  local copies, waits for them, and re-layouts: 22 us -> 7.32 us
  between operations: 14.8 us -> 0.93 us
  other arithmetic: 15.7 us -> 8.77 us
    all_gather x3 -> x0, waiting for transfers between devices: 214 us -> none  [the longest x1 147 us: per_device(): lax.all_gather(frozen_key_weight, 'fsdp', axis=0, tiled=True)]
    reduce_scatter x2 -> x0, waiting for transfers between devices: 63.4 us -> none  [the longest x1 63.4 us: per_device(): lax.psum_scatter(rows_down.astype(jnp.bfloat16), 'adapter', scatter_dimen...]
    ppermute x0 -> x38, starting transfers between devices: none -> 46.1 us  [the longest x9 25.9 us: over_z(): return lax.ppermute(v, 'fsdp', [(i, (i + d) % z_n) for i in range(z_n)])]
    ppermute x0 -> x38, waiting for transfers between devices: none -> 35.8 us  [the longest x9 26.1 us: over_z(): return lax.ppermute(v, 'fsdp', [(i, (i + d) % z_n) for i in range(z_n)])]
    all_to_all x2 -> x0, waiting for transfers between devices: 30.6 us -> none  [the longest x1 30.6 us: per_device(): lax.all_to_all(send_down, 'fsdp', split_axis=2, concat_axis=2, tiled=True)]
    dot_general x9 -> x0, matrix products: 28.7 us -> none  [the longest x1 11.7 us: per_device(): jnp.einsum('jbs,srd->brjd', select_rows, tables_down, preferred_element_t...]
    all_to_all x2 -> x0, blocking collectives: 28.4 us -> none  [the longest x1 19.6 us: per_device(): lax.all_to_all(part_down.astype(jnp.bfloat16), 'fsdp', split_axis=2, conc...]
    pallas_call x0 -> x6, Pallas kernels: none -> 24.3 us  [the longest x2 8.61 us: add_dots(): pl.pallas_call(functools.partial(dots_kernel, z_n, shards, len(totals) //...]
  transfers between devices with their start and end apart: 7 -> 38, of which waited for: 5 -> 11; matrix products, arithmetic and copies ran while one was open for 10% -> 10% of each run, Pallas kernels for 0% -> 13%
where the time goes in v2:
time: 125 us; the launch traced here: 123 us
  starting transfers between devices  46.1 us (37%)
  waiting for transfers between devices  35.8 us (29%)
  Pallas kernels  24.3 us (19%)
  other arithmetic  8.77 us (7%)
  local copies, waits for them, and re-layouts  7.32 us (6%)
    ppermute x9, waiting for transfers between devices, over_z(): return lax.ppermute(v, 'fsdp', [(i, (i + d) % z_n) for i in range(z_n)])  26.1 us
    ppermute x9, starting transfers between devices, over_z(): return lax.ppermute(v, 'fsdp', [(i, (i + d) % z_n) for i in range(z_n)])  25.9 us
    ppermute x9, starting transfers between devices, over_x(): lax.ppermute(v, 'adapter', [(i, (i // 2 + e) % x_n * 2 + i % 2) for i in...  10.2 us
    pallas_call x2, Pallas kernels, add_dots(): pl.pallas_call(functools.partial(dots_kernel, z_n, shards, len(totals) //...  8.61 us
    ppermute x5, starting transfers between devices, over_y(): lax.ppermute(v, 'copies', [(i, (i + g) % copies_n) for i in range(copies_...  6.25 us
    ppermute x9, waiting for transfers between devices, over_x(): lax.ppermute(v, 'adapter', [(i, (i // 2 + e) % x_n * 2 + i % 2) for i in...  5.87 us
    pallas_call x1, Pallas kernels, norm_and_back(): pl.pallas_call(functools.partial(norm_kernel, z_n, len(bases) // 2), in_s...  4.84 us
    pallas_call x1, Pallas kernels, pick_rows(): pl.pallas_call(functools.partial(pick_kernel, sizes), in_specs=[pl.BlockS...  4.47 us
  transfers between devices with their start and end apart: 38, of which 11 were waited for; matrix products, arithmetic and copies ran while one was open for 10% of the time, Pallas kernels for 13%

profile of v2, /device:TPU:0, one launch (start us, length us, event | category | flops | bytes accessed | tf_op | source)
XLA Modules:
  0.0 123.2 jit_solution(11694768968991307042)
XLA Ops:
  4.4 4.5 %shard_map.121 = (bf16[4,64,1536]{2,1,0:T(8,128)(2,1)S(1)}, bf16[4,64,1536]{2,1,0:T(8,128)(2,1)S(1)}, bf16[4,64,1536]{2,1,0:T(8,128)(2,1)}, bf16[4,64,1536]{2,1,0:T(8,128)(2,1)}) custom-call(s32[66]{0:T(128)S(1)} %pad_add_fusion.2.numbers, bf16[12,64,1280]{2,1,0:T(8,128)(2,1)S(1)} %copy-done.1, bf16[12,64,256]{2,1,0:T(8,128)(2,1)S(1)} %copy-done.4), custom_call_target="tpu_custom_call" | custom-call | tf_op jit(solution)/shard_map/pallas_call | solution.py:85
  10.3 1.7 %constant_dynamic-slice_fusion.4 = bf16[1280,128]{1,0:T(8,128)(2,1)} fusion(bf16[1280,1024]{1,0:T(8,128)(2,1)} %param.11, s32[]{:T(128)S(6)} %select_n.94), kind=kLoop, calls=%fused_computation.18 | loop fusion | bytes 655364 | tf_op jit(solution)/shard_map/dynamic_slice | solution.py:459
  12.0 2.6 %collective-permute-start.6 = (bf16[1280,128]{1,0:T(8,128)(2,1)}, bf16[1280,128]{1,0:T(8,128)(2,1)}, u32[]{:S(2)}, u32[]{:S(2)}) collective-permute-start(bf16[1280,128]{1,0:T(8,128)(2,1)} %constant_dynamic-slice_fusion.4), channel_id=1, source_target_pairs={{0,4},{4,8},{8,12},{12,0},{1,5},{5,9},{9,13},{13,1},{2,6},{6,10},{... | collective-permute-start | bytes 983048 | tf_op jit(solution)/shard_map/ppermute | solution.py:451
  14.6 2.0 %collective-permute-start.9 = (bf16[1280,128]{1,0:T(8,128)(2,1)}, bf16[1280,128]{1,0:T(8,128)(2,1)}, u32[]{:S(2)}, u32[]{:S(2)}) collective-permute-start(bf16[1280,128]{1,0:T(8,128)(2,1)} %constant_dynamic-slice_fusion.4), channel_id=1, source_target_pairs={{0,12},{4,0},{8,4},{12,8},{1,13},{5,1},{9,5},{13,9},{2,14},{6,2},{... | collective-permute-start | bytes 983048 | tf_op jit(solution)/shard_map/ppermute | solution.py:451
  16.8 2.4 %add.107 = bf16[4,64,1536]{2,1,0:T(8,128)(2,1)} add(bf16[4,64,1536]{2,1,0:T(8,128)(2,1)} %copy-done.2, bf16[4,64,1536]{2,1,0:T(8,128)(2,1)} %collective-permute-done) | non-fusion elementwise | flops 393216 | bytes 2359296 | tf_op jit(solution)/shard_map/add | solution.py:471
  19.2 2.2 %collective-permute-start.3 = (bf16[4,64,1536]{2,1,0:T(8,128)(2,1)}, bf16[4,64,1536]{2,1,0:T(8,128)(2,1)}, u32[]{:S(2)}, u32[]{:S(2)}) collective-permute-start(bf16[4,64,1536]{2,1,0:T(8,128)(2,1)} %add.107), channel_id=1, source_target_pairs={{0,2},{1,3},{2,0},{3,1},{4,6},{5,7},{6,4},{7,5},{8,10},{9,11},{10,... | collective-permute-start | bytes 2359304 | tf_op jit(solution)/shard_map/ppermute | solution.py:443
  21.4 4.1 %collective-permute-done.6.refs_1_ = bf16[1280,128]{1,0:T(8,128)(2,1)} collective-permute-done((bf16[1280,128]{1,0:T(8,128)(2,1)}, bf16[1280,128]{1,0:T(8,128)(2,1)}, u32[]{:S(2)}, u32[]{:S(2)}) %collective-permute-start.6) | collective-permute-done | bytes 327712 | tf_op jit(solution)/shard_map/ppermute | solution.py:451
  25.5 2.2 %collective-permute-start.7 = (bf16[1280,128]{1,0:T(8,128)(2,1)}, bf16[1280,128]{1,0:T(8,128)(2,1)}, u32[]{:S(2)}, u32[]{:S(2)}) collective-permute-start(bf16[1280,128]{1,0:T(8,128)(2,1)} %collective-permute-done.6.refs_1_), channel_id=1, source_target_pairs={{0,2},{1,3},{2,0},{3,1},{4,6},{5,7},{6,4},{7,5},{8,10},{9,11},{10,... | collective-permute-start | bytes 983048 | tf_op jit(solution)/shard_map/ppermute | solution.py:443
  30.4 10.6 %collective-permute-start.10 = (bf16[1280,128]{1,0:T(8,128)(2,1)}, bf16[1280,128]{1,0:T(8,128)(2,1)S(1)}, u32[]{:S(2)}, u32[]{:S(2)}) collective-permute-start(bf16[1280,128]{1,0:T(8,128)(2,1)} %constant_dynamic-slice_fusion.4), channel_id=1, source_target_pairs={{0,8},{4,12},{8,0},{12,4},{1,9},{5,13},{9,1},{13,5},{2,10},{6,14},... | collective-permute-start | bytes 983048 | tf_op jit(solution)/shard_map/ppermute | solution.py:451
  44.0 5.2 %collective-permute-done.10.refs_3_ = bf16[1280,128]{1,0:T(8,128)(2,1)S(1)} collective-permute-done((bf16[1280,128]{1,0:T(8,128)(2,1)}, bf16[1280,128]{1,0:T(8,128)(2,1)S(1)}, u32[]{:S(2)}, u32[]{:S(2)}) %collective-permute-start.10) | collective-permute-done | bytes 327712 | tf_op jit(solution)/shard_map/ppermute | solution.py:451
  49.2 2.6 %collective-permute-start.15 = (bf16[1280,128]{1,0:T(8,128)(2,1)S(1)}, bf16[1280,128]{1,0:T(8,128)(2,1)S(1)}, u32[]{:S(2)}, u32[]{:S(2)}) collective-permute-start(bf16[1280,128]{1,0:T(8,128)(2,1)S(1)} %collective-permute-done.10.refs_3_), channel_id=1, source_target_pairs={{0,16},{16,0},{1,17},{17,1},{2,18},{18,2},{3,19},{19,3},{4,20},{20... | collective-permute-start | bytes 983048 | tf_op jit(solution)/shard_map/ppermute | solution.py:448
  51.8 1.7 %add_add_fusion = bf16[4,64,1536]{2,1,0:T(8,128)(2,1)S(1)} fusion(bf16[4,64,1536]{2,1,0:T(8,128)(2,1)} %collective-permute-done.3, bf16[4,64,1536]{2,1,0:T(8,128)(2,1)S(1)} %get-tuple-element.51, bf16[4,64,1536]{2,1,0:T(8,128)(2,1)} %collective-permute-done.2), kind=kLoop, calls=%fused_computation | loop fusion | flops 786432 | bytes 3145728 | tf_op jit(solution)/shard_map/add | solution.py:475
  53.6 3.8 %collective-permute-start.5 = (bf16[64,1536]{1,0:T(8,128)(2,1)S(1)}, bf16[64,1536]{1,0:T(8,128)(2,1)S(1)}, u32[]{:S(2)}, u32[]{:S(2)}) collective-permute-start(bf16[64,1536]{1,0:T(8,128)(2,1)S(1)} %get-tuple-element.90), channel_id=1, source_target_pairs={{0,12},{4,0},{8,4},{12,8},{1,13},{5,1},{9,5},{13,9},{2,14},{6,2},{... | collective-permute-start | bytes 589832 | tf_op jit(solution)/shard_map/ppermute | solution.py:451
  58.1 2.3 %collective-permute-done.15.refs_11_ = bf16[1280,128]{1,0:T(8,128)(2,1)S(1)} collective-permute-done((bf16[1280,128]{1,0:T(8,128)(2,1)S(1)}, bf16[1280,128]{1,0:T(8,128)(2,1)S(1)}, u32[]{:S(2)}, u32[]{:S(2)}) %collective-permute-start.15) | collective-permute-done | bytes 327712 | tf_op jit(solution)/shard_map/ppermute | solution.py:448
  64.3 1.8 %collective-permute-start.8 = (bf16[64,1536]{1,0:T(8,128)(2,1)S(1)}, bf16[64,1536]{1,0:T(8,128)(2,1)S(1)}, u32[]{:S(2)}, u32[]{:S(2)}) collective-permute-start(bf16[64,1536]{1,0:T(8,128)(2,1)S(1)} %get-tuple-element.53), channel_id=1, source_target_pairs={{0,8},{4,12},{8,0},{12,4},{1,9},{5,13},{9,1},{13,5},{2,10},{6,14},... | collective-permute-start | bytes 589832 | tf_op jit(solution)/shard_map/ppermute | solution.py:451
  67.5 3.3 %collective-permute-done.8.refs_2_ = bf16[64,1536]{1,0:T(8,128)(2,1)S(1)} collective-permute-done((bf16[64,1536]{1,0:T(8,128)(2,1)S(1)}, bf16[64,1536]{1,0:T(8,128)(2,1)S(1)}, u32[]{:S(2)}, u32[]{:S(2)}) %collective-permute-start.8) | collective-permute-done | bytes 196640 | tf_op jit(solution)/shard_map/ppermute | solution.py:451
  72.2 7.2 %shard_map.122 = (f32[256,128]{1,0:T(8,128)S(1)}, f32[256,128]{1,0:T(8,128)S(1)}, f32[256,128]{1,0:T(8,128)S(1)}, f32[256,128]{1,0:T(8,128)S(1)}, f32[256,128]{1...) custom-call(s32[2]{0:T(128)S(1)} %pad_add_fusion.place_ref, ...), custom_call_target="tpu_custom_call" | custom-call | tf_op jit(solution)/shard_map/pallas_call | solution.py:397
  82.1 2.7 %shard_map.124 = (bf16[256,64]{1,0:T(8,128)(2,1)S(1)}, bf16[64,1024]{1,0:T(8,128)(2,1)S(1)}, f32[256,1024]{1,0:T(8,128)S(1)}) custom-call(s32[2]{0:T(128)S(1)} %pad_add_fusion.place_ref, s32[1,1]{1,0:T(1,128)} %bitcast.6.rank_ref, bf16[256,5120]{1,0:T(8,128)(2,1)S(1)} %copy-done, bf16[64,1536]{1,0:T(8,128)(2,1)S(1)} %get-tuple-element.92.refs_0_, ...), custom_call_target="tpu_custom_call" | custom-call | tf_op jit(solution)/shard_map/pallas_call | solution.py:199
  84.9 4.8 %shard_map.125 = (bf16[256,1024]{1,0:T(8,128)(2,1)}, bf16[64,1536]{1,0:T(8,128)(2,1)S(1)}, bf16[64,1536]{1,0:T(8,128)(2,1)S(1)}, bf16[64,1536]{1,0:T(8,128)(2,1)S(1)}, bf16[64,1536]{1,0:T(8,128)(2,1)S(1)}) custom-call(s32[2]{0:T(128)S(1)} %pad_add_fusion.place_ref, s32[4]{0:T(128)S(1)} %pad_add_fusion.1.columns_ref, s32[1,1]{1,0:T(1,128)} %bitcast.6.rank_ref, ...), custom_call_target="tpu_custom_call" | custom-call | tf_op jit(solution)/shard_map/pallas_call | solution.py:309
  91.4 3.5 %collective-permute-start.30 = (bf16[64,1536]{1,0:T(8,128)(2,1)S(1)}, bf16[64,1536]{1,0:T(8,128)(2,1)S(1)}, u32[]{:S(2)}, u32[]{:S(2)}) collective-permute-start(bf16[64,1536]{1,0:T(8,128)(2,1)S(1)} %get-tuple-element.81), channel_id=1, source_target_pairs={{0,12},{4,0},{8,4},{12,8},{1,13},{5,1},{9,5},{13,9},{2,14},{6,2},{... | collective-permute-start | bytes 589832 | tf_op jit(solution)/shard_map/ppermute | solution.py:451
  94.9 4.4 %collective-permute-done.26 = bf16[64,1536]{1,0:T(8,128)(2,1)S(1)} collective-permute-done((bf16[64,1536]{1,0:T(8,128)(2,1)S(1)}, bf16[64,1536]{1,0:T(8,128)(2,1)S(1)}, u32[]{:S(2)}, u32[]{:S(2)}) %collective-permute-start.26) | collective-permute-done | bytes 196640 | tf_op jit(solution)/shard_map/ppermute | solution.py:451
  104.0 7.1 %collective-permute-done.34 = bf16[64,1536]{1,0:T(8,128)(2,1)S(1)} collective-permute-done((bf16[64,1536]{1,0:T(8,128)(2,1)S(1)}, bf16[64,1536]{1,0:T(8,128)(2,1)S(1)}, u32[]{:S(2)}, u32[]{:S(2)}) %collective-permute-start.34) | collective-permute-done | bytes 196640 | tf_op jit(solution)/shard_map/ppermute | solution.py:451
  113.5 4.5 %collective-permute-done.36.refs_14_ = bf16[1,64,1536]{2,1,0:T(8,128)(2,1)S(1)} collective-permute-done((bf16[1,64,1536]{2,1,0:T(8,128)(2,1)S(1)}, bf16[1,64,1536]{2,1,0:T(8,128)(2,1)S(1)}, u32[]{:S(2)}, u32[]{:S(2)}) %collective-permute-start.36) | collective-permute-done | bytes 196640 | tf_op jit(solution)/shard_map/ppermute | solution.py:443
  119.4 3.7 %shard_map.126 = (f32[12,64,1280]{2,1,0:T(8,128)}, f32[12,64,256]{2,1,0:T(8,128)}) custom-call(s32[66]{0:T(128)S(1)} %pad_add_fusion.2.numbers, bf16[1,64,1536]{2,1,0:T(8,128)(2,1)S(1)} %bitcast.29, bf16[1,64,1536]{2,1,0:T(8,128)(2,1)S(1)} %collective-permute-done.23.refs_1_, bf16[1,64,1536]{2,1,0:T(8,128)(2,1)S(1)} %collective-permute-done.24.refs_2_, ...), custom_call_target="tpu_custom_call" | custom-call | tf_op jit(solution)/shard_map/pallas_call | solution.py:140
  (96 shorter events, 31.1 us)
Async XLA Ops:
  0.6 16.1 %collective-permute-start.1 = (bf16[256,5120]{1,0:T(8,128)(2,1)}, bf16[256,5120]{1,0:T(8,128)(2,1)S(1)}, u32[]{:S(2)}, u32[]{:S(2)}) collective-permute-start(bf16[256,5120]{1,0:T(8,128)(2,1)} %refs_15_.1), channel_id=1, source_target_pairs={{0,1},{1,0},{2,3},{3,2},{4,5},{5,4},{6,7},{7,6},{8,9},{9,8},{10,11... | collective-permute-start | bytes 7864328 | tf_op jit(solution)/shard_map/ppermute | solution.py:440
  12.0 13.5 %collective-permute-start.6 = (bf16[1280,128]{1,0:T(8,128)(2,1)}, bf16[1280,128]{1,0:T(8,128)(2,1)}, u32[]{:S(2)}, u32[]{:S(2)}) collective-permute-start(bf16[1280,128]{1,0:T(8,128)(2,1)} %constant_dynamic-slice_fusion.4), channel_id=1, source_target_pairs={{0,4},{4,8},{8,12},{12,0},{1,5},{5,9},{9,13},{13,1},{2,6},{6,10},{... | collective-permute-start | bytes 983048 | tf_op jit(solution)/shard_map/ppermute | solution.py:451
  14.6 26.6 %collective-permute-start.9 = (bf16[1280,128]{1,0:T(8,128)(2,1)}, bf16[1280,128]{1,0:T(8,128)(2,1)}, u32[]{:S(2)}, u32[]{:S(2)}) collective-permute-start(bf16[1280,128]{1,0:T(8,128)(2,1)} %constant_dynamic-slice_fusion.4), channel_id=1, source_target_pairs={{0,12},{4,0},{8,4},{12,8},{1,13},{5,1},{9,5},{13,9},{2,14},{6,2},{... | collective-permute-start | bytes 983048 | tf_op jit(solution)/shard_map/ppermute | solution.py:451
  19.2 32.6 %collective-permute-start.3 = (bf16[4,64,1536]{2,1,0:T(8,128)(2,1)}, bf16[4,64,1536]{2,1,0:T(8,128)(2,1)}, u32[]{:S(2)}, u32[]{:S(2)}) collective-permute-start(bf16[4,64,1536]{2,1,0:T(8,128)(2,1)} %add.107), channel_id=1, source_target_pairs={{0,2},{1,3},{2,0},{3,1},{4,6},{5,7},{6,4},{7,5},{8,10},{9,11},{10,... | collective-permute-start | bytes 2359304 | tf_op jit(solution)/shard_map/ppermute | solution.py:443
  25.5 28.1 %collective-permute-start.7 = (bf16[1280,128]{1,0:T(8,128)(2,1)}, bf16[1280,128]{1,0:T(8,128)(2,1)}, u32[]{:S(2)}, u32[]{:S(2)}) collective-permute-start(bf16[1280,128]{1,0:T(8,128)(2,1)} %collective-permute-done.6.refs_1_), channel_id=1, source_target_pairs={{0,2},{1,3},{2,0},{3,1},{4,6},{5,7},{6,4},{7,5},{8,10},{9,11},{10,... | collective-permute-start | bytes 983048 | tf_op jit(solution)/shard_map/ppermute | solution.py:443
  27.7 16.2 %collective-permute-start.11 = (bf16[1280,128]{1,0:T(8,128)(2,1)}, bf16[1280,128]{1,0:T(8,128)(2,1)}, u32[]{:S(2)}, u32[]{:S(2)}) collective-permute-start(bf16[1280,128]{1,0:T(8,128)(2,1)} %collective-permute-done.6.refs_1_), channel_id=1, source_target_pairs={{0,16},{16,0},{1,17},{17,1},{2,18},{18,2},{3,19},{19,3},{4,20},{20... | collective-permute-start | bytes 983048 | tf_op jit(solution)/shard_map/ppermute | solution.py:448
  30.4 18.8 %collective-permute-start.10 = (bf16[1280,128]{1,0:T(8,128)(2,1)}, bf16[1280,128]{1,0:T(8,128)(2,1)S(1)}, u32[]{:S(2)}, u32[]{:S(2)}) collective-permute-start(bf16[1280,128]{1,0:T(8,128)(2,1)} %constant_dynamic-slice_fusion.4), channel_id=1, source_target_pairs={{0,8},{4,12},{8,0},{12,4},{1,9},{5,13},{9,1},{13,5},{2,10},{6,14},... | collective-permute-start | bytes 983048 | tf_op jit(solution)/shard_map/ppermute | solution.py:451
  41.3 16.7 %collective-permute-start.14 = (bf16[1280,128]{1,0:T(8,128)(2,1)}, bf16[1280,128]{1,0:T(8,128)(2,1)S(1)}, u32[]{:S(2)}, u32[]{:S(2)}) collective-permute-start(bf16[1280,128]{1,0:T(8,128)(2,1)} %collective-permute-done.9.refs_2_), channel_id=1, source_target_pairs={{0,16},{16,0},{1,17},{17,1},{2,18},{18,2},{3,19},{19,3},{4,20},{20... | collective-permute-start | bytes 983048 | tf_op jit(solution)/shard_map/ppermute | solution.py:448
  44.0 14.1 %collective-permute-start.12 = (bf16[1280,128]{1,0:T(8,128)(2,1)}, bf16[1280,128]{1,0:T(8,128)(2,1)S(1)}, u32[]{:S(2)}, u32[]{:S(2)}) collective-permute-start(bf16[1280,128]{1,0:T(8,128)(2,1)} %collective-permute-done.9.refs_2_), channel_id=1, source_target_pairs={{0,2},{1,3},{2,0},{3,1},{4,6},{5,7},{6,4},{7,5},{8,10},{9,11},{10,... | collective-permute-start | bytes 983048 | tf_op jit(solution)/shard_map/ppermute | solution.py:443
  49.2 11.2 %collective-permute-start.15 = (bf16[1280,128]{1,0:T(8,128)(2,1)S(1)}, bf16[1280,128]{1,0:T(8,128)(2,1)S(1)}, u32[]{:S(2)}, u32[]{:S(2)}) collective-permute-start(bf16[1280,128]{1,0:T(8,128)(2,1)S(1)} %collective-permute-done.10.refs_3_), channel_id=1, source_target_pairs={{0,16},{16,0},{1,17},{17,1},{2,18},{18,2},{3,19},{19,3},{4,20},{20... | collective-permute-start | bytes 983048 | tf_op jit(solution)/shard_map/ppermute | solution.py:448
  53.5 8.7 %collective-permute-start.4 = (bf16[64,1536]{1,0:T(8,128)(2,1)S(1)}, bf16[64,1536]{1,0:T(8,128)(2,1)S(1)}, u32[]{:S(2)}, u32[]{:S(2)}) collective-permute-start(bf16[64,1536]{1,0:T(8,128)(2,1)S(1)} %get-tuple-element.91), channel_id=1, source_target_pairs={{0,4},{4,8},{8,12},{12,0},{1,5},{5,9},{9,13},{13,1},{2,6},{6,10},{... | collective-permute-start | bytes 589832 | tf_op jit(solution)/shard_map/ppermute | solution.py:451
  53.6 10.7 %collective-permute-start.5 = (bf16[64,1536]{1,0:T(8,128)(2,1)S(1)}, bf16[64,1536]{1,0:T(8,128)(2,1)S(1)}, u32[]{:S(2)}, u32[]{:S(2)}) collective-permute-start(bf16[64,1536]{1,0:T(8,128)(2,1)S(1)} %get-tuple-element.90), channel_id=1, source_target_pairs={{0,12},{4,0},{8,4},{12,8},{1,13},{5,1},{9,5},{13,9},{2,14},{6,2},{... | collective-permute-start | bytes 589832 | tf_op jit(solution)/shard_map/ppermute | solution.py:451
  58.0 12.9 %collective-permute-start.16 = (bf16[1280,128]{1,0:T(8,128)(2,1)}, bf16[1280,128]{1,0:T(8,128)(2,1)S(1)}, u32[]{:S(2)}, u32[]{:S(2)}) collective-permute-start(bf16[1280,128]{1,0:T(8,128)(2,1)} %collective-permute-done.7.refs_5_), channel_id=1, source_target_pairs={{0,16},{16,0},{1,17},{17,1},{2,18},{18,2},{3,19},{19,3},{4,20},{20... | collective-permute-start | bytes 983048 | tf_op jit(solution)/shard_map/ppermute | solution.py:448
  60.4 10.5 %collective-permute-start.17 = (bf16[1280,128]{1,0:T(8,128)(2,1)S(1)}, bf16[1280,128]{1,0:T(8,128)(2,1)S(1)}, u32[]{:S(2)}, u32[]{:S(2)}) collective-permute-start(bf16[1280,128]{1,0:T(8,128)(2,1)S(1)} %collective-permute-done.12.refs_6_), channel_id=1, source_target_pairs={{0,16},{16,0},{1,17},{17,1},{2,18},{18,2},{3,19},{19,3},{4,20},{20... | collective-permute-start | bytes 983048 | tf_op jit(solution)/shard_map/ppermute | solution.py:448
  61.6 18.5 %collective-permute-start.18 = (bf16[1280,128]{1,0:T(8,128)(2,1)S(1)}, bf16[1280,128]{1,0:T(8,128)(2,1)S(1)}, u32[]{:S(2)}, u32[]{:S(2)}) collective-permute-start(bf16[1280,128]{1,0:T(8,128)(2,1)S(1)} %collective-permute-done.15.refs_11_), channel_id=1, source_target_pairs={{0,2},{1,3},{2,0},{3,1},{4,6},{5,7},{6,4},{7,5},{8,10},{9,11},{10,... | collective-permute-start | bytes 983048 | tf_op jit(solution)/shard_map/ppermute | solution.py:443
  62.2 10.0 %collective-permute-start.13 = (bf16[1280,128]{1,0:T(8,128)(2,1)S(1)}, bf16[1280,128]{1,0:T(8,128)(2,1)S(1)}, u32[]{:S(2)}, u32[]{:S(2)}) collective-permute-start(bf16[1280,128]{1,0:T(8,128)(2,1)S(1)} %collective-permute-done.10.refs_3_), channel_id=1, source_target_pairs={{0,2},{1,3},{2,0},{3,1},{4,6},{5,7},{6,4},{7,5},{8,10},{9,11},{10,... | collective-permute-start | bytes 983048 | tf_op jit(solution)/shard_map/ppermute | solution.py:443
  89.7 9.7 %collective-permute-start.26 = (bf16[64,1536]{1,0:T(8,128)(2,1)S(1)}, bf16[64,1536]{1,0:T(8,128)(2,1)S(1)}, u32[]{:S(2)}, u32[]{:S(2)}) collective-permute-start(bf16[64,1536]{1,0:T(8,128)(2,1)S(1)} %get-tuple-element.80), channel_id=1, source_target_pairs={{0,4},{4,8},{8,12},{12,0},{1,5},{5,9},{9,13},{13,1},{2,6},{6,10},{... | collective-permute-start | bytes 589832 | tf_op jit(solution)/shard_map/ppermute | solution.py:451
  91.4 8.5 %collective-permute-start.23 = (bf16[1,64,1536]{2,1,0:T(8,128)(2,1)S(1)}, bf16[1,64,1536]{2,1,0:T(8,128)(2,1)S(1)}, u32[]{:S(2)}, u32[]{:S(2)}) collective-permute-start(bf16[1,64,1536]{2,1,0:T(8,128)(2,1)S(1)} %bitcast.28), channel_id=1, source_target_pairs={{0,1},{1,0},{2,3},{3,2},{4,5},{5,4},{6,7},{7,6},{8,9},{9,8},{10,11... | collective-permute-start | bytes 589832 | tf_op jit(solution)/shard_map/ppermute | solution.py:440
  91.4 11.3 %collective-permute-start.30 = (bf16[64,1536]{1,0:T(8,128)(2,1)S(1)}, bf16[64,1536]{1,0:T(8,128)(2,1)S(1)}, u32[]{:S(2)}, u32[]{:S(2)}) collective-permute-start(bf16[64,1536]{1,0:T(8,128)(2,1)S(1)} %get-tuple-element.81), channel_id=1, source_target_pairs={{0,12},{4,0},{8,4},{12,8},{1,13},{5,1},{9,5},{13,9},{2,14},{6,2},{... | collective-permute-start | bytes 589832 | tf_op jit(solution)/shard_map/ppermute | solution.py:451
  94.9 16.2 %collective-permute-start.34 = (bf16[64,1536]{1,0:T(8,128)(2,1)S(1)}, bf16[64,1536]{1,0:T(8,128)(2,1)S(1)}, u32[]{:S(2)}, u32[]{:S(2)}) collective-permute-start(bf16[64,1536]{1,0:T(8,128)(2,1)S(1)} %get-tuple-element.82), channel_id=1, source_target_pairs={{0,8},{4,12},{8,0},{12,4},{1,9},{5,13},{9,1},{13,5},{2,10},{6,14},... | collective-permute-start | bytes 589832 | tf_op jit(solution)/shard_map/ppermute | solution.py:451
  99.4 13.1 %collective-permute-start.27 = (bf16[1,64,1536]{2,1,0:T(8,128)(2,1)S(1)}, bf16[1,64,1536]{2,1,0:T(8,128)(2,1)S(1)}, u32[]{:S(2)}, u32[]{:S(2)}) collective-permute-start(bf16[1,64,1536]{2,1,0:T(8,128)(2,1)S(1)} %bitcast.30), channel_id=1, source_target_pairs={{0,1},{1,0},{2,3},{3,2},{4,5},{5,4},{6,7},{7,6},{8,9},{9,8},{10,11... | collective-permute-start | bytes 589832 | tf_op jit(solution)/shard_map/ppermute | solution.py:440
  99.4 13.1 %collective-permute-start.25 = (bf16[1,64,1536]{2,1,0:T(8,128)(2,1)S(1)}, bf16[1,64,1536]{2,1,0:T(8,128)(2,1)S(1)}, u32[]{:S(2)}, u32[]{:S(2)}) collective-permute-start(bf16[1,64,1536]{2,1,0:T(8,128)(2,1)S(1)} %collective-permute-done.24.refs_2_), channel_id=1, source_target_pairs={{0,1},{1,0},{2,3},{3,2},{4,5},{5,4},{6,7},{7,6},{8,9},{9,8},{10,11... | collective-permute-start | bytes 589832 | tf_op jit(solution)/shard_map/ppermute | solution.py:440
  99.9 13.1 %collective-permute-start.28 = (bf16[1,64,1536]{2,1,0:T(8,128)(2,1)S(1)}, bf16[1,64,1536]{2,1,0:T(8,128)(2,1)S(1)}, u32[]{:S(2)}, u32[]{:S(2)}) collective-permute-start(bf16[1,64,1536]{2,1,0:T(8,128)(2,1)S(1)} %bitcast.31), channel_id=1, source_target_pairs={{0,2},{1,3},{2,0},{3,1},{4,6},{5,7},{6,4},{7,5},{8,10},{9,11},{10,... | collective-permute-start | bytes 589832 | tf_op jit(solution)/shard_map/ppermute | solution.py:443
  102.7 10.4 %collective-permute-start.32 = (bf16[1,64,1536]{2,1,0:T(8,128)(2,1)S(1)}, bf16[1,64,1536]{2,1,0:T(8,128)(2,1)S(1)}, u32[]{:S(2)}, u32[]{:S(2)}) collective-permute-start(bf16[1,64,1536]{2,1,0:T(8,128)(2,1)S(1)} %bitcast.33), channel_id=1, source_target_pairs={{0,2},{1,3},{2,0},{3,1},{4,6},{5,7},{6,4},{7,5},{8,10},{9,11},{10,... | collective-permute-start | bytes 589832 | tf_op jit(solution)/shard_map/ppermute | solution.py:443
  (23 other events, 173.8 us)

commit v3 on v2

--- a/solution.py
+++ b/solution.py
@@ -94,7 +94,7 @@
             pltpu.VMEM((count, rank, up_width), down.dtype),
             pltpu.SemaphoreType.DMA((2, count)),
         ],
-        compiler_params=pltpu.CompilerParams(vmem_limit_bytes=24 * 1024 * 1024),
+        compiler_params=pltpu.CompilerParams(vmem_limit_bytes=56 * 1024 * 1024),
     )(numbers, down, up)
 
 
@@ -102,7 +102,8 @@
     x_n, z_n = sizes
     count = x_n * 2 * len(groups)
     block_refs, down_ref, up_ref = refs[:count], refs[count], refs[count + 1]
-    owned, _, down_width = down_ref.shape
+    owned, tile, down_width = down_ref.shape
+    first_row = pl.multiple_of(pl.program_id(0) * tile, tile)
     z, a = numbers[0], numbers[1]
     x, core = a // 2, a % 2
     down_ref[...] = jnp.zeros_like(down_ref)
@@ -120,7 +121,7 @@
 
                     @pl.when(jnp.logical_and(row >= 0, row < owned))
                     def _():
-                        block = block_refs[i][k].astype(jnp.float32)
+                        block = block_refs[i][k, pl.ds(first_row, tile), :].astype(jnp.float32)
                         down_ref[row] += block[:, :down_width]
                         up_ref[row] += block[:, down_width:]
 
@@ -141,7 +142,7 @@
         functools.partial(owner_sum_kernel, sizes, groups),
         grid=(rank // tile,),
         in_specs=[smem]
-        + [pl.BlockSpec((b.shape[0], tile, width), lambda t: (0, t, 0)) for b in blocks],
+        + [pl.BlockSpec(memory_space=pltpu.VMEM)] * len(blocks),
         out_specs=[
             pl.BlockSpec((owned, tile, down_width), lambda t: (0, t, 0)),
             pl.BlockSpec((owned, tile, width - down_width), lambda t: (0, t, 0)),
@@ -337,10 +338,14 @@
     ]
 
 
-def dots_kernel(z_n, shards, totals, place_ref, tokens_ref, pair_ref, *refs):
+def dots_kernel(z_n, shards, totals, packed, place_ref, tokens_ref, pair_ref, *refs):
     count = sum(len(group) for group in shards)
     unit_refs, refs = refs[:count], refs[count:]
-    total_refs, out_refs = refs[: 2 * totals], refs[2 * totals : 2 * totals + 2 * len(shards)]
+    total_refs, out_refs = refs[:totals], refs[totals : totals + 2 * len(shards)]
+    if packed:
+        out_refs = [refs[totals].at[n] for n in range(2 * len(shards))]
+    if totals == 1:
+        total_refs = [total_refs[0].at[n] for n in range(2 * len(shards))]
     buffers, semaphores = refs[-4:-2], refs[-2:]
     depth = unit_refs[0].shape[0]
     only = {d for group in shards for d in group}
@@ -366,20 +371,22 @@
                 part = jnp.dot(left, unit_refs[n][...], preferred_element_type=jnp.float32)
                 value = part if value is None else value + part
                 n += 1
+            at = side * len(shards) + u
             if totals:
-                value = value + total_refs[side * totals + u][...]
-            out_refs[side * len(shards) + u][...] = value
-
-
-def add_dots(z_n, place, tokens, pair, shards, units, totals):
+                value = total_refs[at][...] + (0.0 if value is None else value)
+            out_refs[at][...] = value
+
+
+def add_dots(z_n, place, tokens, pair, shards, units, totals, packed=False):
     rows = tokens.shape[0]
-    depth, width = units[0][0].shape
+    depth, width = next(unit.shape for group in units for unit in group)
     count = len(shards)
     if depth % 128 or width % 128:
         outs = []
         for side, array in enumerate((tokens, pair)):
             for u, group in enumerate(shards):
-                value = totals[side * count + u] if totals else 0.0
+                at = side * count + u
+                value = 0.0 if not totals else totals[0][at] if len(totals) == 1 else totals[at]
                 for d, unit in zip(group, units[u]):
                     at = ((place[0] - d) % z_n) * depth
                     value = value + jnp.dot(
@@ -388,18 +395,20 @@
                         preferred_element_type=jnp.float32,
                     )
                 outs.append(value)
-        return outs
+        return [jnp.stack(outs)] if packed else outs
     hbm = pl.BlockSpec(memory_space=pltpu.HBM)
     vmem = pl.BlockSpec(memory_space=pltpu.VMEM)
     flat = [unit for group in units for unit in group]
     only = {d for group in shards for d in group}
     buffer = pltpu.VMEM((rows, depth if len(only) == 1 else tokens.shape[1]), tokens.dtype)
     outs = pl.pallas_call(
-        functools.partial(dots_kernel, z_n, shards, len(totals) // 2),
+        functools.partial(dots_kernel, z_n, shards, len(totals), packed),
         in_specs=[pl.BlockSpec(memory_space=pltpu.SMEM), hbm, hbm]
         + [vmem] * (len(flat) + len(totals)),
-        out_specs=[vmem] * (2 * count),
-        out_shape=[jax.ShapeDtypeStruct((rows, width), jnp.float32)] * (2 * count),
+        out_specs=[vmem] * (1 if packed else 2 * count),
+        out_shape=[jax.ShapeDtypeStruct((2 * count, rows, width), jnp.float32)]
+        if packed
+        else [jax.ShapeDtypeStruct((rows, width), jnp.float32)] * (2 * count),
         scratch_shapes=[buffer, buffer, pltpu.SemaphoreType.DMA, pltpu.SemaphoreType.DMA],
         compiler_params=pltpu.CompilerParams(vmem_limit_bytes=20 * 1024 * 1024),
     )(place, tokens, pair, *flat, *totals)
@@ -470,7 +479,10 @@
     taken = [over_core(picked[x_n + e]) for e in range(x_n)]
     away = [picked[e] + after(taken[e], tokens_pair, taken[0]) for e in range(1, x_n)]
     slices = picked[0] + taken[0]
-    from_z = {d: over_z(unit if k < 2 else after(unit, *away), d) for k, d in enumerate(shifts)}
+    from_z = {d: over_z(unit, d) for d in shifts[:2]}
+    for d in shifts[2:]:
+        step = 1 if 2 * d <= z_n else z_n - 1
+        from_z[d] = over_z(after(from_z[(d - step) % z_n], *away), step)
     for e in range(1, x_n):
         slices = slices + over_x(away[e - 1], e)
 
@@ -494,12 +506,22 @@
     own_units = [
         unit_at((y - g) % copies_n, (x - e) % x_n) for g in range(copies_n) for e in range(x_n)
     ]
+    totals = add_dots(
+        z_n,
+        after(place, cosine, sine, live_rank),
+        tokens,
+        tokens_pair,
+        [[0]] * units,
+        [[v] for v in own_units],
+        [],
+        packed=True,
+    )
     along_x, along_y, diagonal = [], [], []
     for k, d in enumerate(shifts):
         gate = away[0] if k < 2 else along_y[k - 2][-1]
         along_y.append([over_y(after(from_z[d], gate), g) for g in range(1, copies_n)])
     for k, d in enumerate(shifts):
-        gate = (away[0], along_y[0][-1], slices)[min(k, 2)]
+        gate = (along_y[0][-1], totals[0], along_y[1][-1])[min(k, 2)]
         along_x.append([over_x(after(from_z[d], gate), e) for e in range(1, x_n)])
     for k, d in enumerate(shifts):
         if k < final:
@@ -507,43 +529,49 @@
             diagonal.append(
                 [[over_y(after(v, gate), g) for v in along_x[k]] for g in range(1, copies_n)]
             )
-    adapter_slices = {0: slices[0]}
-    for k, d in enumerate(shifts):
-        gates = (along_x[0][-1],) if k >= 2 else ()
-        adapter_slices[(-d) % z_n] = over_z(after(slices[d], *gates), d)
     diagonal.append(
         [
             [over_x(after(v, along_x[max(final - 1, 0)][-1]), e) for e in range(1, x_n)]
             for v in along_y[final]
         ]
     )
-    shards = {0: own_units}
+    shards = {}
     for k, d in enumerate(shifts):
         shards[d] = [from_z[d]] + along_x[k]
         for g in range(1, copies_n):
             shards[d] += [along_y[k][g - 1]] + diagonal[k][g - 1]
-    order = [0] + shifts
-    groups = [order] * (units - 1) + [order[:-1]]
-    first = add_dots(
-        z_n,
-        after(place, cosine, sine, live_rank, *adapter_slices.values()),
-        tokens,
-        tokens_pair,
-        groups,
-        [[shards[d][u] for d in group] for u, group in enumerate(groups)],
-        [],
-    )
-    last = add_dots(
+    early, late = [], []
+    for u in range(units):
+        g, e = u // x_n, u % x_n
+        early.append([d for d in shifts if not (g and e) and not (e and d == shifts[final])])
+        late.append([d for d in shifts if d not in early[u]])
+    totals = add_dots(
         z_n,
         place,
         tokens,
         tokens_pair,
-        [order[-1:]],
-        [[shards[order[-1]][-1]]],
-        [first[units - 1], first[-1]],
-    )
-    bases = first[: units - 1] + [last[0]]
-    bases += [over_core(v) for v in first[units:-1] + [last[1]]]
+        early,
+        [[shards[d][u] for d in group] for u, group in enumerate(early)],
+        totals,
+    )
+    adapter_slices = {0: slices[0]}
+    for k, d in enumerate(shifts):
+        gates = ()
+        adapter_slices[(-d) % z_n] = over_z(after(slices[d], *gates), d)
+    open_units = [u for u in range(units) if late[u]]
+    done = add_dots(
+        z_n,
+        after(place, *adapter_slices.values()),
+        tokens,
+        tokens_pair,
+        [late[u] for u in open_units],
+        [[shards[d][u] for d in late[u]] for u in open_units],
+        [totals[u] for u in open_units] + [totals[units + u] for u in open_units],
+    )
+    bases = list(totals)
+    for n, u in enumerate(open_units):
+        bases[u], bases[units + u] = done[n], done[len(open_units) + n]
+    bases = bases[:units] + [over_core(v) for v in bases[units:]]
     head = key_norm_gain.shape[0]
     columns = [
         (((y - g) % copies_n) * x_n + (x - e) % x_n) * unit_width

time: 125 us -> 117 us (0.936); the launches traced: 123 us -> 117 us
  starting transfers between devices: 46.1 us -> 33.2 us
  waiting for transfers between devices: 35.8 us -> 43.3 us
  local copies, waits for them, and re-layouts: 7.32 us -> 5.39 us
    ppermute x9, starting transfers between devices: 25.9 us -> 15.3 us  [over_z(): return lax.ppermute(v, 'fsdp', [(i, (i + d) % z_n) for i in range(z_n)])]
    ppermute x9, waiting for transfers between devices: 5.87 us -> 13.9 us  [over_x(): lax.ppermute(v, 'adapter', [(i, (i // 2 + e) % x_n * 2 + i % 2) for i in...]
    unnamed x18 -> x20, local copies, waits for them, and re-layouts: 3.46 us -> 1.53 us
    ppermute x9, starting transfers between devices: 10.2 us -> 8.56 us  [over_x(): lax.ppermute(v, 'adapter', [(i, (i // 2 + e) % x_n * 2 + i % 2) for i in...]
    ppermute x9, waiting for transfers between devices: 26.1 us -> 24.7 us  [over_z(): return lax.ppermute(v, 'fsdp', [(i, (i + d) % z_n) for i in range(z_n)])]
    pallas_call x2 -> x3, Pallas kernels: 8.61 us -> 9.49 us  [add_dots(): pl.pallas_call(functools.partial(dots_kernel, z_n, shards, len(totals), p...]
  transfers between devices with their start and end apart: 38 -> 38, of which waited for: 11 -> 11; matrix products, arithmetic and copies ran while one was open for 10% -> 11% of each run, Pallas kernels for 13% -> 14%
where the time goes in v3:
time: 117 us
  waiting for transfers between devices  43.3 us (37%)
  starting transfers between devices  33.2 us (28%)
  Pallas kernels  25 us (21%)
  other arithmetic  9.25 us (8%)
  local copies, waits for them, and re-layouts  5.39 us (5%)
    ppermute x9, waiting for transfers between devices, over_z(): return lax.ppermute(v, 'fsdp', [(i, (i + d) % z_n) for i in range(z_n)])  24.7 us
    ppermute x9, starting transfers between devices, over_z(): return lax.ppermute(v, 'fsdp', [(i, (i + d) % z_n) for i in range(z_n)])  15.3 us
    ppermute x9, waiting for transfers between devices, over_x(): lax.ppermute(v, 'adapter', [(i, (i // 2 + e) % x_n * 2 + i % 2) for i in...  13.9 us
    pallas_call x3, Pallas kernels, add_dots(): pl.pallas_call(functools.partial(dots_kernel, z_n, shards, len(totals), p...  9.49 us
    ppermute x9, starting transfers between devices, over_x(): lax.ppermute(v, 'adapter', [(i, (i // 2 + e) % x_n * 2 + i % 2) for i in...  8.56 us
    ppermute x5, starting transfers between devices, over_y(): lax.ppermute(v, 'copies', [(i, (i + g) % copies_n) for i in range(copies_...  5.63 us
    pallas_call x1, Pallas kernels, norm_and_back(): pl.pallas_call(functools.partial(norm_kernel, z_n, len(bases) // 2), in_s...  4.76 us
    pallas_call x1, Pallas kernels, pick_rows(): pl.pallas_call(functools.partial(pick_kernel, sizes), in_specs=[pl.BlockS...  4.52 us
  transfers between devices with their start and end apart: 38, of which 11 were waited for; matrix products, arithmetic and copies ran while one was open for 11% of the time, Pallas kernels for 14%

profile of v3, /device:TPU:0, one launch (start us, length us, event | category | flops | bytes accessed | tf_op | source)
XLA Modules:
  0.0 117.0 jit_solution(7094296429626531595)
XLA Ops:
  2.4 4.5 %shard_map.121 = (bf16[4,64,1536]{2,1,0:T(8,128)(2,1)}, bf16[4,64,1536]{2,1,0:T(8,128)(2,1)}, bf16[4,64,1536]{2,1,0:T(8,128)(2,1)}, bf16[4,64,1536]{2,1,0:T(8,128)(2,1)}) custom-call(s32[66]{0:T(128)} %pad_add_fusion.2.numbers, bf16[12,64,1280]{2,1,0:T(8,128)(2,1)} %down_ref.1, bf16[12,64,256]{2,1,0:T(8,128)(2,1)} %up_ref.1), custom_call_target="tpu_custom_call" | custom-call | tf_op jit(solution)/shard_map/pallas_call | solution.py:85
  7.5 1.7 %constant_dynamic-slice_fusion.4 = bf16[1280,128]{1,0:T(8,128)(2,1)} fusion(bf16[1280,1024]{1,0:T(8,128)(2,1)} %param.11, s32[]{:T(128)S(6)} %select_n.92), kind=kLoop, calls=%fused_computation.18 | loop fusion | bytes 655364 | tf_op jit(solution)/shard_map/dynamic_slice | solution.py:468
  9.3 2.7 %collective-permute-start.3 = (bf16[1280,128]{1,0:T(8,128)(2,1)}, bf16[1280,128]{1,0:T(8,128)(2,1)S(1)}, u32[]{:S(2)}, u32[]{:S(2)}) collective-permute-start(bf16[1280,128]{1,0:T(8,128)(2,1)} %constant_dynamic-slice_fusion.4), channel_id=1, source_target_pairs={{0,4},{4,8},{8,12},{12,0},{1,5},{5,9},{9,13},{13,1},{2,6},{6,10},{... | collective-permute-start | bytes 983048 | tf_op jit(solution)/shard_map/ppermute | solution.py:460
  12.0 2.0 %collective-permute-start.4 = (bf16[1280,128]{1,0:T(8,128)(2,1)}, bf16[1280,128]{1,0:T(8,128)(2,1)S(1)}, u32[]{:S(2)}, u32[]{:S(2)}) collective-permute-start(bf16[1280,128]{1,0:T(8,128)(2,1)} %constant_dynamic-slice_fusion.4), channel_id=1, source_target_pairs={{0,12},{4,0},{8,4},{12,8},{1,13},{5,1},{9,5},{13,9},{2,14},{6,2},{... | collective-permute-start | bytes 983048 | tf_op jit(solution)/shard_map/ppermute | solution.py:460
  15.6 2.6 %add.107 = bf16[4,64,1536]{2,1,0:T(8,128)(2,1)} add(bf16[4,64,1536]{2,1,0:T(8,128)(2,1)} %get-tuple-element.46, bf16[4,64,1536]{2,1,0:T(8,128)(2,1)} %collective-permute-done) | non-fusion elementwise | flops 393216 | bytes 2359296 | tf_op jit(solution)/shard_map/add | solution.py:480
  18.2 4.6 %collective-permute-done.3.refs_0_ = bf16[1280,128]{1,0:T(8,128)(2,1)S(1)} collective-permute-done((bf16[1280,128]{1,0:T(8,128)(2,1)}, bf16[1280,128]{1,0:T(8,128)(2,1)S(1)}, u32[]{:S(2)}, u32[]{:S(2)}) %collective-permute-start.3) | collective-permute-done | bytes 327712 | tf_op jit(solution)/shard_map/ppermute | solution.py:460
  25.9 3.2 %collective-permute-done.4.refs_1_ = bf16[1280,128]{1,0:T(8,128)(2,1)S(1)} collective-permute-done((bf16[1280,128]{1,0:T(8,128)(2,1)}, bf16[1280,128]{1,0:T(8,128)(2,1)S(1)}, u32[]{:S(2)}, u32[]{:S(2)}) %collective-permute-start.4) | collective-permute-done | bytes 327712 | tf_op jit(solution)/shard_map/ppermute | solution.py:460
  36.3 2.4 %shard_map.122.refs_8_ = f32[8,256,128]{2,1,0:T(8,128)S(1)} custom-call(s32[2]{0:T(128)S(1)} %pad_add_fusion.place_ref, bf16[256,5120]{1,0:T(8,128)(2,1)S(1)} %copy-done, bf16[256,5120]{1,0:T(8,128)(2,1)S(1)} %copy-done.2, bf16[1280,128]{1,0:T(8,128)(2,1)S(1)} %get-tuple-element.92.refs_0_, bf16[1280,128]{1,0:T(8,128)(2,1)S(1)} %get-tuple-element.91.refs_1_, ...), custom_call_target="tpu_custom_call" | custom-call | tf_op jit(solution)/shard_map/pallas_call | solution.py:404
  41.4 3.8 %collective-permute-done.11 = bf16[4,64,1536]{2,1,0:T(8,128)(2,1)} collective-permute-done((bf16[4,64,1536]{2,1,0:T(8,128)(2,1)}, bf16[4,64,1536]{2,1,0:T(8,128)(2,1)}, u32[]{:S(2)}, u32[]{:S(2)}) %collective-permute-start.11) | collective-permute-done | bytes 786464 | tf_op jit(solution)/shard_map/ppermute | solution.py:452
  46.8 5.4 %collective-permute-start.13 = (bf16[64,1536]{1,0:T(8,128)(2,1)S(1)}, bf16[64,1536]{1,0:T(8,128)(2,1)S(1)}, u32[]{:S(2)}, u32[]{:S(2)}) collective-permute-start(bf16[64,1536]{1,0:T(8,128)(2,1)S(1)} %get-tuple-element.94), channel_id=1, source_target_pairs={{0,12},{4,0},{8,4},{12,8},{1,13},{5,1},{9,5},{13,9},{2,14},{6,2},{... | collective-permute-start | bytes 589832 | tf_op jit(solution)/shard_map/ppermute | solution.py:460
  52.2 5.0 %collective-permute-done.7.refs_3_ = bf16[1280,128]{1,0:T(8,128)(2,1)S(1)} collective-permute-done((bf16[1280,128]{1,0:T(8,128)(2,1)S(1)}, bf16[1280,128]{1,0:T(8,128)(2,1)S(1)}, u32[]{:S(2)}, u32[]{:S(2)}) %collective-permute-start.7) | collective-permute-done | bytes 327712 | tf_op jit(solution)/shard_map/ppermute | solution.py:452
  62.3 4.5 %shard_map.123 = (f32[256,128]{1,0:T(8,128)S(1)}, f32[256,128]{1,0:T(8,128)S(1)}, f32[256,128]{1,0:T(8,128)S(1)}, f32[256,128]{1,0:T(8,128)S(1)}, f32[256,128]{1...) custom-call(s32[2]{0:T(128)S(1)} %pad_add_fusion.place_ref, ...), custom_call_target="tpu_custom_call" | custom-call | tf_op jit(solution)/shard_map/pallas_call | solution.py:404
  66.9 2.4 %collective-permute-done.12.refs_3_ = bf16[64,1536]{1,0:T(8,128)(2,1)S(1)} collective-permute-done((bf16[64,1536]{1,0:T(8,128)(2,1)S(1)}, bf16[64,1536]{1,0:T(8,128)(2,1)S(1)}, u32[]{:S(2)}, u32[]{:S(2)}) %collective-permute-start.12) | collective-permute-done | bytes 196640 | tf_op jit(solution)/shard_map/ppermute | solution.py:460
  69.7 3.2 %collective-permute-done.17.refs_2_ = bf16[1280,128]{1,0:T(8,128)(2,1)S(1)} collective-permute-done((bf16[1280,128]{1,0:T(8,128)(2,1)S(1)}, bf16[1280,128]{1,0:T(8,128)(2,1)S(1)}, u32[]{:S(2)}, u32[]{:S(2)}) %collective-permute-start.17) | collective-permute-done | bytes 327712 | tf_op jit(solution)/shard_map/ppermute | solution.py:457
  72.9 2.6 %shard_map.124 = (f32[256,128]{1,0:T(8,128)S(1)}, f32[256,128]{1,0:T(8,128)S(1)}, f32[256,128]{1,0:T(8,128)S(1)}, f32[256,128]{1,0:T(8,128)S(1)}) custom-call(s32[2]{0:T(128)S(1)} %pad_add_fusion.place_ref, bf16[256,5120]{1,0:T(8,128)(2,1)S(1)} %copy-done, bf16[256,5120]{1,0:T(8,128)(2,1)S(1)} %copy-done.2, ...), custom_call_target="tpu_custom_call" | custom-call | tf_op jit(solution)/shard_map/pallas_call | solution.py:404
  76.2 2.6 %shard_map.125 = (bf16[256,64]{1,0:T(8,128)(2,1)S(1)}, bf16[64,1024]{1,0:T(8,128)(2,1)S(1)}, f32[256,1024]{1,0:T(8,128)S(1)}) custom-call(s32[2]{0:T(128)S(1)} %pad_add_fusion.place_ref, s32[1,1]{1,0:T(1,128)} %bitcast.6.rank_ref, bf16[256,5120]{1,0:T(8,128)(2,1)S(1)} %copy-done, bf16[64,1536]{1,0:T(8,128)(2,1)S(1)} %get-tuple-element.96.refs_0_, ...), custom_call_target="tpu_custom_call" | custom-call | tf_op jit(solution)/shard_map/pallas_call | solution.py:200
  78.9 4.8 %shard_map.126 = (bf16[256,1024]{1,0:T(8,128)(2,1)}, bf16[64,1536]{1,0:T(8,128)(2,1)S(1)}, bf16[64,1536]{1,0:T(8,128)(2,1)S(1)}, bf16[64,1536]{1,0:T(8,128)(2,1)S(1)}, bf16[64,1536]{1,0:T(8,128)(2,1)S(1)}) custom-call(s32[2]{0:T(128)S(1)} %pad_add_fusion.place_ref, s32[4]{0:T(128)S(1)} %pad_add_fusion.1.columns_ref, s32[1,1]{1,0:T(1,128)} %bitcast.6.rank_ref, ...), custom_call_target="tpu_custom_call" | custom-call | tf_op jit(solution)/shard_map/pallas_call | solution.py:310
  83.7 1.7 %collective-permute-start.26 = (bf16[64,1536]{1,0:T(8,128)(2,1)S(1)}, bf16[64,1536]{1,0:T(8,128)(2,1)S(1)}, u32[]{:S(2)}, u32[]{:S(2)}) collective-permute-start(bf16[64,1536]{1,0:T(8,128)(2,1)S(1)} %get-tuple-element.84), channel_id=1, source_target_pairs={{0,4},{4,8},{8,12},{12,0},{1,5},{5,9},{9,13},{13,1},{2,6},{6,10},{... | collective-permute-start | bytes 589832 | tf_op jit(solution)/shard_map/ppermute | solution.py:460
  86.0 2.4 %collective-permute-start.30 = (bf16[64,1536]{1,0:T(8,128)(2,1)S(1)}, bf16[64,1536]{1,0:T(8,128)(2,1)S(1)}, u32[]{:S(2)}, u32[]{:S(2)}) collective-permute-start(bf16[64,1536]{1,0:T(8,128)(2,1)S(1)} %get-tuple-element.85), channel_id=1, source_target_pairs={{0,12},{4,0},{8,4},{12,8},{1,13},{5,1},{9,5},{13,9},{2,14},{6,2},{... | collective-permute-start | bytes 589832 | tf_op jit(solution)/shard_map/ppermute | solution.py:460
  88.3 5.0 %collective-permute-done.26 = bf16[64,1536]{1,0:T(8,128)(2,1)S(1)} collective-permute-done((bf16[64,1536]{1,0:T(8,128)(2,1)S(1)}, bf16[64,1536]{1,0:T(8,128)(2,1)S(1)}, u32[]{:S(2)}, u32[]{:S(2)}) %collective-permute-start.26) | collective-permute-done | bytes 196640 | tf_op jit(solution)/shard_map/ppermute | solution.py:460
  94.6 2.0 %collective-permute-done.30 = bf16[64,1536]{1,0:T(8,128)(2,1)S(1)} collective-permute-done((bf16[64,1536]{1,0:T(8,128)(2,1)S(1)}, bf16[64,1536]{1,0:T(8,128)(2,1)S(1)}, u32[]{:S(2)}, u32[]{:S(2)}) %collective-permute-start.30) | collective-permute-done | bytes 196640 | tf_op jit(solution)/shard_map/ppermute | solution.py:460
  97.5 7.6 %collective-permute-done.34 = bf16[64,1536]{1,0:T(8,128)(2,1)S(1)} collective-permute-done((bf16[64,1536]{1,0:T(8,128)(2,1)S(1)}, bf16[64,1536]{1,0:T(8,128)(2,1)S(1)}, u32[]{:S(2)}, u32[]{:S(2)}) %collective-permute-start.34) | collective-permute-done | bytes 196640 | tf_op jit(solution)/shard_map/ppermute | solution.py:460
  106.9 5.1 %collective-permute-done.36.refs_14_ = bf16[1,64,1536]{2,1,0:T(8,128)(2,1)S(1)} collective-permute-done((bf16[1,64,1536]{2,1,0:T(8,128)(2,1)S(1)}, bf16[1,64,1536]{2,1,0:T(8,128)(2,1)S(1)}, u32[]{:S(2)}, u32[]{:S(2)}) %collective-permute-start.36) | collective-permute-done | bytes 196640 | tf_op jit(solution)/shard_map/ppermute | solution.py:452
  113.4 3.6 %shard_map.127 = (f32[12,64,1280]{2,1,0:T(8,128)}, f32[12,64,256]{2,1,0:T(8,128)}) custom-call(s32[66]{0:T(128)S(1)} %copy-done.4, bf16[1,64,1536]{2,1,0:T(8,128)(2,1)S(1)} %bitcast.29, bf16[1,64,1536]{2,1,0:T(8,128)(2,1)S(1)} %collective-permute-done.23.refs_1_, bf16[1,64,1536]{2,1,0:T(8,128)(2,1)S(1)} %collective-permute-done.24.refs_2_, ...), custom_call_target="tpu_custom_call" | custom-call | tf_op jit(solution)/shard_map/pallas_call | solution.py:141
  (99 shorter events, 30.7 us)
Async XLA Ops:
  0.6 13.5 %collective-permute-start.1 = (bf16[256,5120]{1,0:T(8,128)(2,1)}, bf16[256,5120]{1,0:T(8,128)(2,1)S(1)}, u32[]{:S(2)}, u32[]{:S(2)}) collective-permute-start(bf16[256,5120]{1,0:T(8,128)(2,1)} %refs_15_.1), channel_id=1, source_target_pairs={{0,1},{1,0},{2,3},{3,2},{4,5},{5,4},{6,7},{7,6},{8,9},{9,8},{10,11... | collective-permute-start | bytes 7864328 | tf_op jit(solution)/shard_map/ppermute | solution.py:449
  9.3 13.6 %collective-permute-start.3 = (bf16[1280,128]{1,0:T(8,128)(2,1)}, bf16[1280,128]{1,0:T(8,128)(2,1)S(1)}, u32[]{:S(2)}, u32[]{:S(2)}) collective-permute-start(bf16[1280,128]{1,0:T(8,128)(2,1)} %constant_dynamic-slice_fusion.4), channel_id=1, source_target_pairs={{0,4},{4,8},{8,12},{12,0},{1,5},{5,9},{9,13},{13,1},{2,6},{6,10},{... | collective-permute-start | bytes 983048 | tf_op jit(solution)/shard_map/ppermute | solution.py:460
  12.0 17.0 %collective-permute-start.4 = (bf16[1280,128]{1,0:T(8,128)(2,1)}, bf16[1280,128]{1,0:T(8,128)(2,1)S(1)}, u32[]{:S(2)}, u32[]{:S(2)}) collective-permute-start(bf16[1280,128]{1,0:T(8,128)(2,1)} %constant_dynamic-slice_fusion.4), channel_id=1, source_target_pairs={{0,12},{4,0},{8,4},{12,8},{1,13},{5,1},{9,5},{13,9},{2,14},{6,2},{... | collective-permute-start | bytes 983048 | tf_op jit(solution)/shard_map/ppermute | solution.py:460
  22.8 17.3 %collective-permute-start.6 = (bf16[1280,128]{1,0:T(8,128)(2,1)S(1)}, bf16[1280,128]{1,0:T(8,128)(2,1)}, u32[]{:S(2)}, u32[]{:S(2)}) collective-permute-start(bf16[1280,128]{1,0:T(8,128)(2,1)S(1)} %collective-permute-done.3.refs_0_), channel_id=1, source_target_pairs={{0,16},{16,0},{1,17},{17,1},{2,18},{18,2},{3,19},{19,3},{4,20},{20... | collective-permute-start | bytes 983048 | tf_op jit(solution)/shard_map/ppermute | solution.py:457
  24.4 16.4 %collective-permute-start.5 = (bf16[1280,128]{1,0:T(8,128)(2,1)S(1)}, bf16[1280,128]{1,0:T(8,128)(2,1)}, u32[]{:S(2)}, u32[]{:S(2)}) collective-permute-start(bf16[1280,128]{1,0:T(8,128)(2,1)S(1)} %collective-permute-done.3.refs_0_), channel_id=1, source_target_pairs={{0,4},{4,8},{8,12},{12,0},{1,5},{5,9},{9,13},{13,1},{2,6},{6,10},{... | collective-permute-start | bytes 983048 | tf_op jit(solution)/shard_map/ppermute | solution.py:460
  24.4 20.8 %collective-permute-start.11 = (bf16[4,64,1536]{2,1,0:T(8,128)(2,1)}, bf16[4,64,1536]{2,1,0:T(8,128)(2,1)}, u32[]{:S(2)}, u32[]{:S(2)}) collective-permute-start(bf16[4,64,1536]{2,1,0:T(8,128)(2,1)} %add.107), channel_id=1, source_target_pairs={{0,2},{1,3},{2,0},{3,1},{4,6},{5,7},{6,4},{7,5},{8,10},{9,11},{10,... | collective-permute-start | bytes 2359304 | tf_op jit(solution)/shard_map/ppermute | solution.py:452
  30.9 21.3 %collective-permute-start.9 = (bf16[1280,128]{1,0:T(8,128)(2,1)S(1)}, bf16[1280,128]{1,0:T(8,128)(2,1)S(1)}, u32[]{:S(2)}, u32[]{:S(2)}) collective-permute-start(bf16[1280,128]{1,0:T(8,128)(2,1)S(1)} %collective-permute-done.4.refs_1_), channel_id=1, source_target_pairs={{0,16},{16,0},{1,17},{17,1},{2,18},{18,2},{3,19},{19,3},{4,20},{20... | collective-permute-start | bytes 983048 | tf_op jit(solution)/shard_map/ppermute | solution.py:457
  38.7 19.8 %collective-permute-start.8 = (bf16[1280,128]{1,0:T(8,128)(2,1)S(1)}, bf16[1280,128]{1,0:T(8,128)(2,1)S(1)}, u32[]{:S(2)}, u32[]{:S(2)}) collective-permute-start(bf16[1280,128]{1,0:T(8,128)(2,1)S(1)} %collective-permute-done.4.refs_1_), channel_id=1, source_target_pairs={{0,2},{1,3},{2,0},{3,1},{4,6},{5,7},{6,4},{7,5},{8,10},{9,11},{10,... | collective-permute-start | bytes 983048 | tf_op jit(solution)/shard_map/ppermute | solution.py:452
  40.1 17.1 %collective-permute-start.7 = (bf16[1280,128]{1,0:T(8,128)(2,1)S(1)}, bf16[1280,128]{1,0:T(8,128)(2,1)S(1)}, u32[]{:S(2)}, u32[]{:S(2)}) collective-permute-start(bf16[1280,128]{1,0:T(8,128)(2,1)S(1)} %collective-permute-done.3.refs_0_), channel_id=1, source_target_pairs={{0,2},{1,3},{2,0},{3,1},{4,6},{5,7},{6,4},{7,5},{8,10},{9,11},{10,... | collective-permute-start | bytes 983048 | tf_op jit(solution)/shard_map/ppermute | solution.py:452
  40.8 18.3 %collective-permute-start.10 = (bf16[1280,128]{1,0:T(8,128)(2,1)}, bf16[1280,128]{1,0:T(8,128)(2,1)S(1)}, u32[]{:S(2)}, u32[]{:S(2)}) collective-permute-start(bf16[1280,128]{1,0:T(8,128)(2,1)} %collective-permute-done.5.refs_2_), channel_id=1, source_target_pairs={{0,16},{16,0},{1,17},{17,1},{2,18},{18,2},{3,19},{19,3},{4,20},{20... | collective-permute-start | bytes 983048 | tf_op jit(solution)/shard_map/ppermute | solution.py:457
  46.8 13.8 %collective-permute-start.13 = (bf16[64,1536]{1,0:T(8,128)(2,1)S(1)}, bf16[64,1536]{1,0:T(8,128)(2,1)S(1)}, u32[]{:S(2)}, u32[]{:S(2)}) collective-permute-start(bf16[64,1536]{1,0:T(8,128)(2,1)S(1)} %get-tuple-element.94), channel_id=1, source_target_pairs={{0,12},{4,0},{8,4},{12,8},{1,13},{5,1},{9,5},{13,9},{2,14},{6,2},{... | collective-permute-start | bytes 589832 | tf_op jit(solution)/shard_map/ppermute | solution.py:460
  57.2 12.0 %collective-permute-start.15 = (bf16[1280,128]{1,0:T(8,128)(2,1)}, bf16[1280,128]{1,0:T(8,128)(2,1)S(1)}, u32[]{:S(2)}, u32[]{:S(2)}) collective-permute-start(bf16[1280,128]{1,0:T(8,128)(2,1)} %collective-permute-done.5.refs_2_), channel_id=1, source_target_pairs={{0,2},{1,3},{2,0},{3,1},{4,6},{5,7},{6,4},{7,5},{8,10},{9,11},{10,... | collective-permute-start | bytes 983048 | tf_op jit(solution)/shard_map/ppermute | solution.py:452
  58.5 11.2 %collective-permute-start.16 = (bf16[1280,128]{1,0:T(8,128)(2,1)S(1)}, bf16[1280,128]{1,0:T(8,128)(2,1)S(1)}, u32[]{:S(2)}, u32[]{:S(2)}) collective-permute-start(bf16[1280,128]{1,0:T(8,128)(2,1)S(1)} %collective-permute-done.7.refs_3_), channel_id=1, source_target_pairs={{0,16},{16,0},{1,17},{17,1},{2,18},{18,2},{3,19},{19,3},{4,20},{20... | collective-permute-start | bytes 983048 | tf_op jit(solution)/shard_map/ppermute | solution.py:457
  59.0 13.9 %collective-permute-start.17 = (bf16[1280,128]{1,0:T(8,128)(2,1)S(1)}, bf16[1280,128]{1,0:T(8,128)(2,1)S(1)}, u32[]{:S(2)}, u32[]{:S(2)}) collective-permute-start(bf16[1280,128]{1,0:T(8,128)(2,1)S(1)} %collective-permute-done.8.refs_4_), channel_id=1, source_target_pairs={{0,16},{16,0},{1,17},{17,1},{2,18},{18,2},{3,19},{19,3},{4,20},{20... | collective-permute-start | bytes 983048 | tf_op jit(solution)/shard_map/ppermute | solution.py:457
  60.6 12.4 %collective-permute-start.18 = (bf16[1280,128]{1,0:T(8,128)(2,1)S(1)}, bf16[1280,128]{1,0:T(8,128)(2,1)S(1)}, u32[]{:S(2)}, u32[]{:S(2)}) collective-permute-start(bf16[1280,128]{1,0:T(8,128)(2,1)S(1)} %collective-permute-done.10.refs_7_), channel_id=1, source_target_pairs={{0,2},{1,3},{2,0},{3,1},{4,6},{5,7},{6,4},{7,5},{8,10},{9,11},{10,... | collective-permute-start | bytes 983048 | tf_op jit(solution)/shard_map/ppermute | solution.py:452
  69.2 9.6 %collective-permute-start.19 = (f32[256,128]{1,0:T(8,128)S(1)}, f32[256,128]{1,0:T(8,128)S(1)}, u32[]{:S(2)}, u32[]{:S(2)}) collective-permute-start(f32[256,128]{1,0:T(8,128)S(1)} %get-tuple-element.74), channel_id=1, source_target_pairs={{0,1},{1,0},{2,3},{3,2},{4,5},{5,4},{6,7},{7,6},{8,9},{9,8},{10,11... | collective-permute-start | bytes 393224 | tf_op jit(solution)/shard_map/ppermute | solution.py:449
  69.2 9.6 %collective-permute-start.21 = (f32[256,128]{1,0:T(8,128)S(1)}, f32[256,128]{1,0:T(8,128)S(1)}, u32[]{:S(2)}, u32[]{:S(2)}) collective-permute-start(f32[256,128]{1,0:T(8,128)S(1)} %get-tuple-element.76), channel_id=1, source_target_pairs={{0,1},{1,0},{2,3},{3,2},{4,5},{5,4},{6,7},{7,6},{8,9},{9,8},{10,11... | collective-permute-start | bytes 393224 | tf_op jit(solution)/shard_map/ppermute | solution.py:449
  83.7 9.7 %collective-permute-start.26 = (bf16[64,1536]{1,0:T(8,128)(2,1)S(1)}, bf16[64,1536]{1,0:T(8,128)(2,1)S(1)}, u32[]{:S(2)}, u32[]{:S(2)}) collective-permute-start(bf16[64,1536]{1,0:T(8,128)(2,1)S(1)} %get-tuple-element.84), channel_id=1, source_target_pairs={{0,4},{4,8},{8,12},{12,0},{1,5},{5,9},{9,13},{13,1},{2,6},{6,10},{... | collective-permute-start | bytes 589832 | tf_op jit(solution)/shard_map/ppermute | solution.py:460
  86.0 10.6 %collective-permute-start.30 = (bf16[64,1536]{1,0:T(8,128)(2,1)S(1)}, bf16[64,1536]{1,0:T(8,128)(2,1)S(1)}, u32[]{:S(2)}, u32[]{:S(2)}) collective-permute-start(bf16[64,1536]{1,0:T(8,128)(2,1)S(1)} %get-tuple-element.85), channel_id=1, source_target_pairs={{0,12},{4,0},{8,4},{12,8},{1,13},{5,1},{9,5},{13,9},{2,14},{6,2},{... | collective-permute-start | bytes 589832 | tf_op jit(solution)/shard_map/ppermute | solution.py:460
  88.3 16.7 %collective-permute-start.34 = (bf16[64,1536]{1,0:T(8,128)(2,1)S(1)}, bf16[64,1536]{1,0:T(8,128)(2,1)S(1)}, u32[]{:S(2)}, u32[]{:S(2)}) collective-permute-start(bf16[64,1536]{1,0:T(8,128)(2,1)S(1)} %get-tuple-element.86), channel_id=1, source_target_pairs={{0,8},{4,12},{8,0},{12,4},{1,9},{5,13},{9,1},{13,5},{2,10},{6,14},... | collective-permute-start | bytes 589832 | tf_op jit(solution)/shard_map/ppermute | solution.py:460
  93.3 12.5 %collective-permute-start.28 = (bf16[1,64,1536]{2,1,0:T(8,128)(2,1)S(1)}, bf16[1,64,1536]{2,1,0:T(8,128)(2,1)S(1)}, u32[]{:S(2)}, u32[]{:S(2)}) collective-permute-start(bf16[1,64,1536]{2,1,0:T(8,128)(2,1)S(1)} %bitcast.30), channel_id=1, source_target_pairs={{0,2},{1,3},{2,0},{3,1},{4,6},{5,7},{6,4},{7,5},{8,10},{9,11},{10,... | collective-permute-start | bytes 589832 | tf_op jit(solution)/shard_map/ppermute | solution.py:452
  94.1 11.7 %collective-permute-start.25 = (bf16[1,64,1536]{2,1,0:T(8,128)(2,1)S(1)}, bf16[1,64,1536]{2,1,0:T(8,128)(2,1)S(1)}, u32[]{:S(2)}, u32[]{:S(2)}) collective-permute-start(bf16[1,64,1536]{2,1,0:T(8,128)(2,1)S(1)} %collective-permute-done.24.refs_2_), channel_id=1, source_target_pairs={{0,1},{1,0},{2,3},{3,2},{4,5},{5,4},{6,7},{7,6},{8,9},{9,8},{10,11... | collective-permute-start | bytes 589832 | tf_op jit(solution)/shard_map/ppermute | solution.py:449
  94.1 12.2 %collective-permute-start.27 = (bf16[1,64,1536]{2,1,0:T(8,128)(2,1)S(1)}, bf16[1,64,1536]{2,1,0:T(8,128)(2,1)S(1)}, u32[]{:S(2)}, u32[]{:S(2)}) collective-permute-start(bf16[1,64,1536]{2,1,0:T(8,128)(2,1)S(1)} %bitcast.31), channel_id=1, source_target_pairs={{0,1},{1,0},{2,3},{3,2},{4,5},{5,4},{6,7},{7,6},{8,9},{9,8},{10,11... | collective-permute-start | bytes 589832 | tf_op jit(solution)/shard_map/ppermute | solution.py:449
  96.6 9.8 %collective-permute-start.32 = (bf16[1,64,1536]{2,1,0:T(8,128)(2,1)S(1)}, bf16[1,64,1536]{2,1,0:T(8,128)(2,1)S(1)}, u32[]{:S(2)}, u32[]{:S(2)}) collective-permute-start(bf16[1,64,1536]{2,1,0:T(8,128)(2,1)S(1)} %bitcast.33), channel_id=1, source_target_pairs={{0,2},{1,3},{2,0},{3,1},{4,6},{5,7},{6,4},{7,5},{8,10},{9,11},{10,... | collective-permute-start | bytes 589832 | tf_op jit(solution)/shard_map/ppermute | solution.py:452
  (24 other events, 247.1 us)

commit v4 on v3

--- a/solution.py
+++ b/solution.py
@@ -136,7 +136,7 @@
 
 def owner_sum(sizes, groups, numbers, blocks, owned, down_width):
     _, rank, width = blocks[0].shape
-    tile = 16
+    tile = 32
     smem = pl.BlockSpec(memory_space=pltpu.SMEM)
     return pl.pallas_call(
         functools.partial(owner_sum_kernel, sizes, groups),
@@ -151,7 +151,7 @@
             jax.ShapeDtypeStruct((owned, rank, down_width), jnp.float32),
             jax.ShapeDtypeStruct((owned, rank, width - down_width), jnp.float32),
         ],
-        compiler_params=pltpu.CompilerParams(vmem_limit_bytes=12 * 1024 * 1024),
+        compiler_params=pltpu.CompilerParams(vmem_limit_bytes=24 * 1024 * 1024),
     )(numbers, *blocks)
 
 
@@ -346,28 +346,14 @@
         out_refs = [refs[totals].at[n] for n in range(2 * len(shards))]
     if totals == 1:
         total_refs = [total_refs[0].at[n] for n in range(2 * len(shards))]
-    buffers, semaphores = refs[-4:-2], refs[-2:]
     depth = unit_refs[0].shape[0]
-    only = {d for group in shards for d in group}
-    fetches = []
     for side, ref in enumerate((tokens_ref, pair_ref)):
-        if len(only) == 1:
-            at = pl.multiple_of(((place_ref[0] - min(only) + z_n) % z_n) * depth, 128)
-            ref = ref.at[:, pl.ds(at, depth)]
-        fetches.append(pltpu.make_async_copy(ref, buffers[side], semaphores[side]))
-        fetches[side].start()
-    for side in range(2):
-        fetches[side].wait()
         n = 0
         for u, group in enumerate(shards):
             value = None
             for d in group:
                 at = pl.multiple_of(((place_ref[0] - d + z_n) % z_n) * depth, 128)
-                left = (
-                    buffers[side][...]
-                    if len(only) == 1
-                    else buffers[side][:, pl.ds(at, depth)]
-                )
+                left = ref[:, pl.ds(at, depth)]
                 part = jnp.dot(left, unit_refs[n][...], preferred_element_type=jnp.float32)
                 value = part if value is None else value + part
                 n += 1
@@ -396,20 +382,15 @@
                     )
                 outs.append(value)
         return [jnp.stack(outs)] if packed else outs
-    hbm = pl.BlockSpec(memory_space=pltpu.HBM)
     vmem = pl.BlockSpec(memory_space=pltpu.VMEM)
     flat = [unit for group in units for unit in group]
-    only = {d for group in shards for d in group}
-    buffer = pltpu.VMEM((rows, depth if len(only) == 1 else tokens.shape[1]), tokens.dtype)
     outs = pl.pallas_call(
         functools.partial(dots_kernel, z_n, shards, len(totals), packed),
-        in_specs=[pl.BlockSpec(memory_space=pltpu.SMEM), hbm, hbm]
-        + [vmem] * (len(flat) + len(totals)),
+        in_specs=[pl.BlockSpec(memory_space=pltpu.SMEM)] + [vmem] * (2 + len(flat) + len(totals)),
         out_specs=[vmem] * (1 if packed else 2 * count),
         out_shape=[jax.ShapeDtypeStruct((2 * count, rows, width), jnp.float32)]
         if packed
         else [jax.ShapeDtypeStruct((rows, width), jnp.float32)] * (2 * count),
-        scratch_shapes=[buffer, buffer, pltpu.SemaphoreType.DMA, pltpu.SemaphoreType.DMA],
         compiler_params=pltpu.CompilerParams(vmem_limit_bytes=20 * 1024 * 1024),
     )(place, tokens, pair, *flat, *totals)
     return list(outs)
@@ -558,10 +539,17 @@
     for k, d in enumerate(shifts):
         gates = ()
         adapter_slices[(-d) % z_n] = over_z(after(slices[d], *gates), d)
+    low, up, update = low_and_update(
+        z_n,
+        place,
+        live_rank,
+        tokens,
+        [adapter_slices[j] for j in range(z_n)],
+    )
     open_units = [u for u in range(units) if late[u]]
     done = add_dots(
         z_n,
-        after(place, *adapter_slices.values()),
+        after(place, low),
         tokens,
         tokens_pair,
         [late[u] for u in open_units],
@@ -594,13 +582,6 @@
         bases = natural
         columns = [jnp.zeros_like(z)]
 
-    low, up, update = low_and_update(
-        z_n,
-        place,
-        live_rank,
-        tokens,
-        [adapter_slices[j] for j in range(z_n)],
-    )
     rotated, sent = norm_and_back(
         z_n,
         place,

time: 117 us -> 115 us (0.983)
  waiting for transfers between devices: 43.3 us -> 36.6 us
  starting transfers between devices: 33.2 us -> 39.4 us
  Pallas kernels: 25 us -> 23.2 us
    ppermute x9, starting transfers between devices: 15.3 us -> 20 us  [over_z(): return lax.ppermute(v, 'fsdp', [(i, (i + d) % z_n) for i in range(z_n)])]
    ppermute x9, waiting for transfers between devices: 24.7 us -> 21 us  [over_z(): return lax.ppermute(v, 'fsdp', [(i, (i + d) % z_n) for i in range(z_n)])]
    ppermute x5, waiting for transfers between devices: 3.2 us -> 0.01 us  [over_y(): lax.ppermute(v, 'copies', [(i, (i + g) % copies_n) for i in range(copies_...]
    pallas_call x3, Pallas kernels: 9.49 us -> 8.16 us  [add_dots(): pl.pallas_call(functools.partial(dots_kernel, z_n, shards, len(totals), p...]
    ppermute x9, starting transfers between devices: 8.56 us -> 9.86 us  [over_x(): lax.ppermute(v, 'adapter', [(i, (i // 2 + e) % x_n * 2 + i % 2) for i in...]
  transfers between devices with their start and end apart: 38 -> 38, of which waited for: 11 -> 11; matrix products, arithmetic and copies ran while one was open for 11% -> 11% of each run, Pallas kernels for 14% -> 13%
where the time goes in v4:
time: 115 us
  starting transfers between devices  39.4 us (34%)
  waiting for transfers between devices  36.6 us (32%)
  Pallas kernels  23.2 us (20%)
  other arithmetic  9.25 us (8%)
  local copies, waits for them, and re-layouts  5.39 us (5%)
    ppermute x9, waiting for transfers between devices, over_z(): return lax.ppermute(v, 'fsdp', [(i, (i + d) % z_n) for i in range(z_n)])  21 us
    ppermute x9, starting transfers between devices, over_z(): return lax.ppermute(v, 'fsdp', [(i, (i + d) % z_n) for i in range(z_n)])  20 us
    ppermute x9, waiting for transfers between devices, over_x(): lax.ppermute(v, 'adapter', [(i, (i // 2 + e) % x_n * 2 + i % 2) for i in...  13.2 us
    ppermute x9, starting transfers between devices, over_x(): lax.ppermute(v, 'adapter', [(i, (i // 2 + e) % x_n * 2 + i % 2) for i in...  9.86 us
    pallas_call x3, Pallas kernels, add_dots(): pl.pallas_call(functools.partial(dots_kernel, z_n, shards, len(totals), p...  8.16 us
    ppermute x5, starting transfers between devices, over_y(): lax.ppermute(v, 'copies', [(i, (i + g) % copies_n) for i in range(copies_...  5.68 us
    pallas_call x1, Pallas kernels, norm_and_back(): pl.pallas_call(functools.partial(norm_kernel, z_n, len(bases) // 2), in_s...  4.76 us
    pallas_call x1, Pallas kernels, pick_rows(): pl.pallas_call(functools.partial(pick_kernel, sizes), in_specs=[pl.BlockS...  4.5 us
  transfers between devices with their start and end apart: 38, of which 11 were waited for; matrix products, arithmetic and copies ran while one was open for 11% of the time, Pallas kernels for 13%

profile of v4, /device:TPU:0, one launch (start us, length us, event | category | flops | bytes accessed | tf_op | source)
XLA Modules:
  0.0 114.7 jit_solution(10733334462760722009)
XLA Ops:
  2.4 4.5 %shard_map.121 = (bf16[4,64,1536]{2,1,0:T(8,128)(2,1)}, bf16[4,64,1536]{2,1,0:T(8,128)(2,1)}, bf16[4,64,1536]{2,1,0:T(8,128)(2,1)}, bf16[4,64,1536]{2,1,0:T(8,128)(2,1)}) custom-call(s32[66]{0:T(128)} %pad_add_fusion.2.numbers, bf16[12,64,1280]{2,1,0:T(8,128)(2,1)} %down_ref.1, bf16[12,64,256]{2,1,0:T(8,128)(2,1)} %up_ref.1), custom_call_target="tpu_custom_call" | custom-call | tf_op jit(solution)/shard_map/pallas_call | solution.py:85
  7.5 1.7 %constant_dynamic-slice_fusion.4 = bf16[1280,128]{1,0:T(8,128)(2,1)} fusion(bf16[1280,1024]{1,0:T(8,128)(2,1)} %param.11, s32[]{:T(128)S(6)} %select_n.92), kind=kLoop, calls=%fused_computation.18 | loop fusion | bytes 655364 | tf_op jit(solution)/shard_map/dynamic_slice | solution.py:449
  9.2 2.6 %collective-permute-start.3 = (bf16[1280,128]{1,0:T(8,128)(2,1)}, bf16[1280,128]{1,0:T(8,128)(2,1)S(1)}, u32[]{:S(2)}, u32[]{:S(2)}) collective-permute-start(bf16[1280,128]{1,0:T(8,128)(2,1)} %constant_dynamic-slice_fusion.4), channel_id=1, source_target_pairs={{0,4},{4,8},{8,12},{12,0},{1,5},{5,9},{9,13},{13,1},{2,6},{6,10},{... | collective-permute-start | bytes 983048 | tf_op jit(solution)/shard_map/ppermute | solution.py:441
  11.9 2.1 %collective-permute-start.4 = (bf16[1280,128]{1,0:T(8,128)(2,1)}, bf16[1280,128]{1,0:T(8,128)(2,1)S(1)}, u32[]{:S(2)}, u32[]{:S(2)}) collective-permute-start(bf16[1280,128]{1,0:T(8,128)(2,1)} %constant_dynamic-slice_fusion.4), channel_id=1, source_target_pairs={{0,12},{4,0},{8,4},{12,8},{1,13},{5,1},{9,5},{13,9},{2,14},{6,2},{... | collective-permute-start | bytes 983048 | tf_op jit(solution)/shard_map/ppermute | solution.py:441
  15.6 2.6 %add.107 = bf16[4,64,1536]{2,1,0:T(8,128)(2,1)} add(bf16[4,64,1536]{2,1,0:T(8,128)(2,1)} %get-tuple-element.46, bf16[4,64,1536]{2,1,0:T(8,128)(2,1)} %collective-permute-done) | non-fusion elementwise | flops 393216 | bytes 2359296 | tf_op jit(solution)/shard_map/add | solution.py:461
  18.2 4.6 %collective-permute-done.3.refs_0_ = bf16[1280,128]{1,0:T(8,128)(2,1)S(1)} collective-permute-done((bf16[1280,128]{1,0:T(8,128)(2,1)}, bf16[1280,128]{1,0:T(8,128)(2,1)S(1)}, u32[]{:S(2)}, u32[]{:S(2)}) %collective-permute-start.3) | collective-permute-done | bytes 327712 | tf_op jit(solution)/shard_map/ppermute | solution.py:441
  24.4 1.7 %collective-permute-start.11 = (bf16[4,64,1536]{2,1,0:T(8,128)(2,1)}, bf16[4,64,1536]{2,1,0:T(8,128)(2,1)}, u32[]{:S(2)}, u32[]{:S(2)}) collective-permute-start(bf16[4,64,1536]{2,1,0:T(8,128)(2,1)} %add.107), channel_id=1, source_target_pairs={{0,2},{1,3},{2,0},{3,1},{4,6},{5,7},{6,4},{7,5},{8,10},{9,11},{10,... | collective-permute-start | bytes 2359304 | tf_op jit(solution)/shard_map/ppermute | solution.py:433
  26.1 2.8 %collective-permute-done.4.refs_1_ = bf16[1280,128]{1,0:T(8,128)(2,1)S(1)} collective-permute-done((bf16[1280,128]{1,0:T(8,128)(2,1)}, bf16[1280,128]{1,0:T(8,128)(2,1)S(1)}, u32[]{:S(2)}, u32[]{:S(2)}) %collective-permute-start.4) | collective-permute-done | bytes 327712 | tf_op jit(solution)/shard_map/ppermute | solution.py:441
  36.3 2.1 %shard_map.122.refs_8_ = f32[8,256,128]{2,1,0:T(8,128)S(1)} custom-call(s32[2]{0:T(128)S(1)} %pad_add_fusion.place_ref, bf16[256,5120]{1,0:T(8,128)(2,1)S(1)} %copy-done, bf16[256,5120]{1,0:T(8,128)(2,1)S(1)} %copy-done.2, bf16[1280,128]{1,0:T(8,128)(2,1)S(1)} %get-tuple-element.92.refs_0_, bf16[1280,128]{1,0:T(8,128)(2,1)S(1)} %get-tuple-element.91.refs_1_, ...), custom_call_target="tpu_custom_call" | custom-call | tf_op jit(solution)/shard_map/pallas_call | solution.py:387
  41.0 4.2 %collective-permute-done.11 = bf16[4,64,1536]{2,1,0:T(8,128)(2,1)} collective-permute-done((bf16[4,64,1536]{2,1,0:T(8,128)(2,1)}, bf16[4,64,1536]{2,1,0:T(8,128)(2,1)}, u32[]{:S(2)}, u32[]{:S(2)}) %collective-permute-start.11) | collective-permute-done | bytes 786464 | tf_op jit(solution)/shard_map/ppermute | solution.py:433
  46.8 3.9 %collective-permute-start.13 = (bf16[64,1536]{1,0:T(8,128)(2,1)S(1)}, bf16[64,1536]{1,0:T(8,128)(2,1)S(1)}, u32[]{:S(2)}, u32[]{:S(2)}) collective-permute-start(bf16[64,1536]{1,0:T(8,128)(2,1)S(1)} %get-tuple-element.94), channel_id=1, source_target_pairs={{0,8},{4,12},{8,0},{12,4},{1,9},{5,13},{9,1},{13,5},{2,10},{6,14},... | collective-permute-start | bytes 589832 | tf_op jit(solution)/shard_map/ppermute | solution.py:441
  50.7 2.2 %collective-permute-start.14 = (bf16[64,1536]{1,0:T(8,128)(2,1)S(1)}, bf16[64,1536]{1,0:T(8,128)(2,1)S(1)}, u32[]{:S(2)}, u32[]{:S(2)}) collective-permute-start(bf16[64,1536]{1,0:T(8,128)(2,1)S(1)} %get-tuple-element.93), channel_id=1, source_target_pairs={{0,4},{4,8},{8,12},{12,0},{1,5},{5,9},{9,13},{13,1},{2,6},{6,10},{... | collective-permute-start | bytes 589832 | tf_op jit(solution)/shard_map/ppermute | solution.py:441
  52.9 4.2 %collective-permute-done.7.refs_3_ = bf16[1280,128]{1,0:T(8,128)(2,1)S(1)} collective-permute-done((bf16[1280,128]{1,0:T(8,128)(2,1)S(1)}, bf16[1280,128]{1,0:T(8,128)(2,1)S(1)}, u32[]{:S(2)}, u32[]{:S(2)}) %collective-permute-start.7) | collective-permute-done | bytes 327712 | tf_op jit(solution)/shard_map/ppermute | solution.py:433
  61.2 4.6 %collective-permute-start.12 = (bf16[64,1536]{1,0:T(8,128)(2,1)S(1)}, bf16[64,1536]{1,0:T(8,128)(2,1)S(1)}, u32[]{:S(2)}, u32[]{:S(2)}) collective-permute-start(bf16[64,1536]{1,0:T(8,128)(2,1)S(1)} %get-tuple-element.95), channel_id=1, source_target_pairs={{0,12},{4,0},{8,4},{12,8},{1,13},{5,1},{9,5},{13,9},{2,14},{6,2},{... | collective-permute-start | bytes 589832 | tf_op jit(solution)/shard_map/ppermute | solution.py:441
  65.7 4.0 %shard_map.123 = (f32[256,128]{1,0:T(8,128)S(1)}, f32[256,128]{1,0:T(8,128)S(1)}, f32[256,128]{1,0:T(8,128)S(1)}, f32[256,128]{1,0:T(8,128)S(1)}, f32[256,128]{1...) custom-call(s32[2]{0:T(128)S(1)} %pad_add_fusion.place_ref, ...), custom_call_target="tpu_custom_call" | custom-call | tf_op jit(solution)/shard_map/pallas_call | solution.py:387
  69.8 2.6 %shard_map.124 = (bf16[256,64]{1,0:T(8,128)(2,1)S(1)}, bf16[64,1024]{1,0:T(8,128)(2,1)S(1)}, f32[256,1024]{1,0:T(8,128)S(1)}) custom-call(s32[2]{0:T(128)S(1)} %pad_add_fusion.place_ref, s32[1,1]{1,0:T(1,128)} %bitcast.6.rank_ref, bf16[256,5120]{1,0:T(8,128)(2,1)S(1)} %copy-done, bf16[64,1536]{1,0:T(8,128)(2,1)S(1)} %get-tuple-element.96.refs_0_, ...), custom_call_target="tpu_custom_call" | custom-call | tf_op jit(solution)/shard_map/pallas_call | solution.py:200
  73.1 2.1 %shard_map.125 = (f32[256,128]{1,0:T(8,128)S(1)}, f32[256,128]{1,0:T(8,128)S(1)}, f32[256,128]{1,0:T(8,128)S(1)}, f32[256,128]{1,0:T(8,128)S(1)}) custom-call(s32[2]{0:T(128)S(1)} %pad_add_fusion.place_ref, bf16[256,5120]{1,0:T(8,128)(2,1)S(1)} %copy-done, bf16[256,5120]{1,0:T(8,128)(2,1)S(1)} %copy-done.2, ...), custom_call_target="tpu_custom_call" | custom-call | tf_op jit(solution)/shard_map/pallas_call | solution.py:387
  76.8 4.8 %shard_map.126 = (bf16[256,1024]{1,0:T(8,128)(2,1)}, bf16[64,1536]{1,0:T(8,128)(2,1)S(1)}, bf16[64,1536]{1,0:T(8,128)(2,1)S(1)}, bf16[64,1536]{1,0:T(8,128)(2,1)S(1)}, bf16[64,1536]{1,0:T(8,128)(2,1)S(1)}) custom-call(s32[2]{0:T(128)S(1)} %pad_add_fusion.place_ref, s32[4]{0:T(128)S(1)} %pad_add_fusion.1.columns_ref, s32[1,1]{1,0:T(1,128)} %bitcast.6.rank_ref, ...), custom_call_target="tpu_custom_call" | custom-call | tf_op jit(solution)/shard_map/pallas_call | solution.py:310
  83.4 3.1 %collective-permute-start.30 = (bf16[64,1536]{1,0:T(8,128)(2,1)S(1)}, bf16[64,1536]{1,0:T(8,128)(2,1)S(1)}, u32[]{:S(2)}, u32[]{:S(2)}) collective-permute-start(bf16[64,1536]{1,0:T(8,128)(2,1)S(1)} %get-tuple-element.85), channel_id=1, source_target_pairs={{0,12},{4,0},{8,4},{12,8},{1,13},{5,1},{9,5},{13,9},{2,14},{6,2},{... | collective-permute-start | bytes 589832 | tf_op jit(solution)/shard_map/ppermute | solution.py:441
  86.7 4.5 %collective-permute-done.26 = bf16[64,1536]{1,0:T(8,128)(2,1)S(1)} collective-permute-done((bf16[64,1536]{1,0:T(8,128)(2,1)S(1)}, bf16[64,1536]{1,0:T(8,128)(2,1)S(1)}, u32[]{:S(2)}, u32[]{:S(2)}) %collective-permute-start.26) | collective-permute-done | bytes 196640 | tf_op jit(solution)/shard_map/ppermute | solution.py:441
  92.8 1.9 %collective-permute-done.30 = bf16[64,1536]{1,0:T(8,128)(2,1)S(1)} collective-permute-done((bf16[64,1536]{1,0:T(8,128)(2,1)S(1)}, bf16[64,1536]{1,0:T(8,128)(2,1)S(1)}, u32[]{:S(2)}, u32[]{:S(2)}) %collective-permute-start.30) | collective-permute-done | bytes 196640 | tf_op jit(solution)/shard_map/ppermute | solution.py:441
  95.9 7.3 %collective-permute-done.34 = bf16[64,1536]{1,0:T(8,128)(2,1)S(1)} collective-permute-done((bf16[64,1536]{1,0:T(8,128)(2,1)S(1)}, bf16[64,1536]{1,0:T(8,128)(2,1)S(1)}, u32[]{:S(2)}, u32[]{:S(2)}) %collective-permute-start.34) | collective-permute-done | bytes 196640 | tf_op jit(solution)/shard_map/ppermute | solution.py:441
  105.3 4.7 %collective-permute-done.36.refs_14_ = bf16[1,64,1536]{2,1,0:T(8,128)(2,1)S(1)} collective-permute-done((bf16[1,64,1536]{2,1,0:T(8,128)(2,1)S(1)}, bf16[1,64,1536]{2,1,0:T(8,128)(2,1)S(1)}, u32[]{:S(2)}, u32[]{:S(2)}) %collective-permute-start.36) | collective-permute-done | bytes 196640 | tf_op jit(solution)/shard_map/ppermute | solution.py:433
  111.5 3.2 %shard_map.127 = (f32[12,64,1280]{2,1,0:T(8,128)}, f32[12,64,256]{2,1,0:T(8,128)}) custom-call(s32[66]{0:T(128)S(1)} %copy-done.4, bf16[1,64,1536]{2,1,0:T(8,128)(2,1)S(1)} %bitcast.29, bf16[1,64,1536]{2,1,0:T(8,128)(2,1)S(1)} %collective-permute-done.23.refs_1_, bf16[1,64,1536]{2,1,0:T(8,128)(2,1)S(1)} %collective-permute-done.24.refs_2_, ...), custom_call_target="tpu_custom_call" | custom-call | tf_op jit(solution)/shard_map/pallas_call | solution.py:141
  (99 shorter events, 31.9 us)
Async XLA Ops:
  0.6 13.4 %collective-permute-start.1 = (bf16[256,5120]{1,0:T(8,128)(2,1)}, bf16[256,5120]{1,0:T(8,128)(2,1)S(1)}, u32[]{:S(2)}, u32[]{:S(2)}) collective-permute-start(bf16[256,5120]{1,0:T(8,128)(2,1)} %refs_15_.1), channel_id=1, source_target_pairs={{0,1},{1,0},{2,3},{3,2},{4,5},{5,4},{6,7},{7,6},{8,9},{9,8},{10,11... | collective-permute-start | bytes 7864328 | tf_op jit(solution)/shard_map/ppermute | solution.py:430
  9.2 13.5 %collective-permute-start.3 = (bf16[1280,128]{1,0:T(8,128)(2,1)}, bf16[1280,128]{1,0:T(8,128)(2,1)S(1)}, u32[]{:S(2)}, u32[]{:S(2)}) collective-permute-start(bf16[1280,128]{1,0:T(8,128)(2,1)} %constant_dynamic-slice_fusion.4), channel_id=1, source_target_pairs={{0,4},{4,8},{8,12},{12,0},{1,5},{5,9},{9,13},{13,1},{2,6},{6,10},{... | collective-permute-start | bytes 983048 | tf_op jit(solution)/shard_map/ppermute | solution.py:441
  11.9 17.0 %collective-permute-start.4 = (bf16[1280,128]{1,0:T(8,128)(2,1)}, bf16[1280,128]{1,0:T(8,128)(2,1)S(1)}, u32[]{:S(2)}, u32[]{:S(2)}) collective-permute-start(bf16[1280,128]{1,0:T(8,128)(2,1)} %constant_dynamic-slice_fusion.4), channel_id=1, source_target_pairs={{0,12},{4,0},{8,4},{12,8},{1,13},{5,1},{9,5},{13,9},{2,14},{6,2},{... | collective-permute-start | bytes 983048 | tf_op jit(solution)/shard_map/ppermute | solution.py:441
  22.8 17.0 %collective-permute-start.6 = (bf16[1280,128]{1,0:T(8,128)(2,1)S(1)}, bf16[1280,128]{1,0:T(8,128)(2,1)}, u32[]{:S(2)}, u32[]{:S(2)}) collective-permute-start(bf16[1280,128]{1,0:T(8,128)(2,1)S(1)} %collective-permute-done.3.refs_0_), channel_id=1, source_target_pairs={{0,16},{16,0},{1,17},{17,1},{2,18},{18,2},{3,19},{19,3},{4,20},{20... | collective-permute-start | bytes 983048 | tf_op jit(solution)/shard_map/ppermute | solution.py:438
  24.4 16.0 %collective-permute-start.5 = (bf16[1280,128]{1,0:T(8,128)(2,1)S(1)}, bf16[1280,128]{1,0:T(8,128)(2,1)}, u32[]{:S(2)}, u32[]{:S(2)}) collective-permute-start(bf16[1280,128]{1,0:T(8,128)(2,1)S(1)} %collective-permute-done.3.refs_0_), channel_id=1, source_target_pairs={{0,4},{4,8},{8,12},{12,0},{1,5},{5,9},{9,13},{13,1},{2,6},{6,10},{... | collective-permute-start | bytes 983048 | tf_op jit(solution)/shard_map/ppermute | solution.py:441
  24.4 20.8 %collective-permute-start.11 = (bf16[4,64,1536]{2,1,0:T(8,128)(2,1)}, bf16[4,64,1536]{2,1,0:T(8,128)(2,1)}, u32[]{:S(2)}, u32[]{:S(2)}) collective-permute-start(bf16[4,64,1536]{2,1,0:T(8,128)(2,1)} %add.107), channel_id=1, source_target_pairs={{0,2},{1,3},{2,0},{3,1},{4,6},{5,7},{6,4},{7,5},{8,10},{9,11},{10,... | collective-permute-start | bytes 2359304 | tf_op jit(solution)/shard_map/ppermute | solution.py:433
  30.8 19.9 %collective-permute-start.9 = (bf16[1280,128]{1,0:T(8,128)(2,1)S(1)}, bf16[1280,128]{1,0:T(8,128)(2,1)S(1)}, u32[]{:S(2)}, u32[]{:S(2)}) collective-permute-start(bf16[1280,128]{1,0:T(8,128)(2,1)S(1)} %collective-permute-done.4.refs_1_), channel_id=1, source_target_pairs={{0,16},{16,0},{1,17},{17,1},{2,18},{18,2},{3,19},{19,3},{4,20},{20... | collective-permute-start | bytes 983048 | tf_op jit(solution)/shard_map/ppermute | solution.py:438
  38.3 19.8 %collective-permute-start.8 = (bf16[1280,128]{1,0:T(8,128)(2,1)S(1)}, bf16[1280,128]{1,0:T(8,128)(2,1)S(1)}, u32[]{:S(2)}, u32[]{:S(2)}) collective-permute-start(bf16[1280,128]{1,0:T(8,128)(2,1)S(1)} %collective-permute-done.4.refs_1_), channel_id=1, source_target_pairs={{0,2},{1,3},{2,0},{3,1},{4,6},{5,7},{6,4},{7,5},{8,10},{9,11},{10,... | collective-permute-start | bytes 983048 | tf_op jit(solution)/shard_map/ppermute | solution.py:433
  39.8 17.3 %collective-permute-start.7 = (bf16[1280,128]{1,0:T(8,128)(2,1)S(1)}, bf16[1280,128]{1,0:T(8,128)(2,1)S(1)}, u32[]{:S(2)}, u32[]{:S(2)}) collective-permute-start(bf16[1280,128]{1,0:T(8,128)(2,1)S(1)} %collective-permute-done.3.refs_0_), channel_id=1, source_target_pairs={{0,2},{1,3},{2,0},{3,1},{4,6},{5,7},{6,4},{7,5},{8,10},{9,11},{10,... | collective-permute-start | bytes 983048 | tf_op jit(solution)/shard_map/ppermute | solution.py:433
  40.4 18.8 %collective-permute-start.10 = (bf16[1280,128]{1,0:T(8,128)(2,1)}, bf16[1280,128]{1,0:T(8,128)(2,1)S(1)}, u32[]{:S(2)}, u32[]{:S(2)}) collective-permute-start(bf16[1280,128]{1,0:T(8,128)(2,1)} %collective-permute-done.5.refs_2_), channel_id=1, source_target_pairs={{0,16},{16,0},{1,17},{17,1},{2,18},{18,2},{3,19},{19,3},{4,20},{20... | collective-permute-start | bytes 983048 | tf_op jit(solution)/shard_map/ppermute | solution.py:438
  46.8 13.4 %collective-permute-start.13 = (bf16[64,1536]{1,0:T(8,128)(2,1)S(1)}, bf16[64,1536]{1,0:T(8,128)(2,1)S(1)}, u32[]{:S(2)}, u32[]{:S(2)}) collective-permute-start(bf16[64,1536]{1,0:T(8,128)(2,1)S(1)} %get-tuple-element.94), channel_id=1, source_target_pairs={{0,8},{4,12},{8,0},{12,4},{1,9},{5,13},{9,1},{13,5},{2,10},{6,14},... | collective-permute-start | bytes 589832 | tf_op jit(solution)/shard_map/ppermute | solution.py:441
  50.7 10.5 %collective-permute-start.14 = (bf16[64,1536]{1,0:T(8,128)(2,1)S(1)}, bf16[64,1536]{1,0:T(8,128)(2,1)S(1)}, u32[]{:S(2)}, u32[]{:S(2)}) collective-permute-start(bf16[64,1536]{1,0:T(8,128)(2,1)S(1)} %get-tuple-element.93), channel_id=1, source_target_pairs={{0,4},{4,8},{8,12},{12,0},{1,5},{5,9},{9,13},{13,1},{2,6},{6,10},{... | collective-permute-start | bytes 589832 | tf_op jit(solution)/shard_map/ppermute | solution.py:441
  57.1 15.4 %collective-permute-start.15 = (bf16[1280,128]{1,0:T(8,128)(2,1)}, bf16[1280,128]{1,0:T(8,128)(2,1)S(1)}, u32[]{:S(2)}, u32[]{:S(2)}) collective-permute-start(bf16[1280,128]{1,0:T(8,128)(2,1)} %collective-permute-done.5.refs_2_), channel_id=1, source_target_pairs={{0,2},{1,3},{2,0},{3,1},{4,6},{5,7},{6,4},{7,5},{8,10},{9,11},{10,... | collective-permute-start | bytes 983048 | tf_op jit(solution)/shard_map/ppermute | solution.py:433
  58.1 14.9 %collective-permute-start.16 = (bf16[1280,128]{1,0:T(8,128)(2,1)S(1)}, bf16[1280,128]{1,0:T(8,128)(2,1)S(1)}, u32[]{:S(2)}, u32[]{:S(2)}) collective-permute-start(bf16[1280,128]{1,0:T(8,128)(2,1)S(1)} %collective-permute-done.7.refs_3_), channel_id=1, source_target_pairs={{0,16},{16,0},{1,17},{17,1},{2,18},{18,2},{3,19},{19,3},{4,20},{20... | collective-permute-start | bytes 983048 | tf_op jit(solution)/shard_map/ppermute | solution.py:438
  59.2 13.9 %collective-permute-start.17 = (bf16[1280,128]{1,0:T(8,128)(2,1)S(1)}, bf16[1280,128]{1,0:T(8,128)(2,1)S(1)}, u32[]{:S(2)}, u32[]{:S(2)}) collective-permute-start(bf16[1280,128]{1,0:T(8,128)(2,1)S(1)} %collective-permute-done.8.refs_4_), channel_id=1, source_target_pairs={{0,16},{16,0},{1,17},{17,1},{2,18},{18,2},{3,19},{19,3},{4,20},{20... | collective-permute-start | bytes 983048 | tf_op jit(solution)/shard_map/ppermute | solution.py:438
  60.2 12.9 %collective-permute-start.18 = (bf16[1280,128]{1,0:T(8,128)(2,1)S(1)}, bf16[1280,128]{1,0:T(8,128)(2,1)S(1)}, u32[]{:S(2)}, u32[]{:S(2)}) collective-permute-start(bf16[1280,128]{1,0:T(8,128)(2,1)S(1)} %collective-permute-done.10.refs_7_), channel_id=1, source_target_pairs={{0,2},{1,3},{2,0},{3,1},{4,6},{5,7},{6,4},{7,5},{8,10},{9,11},{10,... | collective-permute-start | bytes 983048 | tf_op jit(solution)/shard_map/ppermute | solution.py:433
  81.5 9.6 %collective-permute-start.26 = (bf16[64,1536]{1,0:T(8,128)(2,1)S(1)}, bf16[64,1536]{1,0:T(8,128)(2,1)S(1)}, u32[]{:S(2)}, u32[]{:S(2)}) collective-permute-start(bf16[64,1536]{1,0:T(8,128)(2,1)S(1)} %get-tuple-element.84), channel_id=1, source_target_pairs={{0,4},{4,8},{8,12},{12,0},{1,5},{5,9},{9,13},{13,1},{2,6},{6,10},{... | collective-permute-start | bytes 589832 | tf_op jit(solution)/shard_map/ppermute | solution.py:441
  82.9 9.4 %collective-permute-start.24 = (bf16[1,64,1536]{2,1,0:T(8,128)(2,1)S(1)}, bf16[1,64,1536]{2,1,0:T(8,128)(2,1)S(1)}, u32[]{:S(2)}, u32[]{:S(2)}) collective-permute-start(bf16[1,64,1536]{2,1,0:T(8,128)(2,1)S(1)} %bitcast.27), channel_id=1, source_target_pairs={{0,2},{1,3},{2,0},{3,1},{4,6},{5,7},{6,4},{7,5},{8,10},{9,11},{10,... | collective-permute-start | bytes 589832 | tf_op jit(solution)/shard_map/ppermute | solution.py:433
  83.4 11.3 %collective-permute-start.30 = (bf16[64,1536]{1,0:T(8,128)(2,1)S(1)}, bf16[64,1536]{1,0:T(8,128)(2,1)S(1)}, u32[]{:S(2)}, u32[]{:S(2)}) collective-permute-start(bf16[64,1536]{1,0:T(8,128)(2,1)S(1)} %get-tuple-element.85), channel_id=1, source_target_pairs={{0,12},{4,0},{8,4},{12,8},{1,13},{5,1},{9,5},{13,9},{2,14},{6,2},{... | collective-permute-start | bytes 589832 | tf_op jit(solution)/shard_map/ppermute | solution.py:441
  86.6 16.6 %collective-permute-start.34 = (bf16[64,1536]{1,0:T(8,128)(2,1)S(1)}, bf16[64,1536]{1,0:T(8,128)(2,1)S(1)}, u32[]{:S(2)}, u32[]{:S(2)}) collective-permute-start(bf16[64,1536]{1,0:T(8,128)(2,1)S(1)} %get-tuple-element.86), channel_id=1, source_target_pairs={{0,8},{4,12},{8,0},{12,4},{1,9},{5,13},{9,1},{13,5},{2,10},{6,14},... | collective-permute-start | bytes 589832 | tf_op jit(solution)/shard_map/ppermute | solution.py:441
  91.1 13.2 %collective-permute-start.28 = (bf16[1,64,1536]{2,1,0:T(8,128)(2,1)S(1)}, bf16[1,64,1536]{2,1,0:T(8,128)(2,1)S(1)}, u32[]{:S(2)}, u32[]{:S(2)}) collective-permute-start(bf16[1,64,1536]{2,1,0:T(8,128)(2,1)S(1)} %bitcast.30), channel_id=1, source_target_pairs={{0,2},{1,3},{2,0},{3,1},{4,6},{5,7},{6,4},{7,5},{8,10},{9,11},{10,... | collective-permute-start | bytes 589832 | tf_op jit(solution)/shard_map/ppermute | solution.py:433
  92.3 12.0 %collective-permute-start.25 = (bf16[1,64,1536]{2,1,0:T(8,128)(2,1)S(1)}, bf16[1,64,1536]{2,1,0:T(8,128)(2,1)S(1)}, u32[]{:S(2)}, u32[]{:S(2)}) collective-permute-start(bf16[1,64,1536]{2,1,0:T(8,128)(2,1)S(1)} %collective-permute-done.24.refs_2_), channel_id=1, source_target_pairs={{0,1},{1,0},{2,3},{3,2},{4,5},{5,4},{6,7},{7,6},{8,9},{9,8},{10,11... | collective-permute-start | bytes 589832 | tf_op jit(solution)/shard_map/ppermute | solution.py:430
  92.3 12.5 %collective-permute-start.27 = (bf16[1,64,1536]{2,1,0:T(8,128)(2,1)S(1)}, bf16[1,64,1536]{2,1,0:T(8,128)(2,1)S(1)}, u32[]{:S(2)}, u32[]{:S(2)}) collective-permute-start(bf16[1,64,1536]{2,1,0:T(8,128)(2,1)S(1)} %bitcast.31), channel_id=1, source_target_pairs={{0,1},{1,0},{2,3},{3,2},{4,5},{5,4},{6,7},{7,6},{8,9},{9,8},{10,11... | collective-permute-start | bytes 589832 | tf_op jit(solution)/shard_map/ppermute | solution.py:430
  94.7 10.2 %collective-permute-start.32 = (bf16[1,64,1536]{2,1,0:T(8,128)(2,1)S(1)}, bf16[1,64,1536]{2,1,0:T(8,128)(2,1)S(1)}, u32[]{:S(2)}, u32[]{:S(2)}) collective-permute-start(bf16[1,64,1536]{2,1,0:T(8,128)(2,1)S(1)} %bitcast.33), channel_id=1, source_target_pairs={{0,2},{1,3},{2,0},{3,1},{4,6},{5,7},{6,4},{7,5},{8,10},{9,11},{10,... | collective-permute-start | bytes 589832 | tf_op jit(solution)/shard_map/ppermute | solution.py:433
  (24 other events, 236.0 us)

commit v5 on v4

--- a/solution.py
+++ b/solution.py
@@ -29,21 +29,21 @@
     return index_iota - first_index
 
 
-def block_row(numbers, blocks, z_to, group_to, group_n):
-    return numbers[2 + blocks + numbers[2 + z_to * group_n + group_to]]
-
-
-def pick_kernel(sizes, numbers, down_ref, up_ref, *refs):
+def block_row(packed, storage, z_to, group_to, group_n):
+    return storage[packed[z_to * group_n + group_to]]
+
+
+def pick_kernel(sizes, packed, storage, down_ref, up_ref, *refs):
     x_n, z_n = sizes
     out_refs, (down_buffer, up_buffer, semaphores) = refs[: 2 * x_n], refs[2 * x_n :]
     owned = down_ref.shape[0]
-    z, a = numbers[0], numbers[1]
+    z, a = lax.axis_index("fsdp"), lax.axis_index("adapter")
     x, core = a // 2, a % 2
 
     def for_block(n, act):
         pair, e, j = n // (x_n * z_n), n // z_n % x_n, n % z_n
         group_to = ((x + e) % x_n) * 2 + (core + pair) % 2
-        row = block_row(numbers, 2 * x_n * z_n, (z + j) % z_n, group_to, 2 * x_n) - a * owned
+        row = block_row(packed, storage, (z + j) % z_n, group_to, 2 * x_n) - a * owned
         hit = jnp.logical_and(row >= 0, row < owned)
 
         @pl.when(hit)
@@ -77,14 +77,14 @@
         lax.fori_loop(0, z_n, finish, 0)
 
 
-def pick_rows(sizes, numbers, down, up):
+def pick_rows(sizes, packed, storage, down, up):
     x_n, z_n = sizes
     count = 2 * x_n * z_n
     _, rank, down_width = down.shape
     up_width = up.shape[2]
     return pl.pallas_call(
         functools.partial(pick_kernel, sizes),
-        in_specs=[pl.BlockSpec(memory_space=pltpu.SMEM)]
+        in_specs=[pl.BlockSpec(memory_space=pltpu.SMEM)] * 2
         + [pl.BlockSpec(memory_space=pltpu.HBM)] * 2,
         out_specs=[pl.BlockSpec(memory_space=pltpu.VMEM)] * (2 * x_n),
         out_shape=[jax.ShapeDtypeStruct((z_n, rank, down_width + up_width), down.dtype)]
@@ -95,16 +95,16 @@
             pltpu.SemaphoreType.DMA((2, count)),
         ],
         compiler_params=pltpu.CompilerParams(vmem_limit_bytes=56 * 1024 * 1024),
-    )(numbers, down, up)
-
-
-def owner_sum_kernel(sizes, groups, numbers, *refs):
+    )(packed, storage, down, up)
+
+
+def owner_sum_kernel(sizes, groups, packed, storage, *refs):
     x_n, z_n = sizes
     count = x_n * 2 * len(groups)
     block_refs, down_ref, up_ref = refs[:count], refs[count], refs[count + 1]
     owned, tile, down_width = down_ref.shape
     first_row = pl.multiple_of(pl.program_id(0) * tile, tile)
-    z, a = numbers[0], numbers[1]
+    z, a = lax.axis_index("fsdp"), lax.axis_index("adapter")
     x, core = a // 2, a % 2
     down_ref[...] = jnp.zeros_like(down_ref)
     up_ref[...] = jnp.zeros_like(up_ref)
@@ -116,7 +116,7 @@
 
                 def one(k, carry, i=i, first=group[0], group_from=group_from):
                     z_from = (z - first - k + z_n) % z_n
-                    row = block_row(numbers, 2 * x_n * z_n, z_from, group_from, 2 * x_n)
+                    row = block_row(packed, storage, z_from, group_from, 2 * x_n)
                     row = row - a * owned
 
                     @pl.when(jnp.logical_and(row >= 0, row < owned))
@@ -134,15 +134,14 @@
                 i += 1
 
 
-def owner_sum(sizes, groups, numbers, blocks, owned, down_width):
+def owner_sum(sizes, groups, packed, storage, blocks, owned, down_width):
     _, rank, width = blocks[0].shape
     tile = 32
     smem = pl.BlockSpec(memory_space=pltpu.SMEM)
     return pl.pallas_call(
         functools.partial(owner_sum_kernel, sizes, groups),
         grid=(rank // tile,),
-        in_specs=[smem]
-        + [pl.BlockSpec(memory_space=pltpu.VMEM)] * len(blocks),
+        in_specs=[smem] * 2 + [pl.BlockSpec(memory_space=pltpu.VMEM)] * len(blocks),
         out_specs=[
             pl.BlockSpec((owned, tile, down_width), lambda t: (0, t, 0)),
             pl.BlockSpec((owned, tile, width - down_width), lambda t: (0, t, 0)),
@@ -151,8 +150,8 @@
             jax.ShapeDtypeStruct((owned, rank, down_width), jnp.float32),
             jax.ShapeDtypeStruct((owned, rank, width - down_width), jnp.float32),
         ],
-        compiler_params=pltpu.CompilerParams(vmem_limit_bytes=24 * 1024 * 1024),
-    )(numbers, *blocks)
+        compiler_params=pltpu.CompilerParams(vmem_limit_bytes=16 * 1024 * 1024),
+    )(packed, storage, *blocks)
 
 
 def low_kernel(
@@ -318,7 +317,7 @@
             pltpu.VMEM((rank, features), jnp.bfloat16),
             pltpu.SemaphoreType.DMA((2,)),
         ],
-        compiler_params=pltpu.CompilerParams(vmem_limit_bytes=24 * 1024 * 1024),
+        compiler_params=pltpu.CompilerParams(vmem_limit_bytes=12 * 1024 * 1024),
     )(
         place, columns, live_rank, *bases, update, low, up, cosine, sine, gain,
         gradient, tokens,
@@ -451,12 +450,13 @@
     unit = unit_at(y, x)
     sizes = (x_n, z_n)
     place = jnp.stack([z, a]).astype(jnp.int32)
-    numbers = jnp.concatenate([place, packed_block_adapter, adapter_storage_row])
     shifts = sorted(range(1, z_n), key=lambda d: min(d, z_n - d))
     final = len(shifts) - 1
 
     tokens_pair = over_core(tokens)
-    picked = pick_rows(sizes, numbers, adapter_down_weight, adapter_up_weight)
+    picked = pick_rows(
+        sizes, packed_block_adapter, adapter_storage_row, adapter_down_weight, adapter_up_weight
+    )
     taken = [over_core(picked[x_n + e]) for e in range(x_n)]
     away = [picked[e] + after(taken[e], tokens_pair, taken[0]) for e in range(1, x_n)]
     slices = picked[0] + taken[0]
@@ -613,7 +613,8 @@
     grad_down, grad_up = owner_sum(
         sizes,
         groups,
-        numbers,
+        packed_block_adapter,
+        adapter_storage_row,
         blocks,
         owned,
         down_width,

time: 115 us -> 114 us (level)
  other arithmetic: 9.25 us -> 8.04 us
    concatenate x1 -> x0, other arithmetic: 1.28 us -> none  [per_device(): jnp.concatenate([place, packed_block_adapter, adapter_storage_row])]
  transfers between devices with their start and end apart: 38 -> 38, of which waited for: 11 -> 12; matrix products, arithmetic and copies ran while one was open for 11% -> 10% of each run, Pallas kernels for 13% -> 13%
where the time goes in v5:
time: 114 us
  starting transfers between devices  40.3 us (35%)
  waiting for transfers between devices  36 us (32%)
  Pallas kernels  23.1 us (20%)
  other arithmetic  8.04 us (7%)
  local copies, waits for them, and re-layouts  5.38 us (5%)
    ppermute x9, waiting for transfers between devices, over_z(): return lax.ppermute(v, 'fsdp', [(i, (i + d) % z_n) for i in range(z_n)])  20.5 us
    ppermute x9, starting transfers between devices, over_z(): return lax.ppermute(v, 'fsdp', [(i, (i + d) % z_n) for i in range(z_n)])  20.2 us
    ppermute x9, waiting for transfers between devices, over_x(): lax.ppermute(v, 'adapter', [(i, (i // 2 + e) % x_n * 2 + i % 2) for i in...  12.8 us
    ppermute x9, starting transfers between devices, over_x(): lax.ppermute(v, 'adapter', [(i, (i // 2 + e) % x_n * 2 + i % 2) for i in...  10.4 us
    pallas_call x3, Pallas kernels, add_dots(): pl.pallas_call(functools.partial(dots_kernel, z_n, shards, len(totals), p...  8.17 us
    ppermute x5, starting transfers between devices, over_y(): lax.ppermute(v, 'copies', [(i, (i + g) % copies_n) for i in range(copies_...  5.74 us
    pallas_call x1, Pallas kernels, norm_and_back(): pl.pallas_call(functools.partial(norm_kernel, z_n, len(bases) // 2), in_s...  4.77 us
    pallas_call x1, Pallas kernels, pick_rows(): pl.pallas_call(functools.partial(pick_kernel, sizes), in_specs=[pl.BlockS...  4.39 us
  transfers between devices with their start and end apart: 38, of which 12 were waited for; matrix products, arithmetic and copies ran while one was open for 10% of the time, Pallas kernels for 13%

profile of v5, /device:TPU:0, one launch (start us, length us, event | category | flops | bytes accessed | tf_op | source)
XLA Modules:
  0.0 113.7 jit_solution(4234296796009882971)
XLA Ops:
  1.2 4.4 %shard_map.121 = (bf16[4,64,1536]{2,1,0:T(8,128)(2,1)}, bf16[4,64,1536]{2,1,0:T(8,128)(2,1)}, bf16[4,64,1536]{2,1,0:T(8,128)(2,1)}, bf16[4,64,1536]{2,1,0:T(8,128)(2,1)}) custom-call(s32[16]{0:T(128)} %packed.3, s32[48]{0:T(128)} %storage.3, bf16[12,64,1280]{2,1,0:T(8,128)(2,1)} %down_ref.1, bf16[12,64,256]{2,1,0:T(8,128)(2,1)} %up_ref.1), custom_call_target="tpu_custom_call" | custom-call | tf_op jit(solution)/shard_map/pallas_call | solution.py:85
  6.2 1.7 %constant_dynamic-slice_fusion.4 = bf16[1280,128]{1,0:T(8,128)(2,1)} fusion(bf16[1280,1024]{1,0:T(8,128)(2,1)} %param.11, s32[]{:T(128)S(6)} %select_n.92), kind=kLoop, calls=%fused_computation.18 | loop fusion | bytes 655364 | tf_op jit(solution)/shard_map/dynamic_slice | solution.py:448
  7.9 2.6 %collective-permute-start.3 = (bf16[1280,128]{1,0:T(8,128)(2,1)}, bf16[1280,128]{1,0:T(8,128)(2,1)S(1)}, u32[]{:S(2)}, u32[]{:S(2)}) collective-permute-start(bf16[1280,128]{1,0:T(8,128)(2,1)} %constant_dynamic-slice_fusion.4), channel_id=1, source_target_pairs={{0,4},{4,8},{8,12},{12,0},{1,5},{5,9},{9,13},{13,1},{2,6},{6,10},{... | collective-permute-start | bytes 983048 | tf_op jit(solution)/shard_map/ppermute | solution.py:440
  10.5 2.1 %collective-permute-start.4 = (bf16[1280,128]{1,0:T(8,128)(2,1)}, bf16[1280,128]{1,0:T(8,128)(2,1)S(1)}, u32[]{:S(2)}, u32[]{:S(2)}) collective-permute-start(bf16[1280,128]{1,0:T(8,128)(2,1)} %constant_dynamic-slice_fusion.4), channel_id=1, source_target_pairs={{0,12},{4,0},{8,4},{12,8},{1,13},{5,1},{9,5},{13,9},{2,14},{6,2},{... | collective-permute-start | bytes 983048 | tf_op jit(solution)/shard_map/ppermute | solution.py:440
  14.1 2.6 %add.107 = bf16[4,64,1536]{2,1,0:T(8,128)(2,1)} add(bf16[4,64,1536]{2,1,0:T(8,128)(2,1)} %get-tuple-element.46, bf16[4,64,1536]{2,1,0:T(8,128)(2,1)} %collective-permute-done) | non-fusion elementwise | flops 393216 | bytes 2359296 | tf_op jit(solution)/shard_map/add | solution.py:461
  16.8 4.6 %collective-permute-done.3.refs_0_ = bf16[1280,128]{1,0:T(8,128)(2,1)S(1)} collective-permute-done((bf16[1280,128]{1,0:T(8,128)(2,1)}, bf16[1280,128]{1,0:T(8,128)(2,1)S(1)}, u32[]{:S(2)}, u32[]{:S(2)}) %collective-permute-start.3) | collective-permute-done | bytes 327712 | tf_op jit(solution)/shard_map/ppermute | solution.py:440
  21.4 1.7 %collective-permute-start.6 = (bf16[1280,128]{1,0:T(8,128)(2,1)S(1)}, bf16[1280,128]{1,0:T(8,128)(2,1)}, u32[]{:S(2)}, u32[]{:S(2)}) collective-permute-start(bf16[1280,128]{1,0:T(8,128)(2,1)S(1)} %collective-permute-done.3.refs_0_), channel_id=1, source_target_pairs={{0,16},{16,0},{1,17},{17,1},{2,18},{18,2},{3,19},{19,3},{4,20},{20... | collective-permute-start | bytes 983048 | tf_op jit(solution)/shard_map/ppermute | solution.py:437
  24.5 3.0 %collective-permute-done.4.refs_1_ = bf16[1280,128]{1,0:T(8,128)(2,1)S(1)} collective-permute-done((bf16[1280,128]{1,0:T(8,128)(2,1)}, bf16[1280,128]{1,0:T(8,128)(2,1)S(1)}, u32[]{:S(2)}, u32[]{:S(2)}) %collective-permute-start.4) | collective-permute-done | bytes 327712 | tf_op jit(solution)/shard_map/ppermute | solution.py:440
  34.9 2.1 %shard_map.122.refs_8_ = f32[8,256,128]{2,1,0:T(8,128)S(1)} custom-call(s32[2]{0:T(128)S(1)} %pad_add_fusion.place_ref, bf16[256,5120]{1,0:T(8,128)(2,1)S(1)} %copy-done, bf16[256,5120]{1,0:T(8,128)(2,1)S(1)} %copy-done.2, bf16[1280,128]{1,0:T(8,128)(2,1)S(1)} %get-tuple-element.92.refs_0_, bf16[1280,128]{1,0:T(8,128)(2,1)S(1)} %get-tuple-element.91.refs_1_, ...), custom_call_target="tpu_custom_call" | custom-call | tf_op jit(solution)/shard_map/pallas_call | solution.py:386
  39.5 4.3 %collective-permute-done.11 = bf16[4,64,1536]{2,1,0:T(8,128)(2,1)} collective-permute-done((bf16[4,64,1536]{2,1,0:T(8,128)(2,1)}, bf16[4,64,1536]{2,1,0:T(8,128)(2,1)}, u32[]{:S(2)}, u32[]{:S(2)}) %collective-permute-start.11) | collective-permute-done | bytes 786464 | tf_op jit(solution)/shard_map/ppermute | solution.py:432
  45.5 4.0 %collective-permute-start.13 = (bf16[64,1536]{1,0:T(8,128)(2,1)S(1)}, bf16[64,1536]{1,0:T(8,128)(2,1)S(1)}, u32[]{:S(2)}, u32[]{:S(2)}) collective-permute-start(bf16[64,1536]{1,0:T(8,128)(2,1)S(1)} %get-tuple-element.94), channel_id=1, source_target_pairs={{0,8},{4,12},{8,0},{12,4},{1,9},{5,13},{9,1},{13,5},{2,10},{6,14},... | collective-permute-start | bytes 589832 | tf_op jit(solution)/shard_map/ppermute | solution.py:440
  49.4 2.2 %collective-permute-start.14 = (bf16[64,1536]{1,0:T(8,128)(2,1)S(1)}, bf16[64,1536]{1,0:T(8,128)(2,1)S(1)}, u32[]{:S(2)}, u32[]{:S(2)}) collective-permute-start(bf16[64,1536]{1,0:T(8,128)(2,1)S(1)} %get-tuple-element.93), channel_id=1, source_target_pairs={{0,4},{4,8},{8,12},{12,0},{1,5},{5,9},{9,13},{13,1},{2,6},{6,10},{... | collective-permute-start | bytes 589832 | tf_op jit(solution)/shard_map/ppermute | solution.py:440
  51.6 4.1 %collective-permute-done.7.refs_3_ = bf16[1280,128]{1,0:T(8,128)(2,1)S(1)} collective-permute-done((bf16[1280,128]{1,0:T(8,128)(2,1)S(1)}, bf16[1280,128]{1,0:T(8,128)(2,1)S(1)}, u32[]{:S(2)}, u32[]{:S(2)}) %collective-permute-start.7) | collective-permute-done | bytes 327712 | tf_op jit(solution)/shard_map/ppermute | solution.py:432
  55.7 1.6 %collective-permute-start.15 = (bf16[1280,128]{1,0:T(8,128)(2,1)}, bf16[1280,128]{1,0:T(8,128)(2,1)S(1)}, u32[]{:S(2)}, u32[]{:S(2)}) collective-permute-start(bf16[1280,128]{1,0:T(8,128)(2,1)} %collective-permute-done.5.refs_2_), channel_id=1, source_target_pairs={{0,2},{1,3},{2,0},{3,1},{4,6},{5,7},{6,4},{7,5},{8,10},{9,11},{10,... | collective-permute-start | bytes 983048 | tf_op jit(solution)/shard_map/ppermute | solution.py:432
  59.8 4.6 %collective-permute-start.12 = (bf16[64,1536]{1,0:T(8,128)(2,1)S(1)}, bf16[64,1536]{1,0:T(8,128)(2,1)S(1)}, u32[]{:S(2)}, u32[]{:S(2)}) collective-permute-start(bf16[64,1536]{1,0:T(8,128)(2,1)S(1)} %get-tuple-element.95), channel_id=1, source_target_pairs={{0,12},{4,0},{8,4},{12,8},{1,13},{5,1},{9,5},{13,9},{2,14},{6,2},{... | collective-permute-start | bytes 589832 | tf_op jit(solution)/shard_map/ppermute | solution.py:440
  64.4 4.0 %shard_map.123 = (f32[256,128]{1,0:T(8,128)S(1)}, f32[256,128]{1,0:T(8,128)S(1)}, f32[256,128]{1,0:T(8,128)S(1)}, f32[256,128]{1,0:T(8,128)S(1)}, f32[256,128]{1...) custom-call(s32[2]{0:T(128)S(1)} %pad_add_fusion.place_ref, ...), custom_call_target="tpu_custom_call" | custom-call | tf_op jit(solution)/shard_map/pallas_call | solution.py:386
  68.5 2.6 %shard_map.124 = (bf16[256,64]{1,0:T(8,128)(2,1)S(1)}, bf16[64,1024]{1,0:T(8,128)(2,1)S(1)}, f32[256,1024]{1,0:T(8,128)S(1)}) custom-call(s32[2]{0:T(128)S(1)} %pad_add_fusion.place_ref, s32[1,1]{1,0:T(1,128)} %bitcast.6.rank_ref, bf16[256,5120]{1,0:T(8,128)(2,1)S(1)} %copy-done, bf16[64,1536]{1,0:T(8,128)(2,1)S(1)} %get-tuple-element.96.refs_0_, ...), custom_call_target="tpu_custom_call" | custom-call | tf_op jit(solution)/shard_map/pallas_call | solution.py:199
  72.0 2.1 %shard_map.125 = (f32[256,128]{1,0:T(8,128)S(1)}, f32[256,128]{1,0:T(8,128)S(1)}, f32[256,128]{1,0:T(8,128)S(1)}, f32[256,128]{1,0:T(8,128)S(1)}) custom-call(s32[2]{0:T(128)S(1)} %pad_add_fusion.place_ref, bf16[256,5120]{1,0:T(8,128)(2,1)S(1)} %copy-done, bf16[256,5120]{1,0:T(8,128)(2,1)S(1)} %copy-done.2, ...), custom_call_target="tpu_custom_call" | custom-call | tf_op jit(solution)/shard_map/pallas_call | solution.py:386
  75.7 4.8 %shard_map.126 = (bf16[256,1024]{1,0:T(8,128)(2,1)}, bf16[64,1536]{1,0:T(8,128)(2,1)S(1)}, bf16[64,1536]{1,0:T(8,128)(2,1)S(1)}, bf16[64,1536]{1,0:T(8,128)(2,1)S(1)}, bf16[64,1536]{1,0:T(8,128)(2,1)S(1)}) custom-call(s32[2]{0:T(128)S(1)} %pad_add_fusion.place_ref, s32[4]{0:T(128)S(1)} %pad_add_fusion.1.columns_ref, s32[1,1]{1,0:T(1,128)} %bitcast.6.rank_ref, ...), custom_call_target="tpu_custom_call" | custom-call | tf_op jit(solution)/shard_map/pallas_call | solution.py:309
  82.1 3.7 %collective-permute-start.30 = (bf16[64,1536]{1,0:T(8,128)(2,1)S(1)}, bf16[64,1536]{1,0:T(8,128)(2,1)S(1)}, u32[]{:S(2)}, u32[]{:S(2)}) collective-permute-start(bf16[64,1536]{1,0:T(8,128)(2,1)S(1)} %get-tuple-element.85), channel_id=1, source_target_pairs={{0,12},{4,0},{8,4},{12,8},{1,13},{5,1},{9,5},{13,9},{2,14},{6,2},{... | collective-permute-start | bytes 589832 | tf_op jit(solution)/shard_map/ppermute | solution.py:440
  85.9 4.2 %collective-permute-done.26 = bf16[64,1536]{1,0:T(8,128)(2,1)S(1)} collective-permute-done((bf16[64,1536]{1,0:T(8,128)(2,1)S(1)}, bf16[64,1536]{1,0:T(8,128)(2,1)S(1)}, u32[]{:S(2)}, u32[]{:S(2)}) %collective-permute-start.26) | collective-permute-done | bytes 196640 | tf_op jit(solution)/shard_map/ppermute | solution.py:440
  95.0 7.1 %collective-permute-done.34 = bf16[64,1536]{1,0:T(8,128)(2,1)S(1)} collective-permute-done((bf16[64,1536]{1,0:T(8,128)(2,1)S(1)}, bf16[64,1536]{1,0:T(8,128)(2,1)S(1)}, u32[]{:S(2)}, u32[]{:S(2)}) %collective-permute-start.34) | collective-permute-done | bytes 196640 | tf_op jit(solution)/shard_map/ppermute | solution.py:440
  104.6 4.4 %collective-permute-done.36.refs_14_ = bf16[1,64,1536]{2,1,0:T(8,128)(2,1)S(1)} collective-permute-done((bf16[1,64,1536]{2,1,0:T(8,128)(2,1)S(1)}, bf16[1,64,1536]{2,1,0:T(8,128)(2,1)S(1)}, u32[]{:S(2)}, u32[]{:S(2)}) %collective-permute-start.36) | collective-permute-done | bytes 196640 | tf_op jit(solution)/shard_map/ppermute | solution.py:432
  110.5 3.2 %shard_map.127 = (f32[12,64,1280]{2,1,0:T(8,128)}, f32[12,64,256]{2,1,0:T(8,128)}) custom-call(s32[16]{0:T(128)S(1)} %copy-done.4, s32[48]{0:T(128)S(1)} %copy-done.5, bf16[1,64,1536]{2,1,0:T(8,128)(2,1)S(1)} %bitcast.29, bf16[1,64,1536]{2,1,0:T(8,128)(2,1)S(1)} %collective-permute-done.23.refs_1_, bf16[1,64,1536]{2,1,0:T(8,128)(2,1)S(1)} %collective-permute-done.24.refs_2_, ...), custom_call_target="tpu_custom_call" | custom-call | tf_op jit(solution)/shard_map/pallas_call | solution.py:141
  (98 shorter events, 31.2 us)
Async XLA Ops:
  0.7 12.0 %collective-permute-start.1 = (bf16[256,5120]{1,0:T(8,128)(2,1)}, bf16[256,5120]{1,0:T(8,128)(2,1)S(1)}, u32[]{:S(2)}, u32[]{:S(2)}) collective-permute-start(bf16[256,5120]{1,0:T(8,128)(2,1)} %refs_15_.1), channel_id=1, source_target_pairs={{0,1},{1,0},{2,3},{3,2},{4,5},{5,4},{6,7},{7,6},{8,9},{9,8},{10,11... | collective-permute-start | bytes 7864328 | tf_op jit(solution)/shard_map/ppermute | solution.py:429
  7.9 13.5 %collective-permute-start.3 = (bf16[1280,128]{1,0:T(8,128)(2,1)}, bf16[1280,128]{1,0:T(8,128)(2,1)S(1)}, u32[]{:S(2)}, u32[]{:S(2)}) collective-permute-start(bf16[1280,128]{1,0:T(8,128)(2,1)} %constant_dynamic-slice_fusion.4), channel_id=1, source_target_pairs={{0,4},{4,8},{8,12},{12,0},{1,5},{5,9},{9,13},{13,1},{2,6},{6,10},{... | collective-permute-start | bytes 983048 | tf_op jit(solution)/shard_map/ppermute | solution.py:440
  10.5 17.0 %collective-permute-start.4 = (bf16[1280,128]{1,0:T(8,128)(2,1)}, bf16[1280,128]{1,0:T(8,128)(2,1)S(1)}, u32[]{:S(2)}, u32[]{:S(2)}) collective-permute-start(bf16[1280,128]{1,0:T(8,128)(2,1)} %constant_dynamic-slice_fusion.4), channel_id=1, source_target_pairs={{0,12},{4,0},{8,4},{12,8},{1,13},{5,1},{9,5},{13,9},{2,14},{6,2},{... | collective-permute-start | bytes 983048 | tf_op jit(solution)/shard_map/ppermute | solution.py:440
  21.4 17.2 %collective-permute-start.6 = (bf16[1280,128]{1,0:T(8,128)(2,1)S(1)}, bf16[1280,128]{1,0:T(8,128)(2,1)}, u32[]{:S(2)}, u32[]{:S(2)}) collective-permute-start(bf16[1280,128]{1,0:T(8,128)(2,1)S(1)} %collective-permute-done.3.refs_0_), channel_id=1, source_target_pairs={{0,16},{16,0},{1,17},{17,1},{2,18},{18,2},{3,19},{19,3},{4,20},{20... | collective-permute-start | bytes 983048 | tf_op jit(solution)/shard_map/ppermute | solution.py:437
  23.1 16.0 %collective-permute-start.5 = (bf16[1280,128]{1,0:T(8,128)(2,1)S(1)}, bf16[1280,128]{1,0:T(8,128)(2,1)}, u32[]{:S(2)}, u32[]{:S(2)}) collective-permute-start(bf16[1280,128]{1,0:T(8,128)(2,1)S(1)} %collective-permute-done.3.refs_0_), channel_id=1, source_target_pairs={{0,4},{4,8},{8,12},{12,0},{1,5},{5,9},{9,13},{13,1},{2,6},{6,10},{... | collective-permute-start | bytes 983048 | tf_op jit(solution)/shard_map/ppermute | solution.py:440
  23.1 20.8 %collective-permute-start.11 = (bf16[4,64,1536]{2,1,0:T(8,128)(2,1)}, bf16[4,64,1536]{2,1,0:T(8,128)(2,1)}, u32[]{:S(2)}, u32[]{:S(2)}) collective-permute-start(bf16[4,64,1536]{2,1,0:T(8,128)(2,1)} %add.107), channel_id=1, source_target_pairs={{0,2},{1,3},{2,0},{3,1},{4,6},{5,7},{6,4},{7,5},{8,10},{9,11},{10,... | collective-permute-start | bytes 2359304 | tf_op jit(solution)/shard_map/ppermute | solution.py:432
  29.3 20.1 %collective-permute-start.9 = (bf16[1280,128]{1,0:T(8,128)(2,1)S(1)}, bf16[1280,128]{1,0:T(8,128)(2,1)S(1)}, u32[]{:S(2)}, u32[]{:S(2)}) collective-permute-start(bf16[1280,128]{1,0:T(8,128)(2,1)S(1)} %collective-permute-done.4.refs_1_), channel_id=1, source_target_pairs={{0,16},{16,0},{1,17},{17,1},{2,18},{18,2},{3,19},{19,3},{4,20},{20... | collective-permute-start | bytes 983048 | tf_op jit(solution)/shard_map/ppermute | solution.py:437
  36.9 20.4 %collective-permute-start.8 = (bf16[1280,128]{1,0:T(8,128)(2,1)S(1)}, bf16[1280,128]{1,0:T(8,128)(2,1)S(1)}, u32[]{:S(2)}, u32[]{:S(2)}) collective-permute-start(bf16[1280,128]{1,0:T(8,128)(2,1)S(1)} %collective-permute-done.4.refs_1_), channel_id=1, source_target_pairs={{0,2},{1,3},{2,0},{3,1},{4,6},{5,7},{6,4},{7,5},{8,10},{9,11},{10,... | collective-permute-start | bytes 983048 | tf_op jit(solution)/shard_map/ppermute | solution.py:432
  38.5 17.2 %collective-permute-start.7 = (bf16[1280,128]{1,0:T(8,128)(2,1)S(1)}, bf16[1280,128]{1,0:T(8,128)(2,1)S(1)}, u32[]{:S(2)}, u32[]{:S(2)}) collective-permute-start(bf16[1280,128]{1,0:T(8,128)(2,1)S(1)} %collective-permute-done.3.refs_0_), channel_id=1, source_target_pairs={{0,2},{1,3},{2,0},{3,1},{4,6},{5,7},{6,4},{7,5},{8,10},{9,11},{10,... | collective-permute-start | bytes 983048 | tf_op jit(solution)/shard_map/ppermute | solution.py:432
  39.0 18.8 %collective-permute-start.10 = (bf16[1280,128]{1,0:T(8,128)(2,1)}, bf16[1280,128]{1,0:T(8,128)(2,1)S(1)}, u32[]{:S(2)}, u32[]{:S(2)}) collective-permute-start(bf16[1280,128]{1,0:T(8,128)(2,1)} %collective-permute-done.5.refs_2_), channel_id=1, source_target_pairs={{0,16},{16,0},{1,17},{17,1},{2,18},{18,2},{3,19},{19,3},{4,20},{20... | collective-permute-start | bytes 983048 | tf_op jit(solution)/shard_map/ppermute | solution.py:437
  45.5 13.9 %collective-permute-start.13 = (bf16[64,1536]{1,0:T(8,128)(2,1)S(1)}, bf16[64,1536]{1,0:T(8,128)(2,1)S(1)}, u32[]{:S(2)}, u32[]{:S(2)}) collective-permute-start(bf16[64,1536]{1,0:T(8,128)(2,1)S(1)} %get-tuple-element.94), channel_id=1, source_target_pairs={{0,8},{4,12},{8,0},{12,4},{1,9},{5,13},{9,1},{13,5},{2,10},{6,14},... | collective-permute-start | bytes 589832 | tf_op jit(solution)/shard_map/ppermute | solution.py:440
  49.4 10.4 %collective-permute-start.14 = (bf16[64,1536]{1,0:T(8,128)(2,1)S(1)}, bf16[64,1536]{1,0:T(8,128)(2,1)S(1)}, u32[]{:S(2)}, u32[]{:S(2)}) collective-permute-start(bf16[64,1536]{1,0:T(8,128)(2,1)S(1)} %get-tuple-element.93), channel_id=1, source_target_pairs={{0,4},{4,8},{8,12},{12,0},{1,5},{5,9},{9,13},{13,1},{2,6},{6,10},{... | collective-permute-start | bytes 589832 | tf_op jit(solution)/shard_map/ppermute | solution.py:440
  55.7 15.4 %collective-permute-start.15 = (bf16[1280,128]{1,0:T(8,128)(2,1)}, bf16[1280,128]{1,0:T(8,128)(2,1)S(1)}, u32[]{:S(2)}, u32[]{:S(2)}) collective-permute-start(bf16[1280,128]{1,0:T(8,128)(2,1)} %collective-permute-done.5.refs_2_), channel_id=1, source_target_pairs={{0,2},{1,3},{2,0},{3,1},{4,6},{5,7},{6,4},{7,5},{8,10},{9,11},{10,... | collective-permute-start | bytes 983048 | tf_op jit(solution)/shard_map/ppermute | solution.py:432
  57.4 14.4 %collective-permute-start.16 = (bf16[1280,128]{1,0:T(8,128)(2,1)S(1)}, bf16[1280,128]{1,0:T(8,128)(2,1)S(1)}, u32[]{:S(2)}, u32[]{:S(2)}) collective-permute-start(bf16[1280,128]{1,0:T(8,128)(2,1)S(1)} %collective-permute-done.7.refs_3_), channel_id=1, source_target_pairs={{0,16},{16,0},{1,17},{17,1},{2,18},{18,2},{3,19},{19,3},{4,20},{20... | collective-permute-start | bytes 983048 | tf_op jit(solution)/shard_map/ppermute | solution.py:437
  57.8 14.1 %collective-permute-start.17 = (bf16[1280,128]{1,0:T(8,128)(2,1)S(1)}, bf16[1280,128]{1,0:T(8,128)(2,1)S(1)}, u32[]{:S(2)}, u32[]{:S(2)}) collective-permute-start(bf16[1280,128]{1,0:T(8,128)(2,1)S(1)} %collective-permute-done.8.refs_4_), channel_id=1, source_target_pairs={{0,16},{16,0},{1,17},{17,1},{2,18},{18,2},{3,19},{19,3},{4,20},{20... | collective-permute-start | bytes 983048 | tf_op jit(solution)/shard_map/ppermute | solution.py:437
  59.4 12.6 %collective-permute-start.18 = (bf16[1280,128]{1,0:T(8,128)(2,1)S(1)}, bf16[1280,128]{1,0:T(8,128)(2,1)S(1)}, u32[]{:S(2)}, u32[]{:S(2)}) collective-permute-start(bf16[1280,128]{1,0:T(8,128)(2,1)S(1)} %collective-permute-done.10.refs_7_), channel_id=1, source_target_pairs={{0,2},{1,3},{2,0},{3,1},{4,6},{5,7},{6,4},{7,5},{8,10},{9,11},{10,... | collective-permute-start | bytes 983048 | tf_op jit(solution)/shard_map/ppermute | solution.py:432
  80.5 9.6 %collective-permute-start.26 = (bf16[64,1536]{1,0:T(8,128)(2,1)S(1)}, bf16[64,1536]{1,0:T(8,128)(2,1)S(1)}, u32[]{:S(2)}, u32[]{:S(2)}) collective-permute-start(bf16[64,1536]{1,0:T(8,128)(2,1)S(1)} %get-tuple-element.84), channel_id=1, source_target_pairs={{0,4},{4,8},{8,12},{12,0},{1,5},{5,9},{9,13},{13,1},{2,6},{6,10},{... | collective-permute-start | bytes 589832 | tf_op jit(solution)/shard_map/ppermute | solution.py:440
  81.5 10.1 %collective-permute-start.24 = (bf16[1,64,1536]{2,1,0:T(8,128)(2,1)S(1)}, bf16[1,64,1536]{2,1,0:T(8,128)(2,1)S(1)}, u32[]{:S(2)}, u32[]{:S(2)}) collective-permute-start(bf16[1,64,1536]{2,1,0:T(8,128)(2,1)S(1)} %bitcast.27), channel_id=1, source_target_pairs={{0,2},{1,3},{2,0},{3,1},{4,6},{5,7},{6,4},{7,5},{8,10},{9,11},{10,... | collective-permute-start | bytes 589832 | tf_op jit(solution)/shard_map/ppermute | solution.py:432
  82.1 11.5 %collective-permute-start.30 = (bf16[64,1536]{1,0:T(8,128)(2,1)S(1)}, bf16[64,1536]{1,0:T(8,128)(2,1)S(1)}, u32[]{:S(2)}, u32[]{:S(2)}) collective-permute-start(bf16[64,1536]{1,0:T(8,128)(2,1)S(1)} %get-tuple-element.85), channel_id=1, source_target_pairs={{0,12},{4,0},{8,4},{12,8},{1,13},{5,1},{9,5},{13,9},{2,14},{6,2},{... | collective-permute-start | bytes 589832 | tf_op jit(solution)/shard_map/ppermute | solution.py:440
  85.8 16.3 %collective-permute-start.34 = (bf16[64,1536]{1,0:T(8,128)(2,1)S(1)}, bf16[64,1536]{1,0:T(8,128)(2,1)S(1)}, u32[]{:S(2)}, u32[]{:S(2)}) collective-permute-start(bf16[64,1536]{1,0:T(8,128)(2,1)S(1)} %get-tuple-element.86), channel_id=1, source_target_pairs={{0,8},{4,12},{8,0},{12,4},{1,9},{5,13},{9,1},{13,5},{2,10},{6,14},... | collective-permute-start | bytes 589832 | tf_op jit(solution)/shard_map/ppermute | solution.py:440
  90.1 13.5 %collective-permute-start.28 = (bf16[1,64,1536]{2,1,0:T(8,128)(2,1)S(1)}, bf16[1,64,1536]{2,1,0:T(8,128)(2,1)S(1)}, u32[]{:S(2)}, u32[]{:S(2)}) collective-permute-start(bf16[1,64,1536]{2,1,0:T(8,128)(2,1)S(1)} %bitcast.30), channel_id=1, source_target_pairs={{0,2},{1,3},{2,0},{3,1},{4,6},{5,7},{6,4},{7,5},{8,10},{9,11},{10,... | collective-permute-start | bytes 589832 | tf_op jit(solution)/shard_map/ppermute | solution.py:432
  91.5 12.0 %collective-permute-start.25 = (bf16[1,64,1536]{2,1,0:T(8,128)(2,1)S(1)}, bf16[1,64,1536]{2,1,0:T(8,128)(2,1)S(1)}, u32[]{:S(2)}, u32[]{:S(2)}) collective-permute-start(bf16[1,64,1536]{2,1,0:T(8,128)(2,1)S(1)} %collective-permute-done.24.refs_2_), channel_id=1, source_target_pairs={{0,1},{1,0},{2,3},{3,2},{4,5},{5,4},{6,7},{7,6},{8,9},{9,8},{10,11... | collective-permute-start | bytes 589832 | tf_op jit(solution)/shard_map/ppermute | solution.py:429
  91.6 12.5 %collective-permute-start.27 = (bf16[1,64,1536]{2,1,0:T(8,128)(2,1)S(1)}, bf16[1,64,1536]{2,1,0:T(8,128)(2,1)S(1)}, u32[]{:S(2)}, u32[]{:S(2)}) collective-permute-start(bf16[1,64,1536]{2,1,0:T(8,128)(2,1)S(1)} %bitcast.31), channel_id=1, source_target_pairs={{0,1},{1,0},{2,3},{3,2},{4,5},{5,4},{6,7},{7,6},{8,9},{9,8},{10,11... | collective-permute-start | bytes 589832 | tf_op jit(solution)/shard_map/ppermute | solution.py:429
  93.6 10.5 %collective-permute-start.32 = (bf16[1,64,1536]{2,1,0:T(8,128)(2,1)S(1)}, bf16[1,64,1536]{2,1,0:T(8,128)(2,1)S(1)}, u32[]{:S(2)}, u32[]{:S(2)}) collective-permute-start(bf16[1,64,1536]{2,1,0:T(8,128)(2,1)S(1)} %bitcast.33), channel_id=1, source_target_pairs={{0,2},{1,3},{2,0},{3,1},{4,6},{5,7},{6,4},{7,5},{8,10},{9,11},{10,... | collective-permute-start | bytes 589832 | tf_op jit(solution)/shard_map/ppermute | solution.py:432
  (24 other events, 236.8 us)
